TPU v7x, 32 devices: a whole 2x2x4 slice. The times are simulated.
32 devices in a mesh: fsdp: 4 (over z), ctx: 2 (over core), tp: 4 (over y, x).
Axes of the slice: x: 2, y: 2, z: 4, core: 2. Of those that a mesh axis runs over, the one named last changes fastest.
Arguments:
- tokens: bfloat16 [8, 2048, 1024], P('fsdp', 'ctx', 'tp'), may hold values from -6 to 6
- lengths: int32 [8], P('fsdp'), may hold values from 512 to 2048, as said below
- w_query: bfloat16 [1024, 1024], P('fsdp', 'tp'), may hold values from -0.1875 to 0.1875
- w_keyval: bfloat16 [1024, 256], P('fsdp'), may hold values from -0.1875 to 0.1875
- w_out: bfloat16 [1024, 1024], P('tp', 'fsdp'), may hold values from -3 to 3
- w_gateup: bfloat16 [2, 1024, 3072], P(None, 'fsdp', 'tp'), may hold values from -0.1875 to 0.1875
- w_down: bfloat16 [3072, 1024], P('tp', 'fsdp'), may hold values from -0.109375 to 0.109375
- gain_attn: bfloat16 [1024], P('tp'), may hold values from 0.5 to 1.5
- gain_mlp: bfloat16 [1024], P('tp'), may hold values from 0.5 to 1.5
- cotangent: bfloat16 [8, 2048, 1024], P('fsdp', 'ctx', 'tp'), may hold values from -6 to 6
Outputs:
- outputs: bfloat16 [8, 2048, 1024], P('fsdp', 'ctx', 'tp')
- grad_tokens: float32 [8, 2048, 1024], P('fsdp', 'ctx', 'tp')
- grad_query: float32 [1024, 1024], P(('fsdp', 'ctx'), 'tp')
- grad_keyval: float32 [1024, 256], P(('fsdp', 'ctx'))
- grad_output_proj: float32 [1024, 1024], P('tp', ('fsdp', 'ctx'))
- grad_gateup: float32 [2, 1024, 3072], P(None, ('fsdp', 'ctx'), 'tp')
- grad_down: float32 [3072, 1024], P('tp', ('fsdp', 'ctx'))
- grad_gain_attn: float32 [1024], P('tp')
- grad_gain_mlp: float32 [1024], P('tp')
Inputs may be any that keep to these rules, and one draw needn't show every extreme that they name: `lengths`: in every aligned block of 2 slots one slot has 1536 valid tokens or more; some slot has exactly 2048 and some exactly 512.
All inputs are finite; a program needn't handle non-finite values.
Results may differ from a plain program's by a relative error of at most 0.015.
Values may be sent and summed in bfloat16 or wider, within the bound.
No kernel may reach another device: no remote copies, remote signals or barrier semaphores. Data moves between devices by JAX's collectives and lax.ppermute only.
A program may use at most 128 MiB of HBM per device.

v0:
```python
import jax
import jax.numpy as jnp
from jax import lax
from jax.sharding import PartitionSpec as P

D = 1024
HEAD = 128
WINDOW = 1024


epsilon = 1e-06


def passed_along(value, axis, steps):
    count = lax.axis_size(axis)
    first, last = (max(0, -steps), min(count, count - steps))
    return lax.ppermute(value, axis, [(source, source + steps) for source in range(first, last)])


def rotary(vectors, positions, direction):
    half_width = vectors.shape[-1] // 2
    freq_table = 10000.0 ** (-jnp.arange(half_width, dtype=jnp.float32) / half_width)
    angles = positions.astype(jnp.float32)[:, None] * freq_table[None, :]
    cosine = jnp.cos(angles)[:, None, :]
    sine_part = direction * jnp.sin(angles)[:, None, :]
    leading = vectors[..., :half_width]
    trailing = vectors[..., half_width:]
    return jnp.concatenate(
        [leading * cosine - trailing * sine_part, trailing * cosine + leading * sine_part], axis=-1
    )


def gated(gate_proj, up_proj):
    return jax.nn.gelu(gate_proj, approximate=True) * up_proj


def body(
    tokens, lengths, w_query, w_keyval, w_out, w_gateup, w_down, gain_attn, gain_mlp, cotangent
):
    tp_count = lax.axis_size("tp")
    ctx_count = lax.axis_size("ctx")
    group_count = lax.axis_size("fsdp") * ctx_count
    tokens_in, cot_in, lengths_in = (tokens, cotangent, lengths)
    seq_rows = tokens.shape[1]
    row_base = lax.axis_index("ctx") * seq_rows
    key_pos = row_base - seq_rows + jnp.arange(2 * seq_rows, dtype=jnp.int32)
    positions = row_base + jnp.arange(seq_rows, dtype=jnp.int32)
    heads_local = w_query.shape[1] // HEAD
    block_rows = min(512, seq_rows)
    block_count = seq_rows // block_rows
    score_scale = HEAD ** (-0.5)
    gain_attn_f = gain_attn.astype(jnp.float32)
    gain_mlp_f = gain_mlp.astype(jnp.float32)

    def row_total(values):
        return lax.psum(values, "tp")

    def normalize(values, gain_vec):
        total = row_total(jnp.sum(values * values, axis=1))
        inverse = lax.rsqrt(total / D + epsilon)[:, None]
        scaled = values * inverse
        return ((scaled * gain_vec).astype(jnp.bfloat16), scaled, inverse)

    def normalize_back(grad_normed, scaled, inverse, gain_vec):
        grad_scaled = grad_normed * gain_vec
        inner = row_total(jnp.sum(grad_scaled * scaled, axis=1)) / D
        return (
            inverse * (grad_scaled - scaled * inner[:, None]),
            jnp.sum(grad_normed * scaled, axis=0),
        )

    def gather_rows(values):
        return lax.all_gather(values, "tp", axis=1, tiled=True)

    def gather_grads(values):
        return lax.all_gather(values, "tp", axis=1, tiled=True)

    def sum_branch(values):
        return lax.psum_scatter(values, "tp", scatter_dimension=1, tiled=True)

    def sum_normed(values):
        return lax.psum_scatter(values, "tp", scatter_dimension=1, tiled=True)

    def allowed_mask(block_index, length):
        query_pos = row_base + block_index * block_rows + jnp.arange(block_rows, dtype=jnp.int32)
        inside = (key_pos[None, :] <= query_pos[:, None]) & (
            key_pos[None, :] > query_pos[:, None] - WINDOW
        )
        inside = inside & (key_pos[None, :] >= 0) & (key_pos[None, :] < length)
        return inside | (key_pos[None, :] == query_pos[:, None])

    def slot_step(totals, slot_data):
        inputs, cot_rows, length = slot_data
        w_q_full, w_kv_full, w_o_full, w_gu_full, w_d_full = (
            lax.all_gather(w_query, "fsdp", axis=0, tiled=True),
            lax.all_gather(w_keyval, "fsdp", axis=0, tiled=True),
            lax.all_gather(w_out, "fsdp", axis=1, tiled=True),
            lax.all_gather(w_gateup, "fsdp", axis=1, tiled=True),
            lax.all_gather(w_down, "fsdp", axis=1, tiled=True),
        )
        residual = inputs.astype(jnp.float32)
        normed_attn, scaled_attn, inverse_attn = normalize(residual, gain_attn_f)
        rows_attn = gather_rows(normed_attn)
        query_lin = jnp.dot(rows_attn, w_q_full, preferred_element_type=jnp.float32)
        keyval_lin = jnp.dot(rows_attn, w_kv_full, preferred_element_type=jnp.float32)
        queries = rotary(query_lin.reshape(seq_rows, heads_local, HEAD), positions, 1.0).astype(
            jnp.bfloat16
        )
        key_own = rotary(keyval_lin[:, None, :HEAD], positions, 1.0)[:, 0]
        keyval_own = jnp.concatenate([key_own, keyval_lin[:, HEAD:]], axis=1).astype(jnp.bfloat16)
        keyval_prev = passed_along(keyval_own, "ctx", 1)
        keyval_all = jnp.concatenate([keyval_prev, keyval_own], axis=0)
        keys_all = keyval_all[:, :HEAD]
        values_all = keyval_all[:, HEAD:]

        def block_scores(block_index, block_query):
            scores = (
                jnp.einsum("rhe,se->rhs", block_query, keys_all, preferred_element_type=jnp.float32)
                * score_scale
            )
            return jnp.where(allowed_mask(block_index, length)[:, None, :], scores, -1e30)

        def forward_block(block_index):
            block_query = lax.dynamic_slice_in_dim(queries, block_index * block_rows, block_rows, 0)
            scores = block_scores(block_index, block_query)
            row_max = jnp.max(scores, axis=-1, keepdims=True)
            exp_scores = jnp.exp(scores - row_max)
            row_sum = jnp.sum(exp_scores, axis=-1, keepdims=True)
            soft_weights = (exp_scores / row_sum).astype(jnp.bfloat16)
            mixed_block = jnp.einsum(
                "rhs,se->rhe", soft_weights, values_all, preferred_element_type=jnp.float32
            )
            return (mixed_block, (row_max + jnp.log(row_sum))[..., 0])

        mixed_blocks, log_blocks = lax.map(forward_block, jnp.arange(block_count, dtype=jnp.int32))
        mixed_heads = mixed_blocks.reshape(seq_rows, heads_local * HEAD).astype(jnp.bfloat16)
        log_sums = log_blocks.reshape(seq_rows, heads_local)
        hidden = residual + sum_branch(
            jnp.dot(mixed_heads, w_o_full, preferred_element_type=jnp.float32)
        )
        normed_mlp, scaled_mlp, inverse_mlp = normalize(hidden, gain_mlp_f)
        rows_mlp = gather_rows(normed_mlp)
        gate_proj = jnp.dot(rows_mlp, w_gu_full[0], preferred_element_type=jnp.float32)
        up_proj = jnp.dot(rows_mlp, w_gu_full[1], preferred_element_type=jnp.float32)
        active_full, gated_back = jax.vjp(gated, gate_proj, up_proj)
        active = active_full.astype(jnp.bfloat16)
        branch_mlp = sum_branch(jnp.dot(active, w_d_full, preferred_element_type=jnp.float32))
        outputs = (hidden + branch_mlp).astype(jnp.bfloat16)
        valid_rows = (positions < length)[:, None]
        grad_final = jnp.where(valid_rows, cot_rows.astype(jnp.float32), 0.0)
        grad_mlp_rows = gather_grads(grad_final.astype(jnp.bfloat16))
        grad_active = jnp.dot(grad_mlp_rows, w_d_full.T, preferred_element_type=jnp.float32)
        grad_wdown = jnp.dot(active.T, grad_mlp_rows, preferred_element_type=jnp.float32)
        grad_gate, grad_up = gated_back(grad_active)
        grad_gate = grad_gate.astype(jnp.bfloat16)
        grad_up = grad_up.astype(jnp.bfloat16)
        grad_wgateup = jnp.stack(
            [
                jnp.dot(rows_mlp.T, grad_gate, preferred_element_type=jnp.float32),
                jnp.dot(rows_mlp.T, grad_up, preferred_element_type=jnp.float32),
            ]
        )
        grad_normed_mlp = sum_normed(
            jnp.dot(grad_gate, w_gu_full[0].T, preferred_element_type=jnp.float32)
            + jnp.dot(grad_up, w_gu_full[1].T, preferred_element_type=jnp.float32)
        )
        grad_hidden_norm, gain_mlp_term = normalize_back(
            grad_normed_mlp, scaled_mlp, inverse_mlp, gain_mlp_f
        )
        grad_hidden = grad_final + grad_hidden_norm
        grad_attn_rows = gather_grads(grad_hidden.astype(jnp.bfloat16))
        grad_mixed = jnp.dot(grad_attn_rows, w_o_full.T, preferred_element_type=jnp.float32).astype(
            jnp.bfloat16
        )
        grad_wout = jnp.dot(mixed_heads.T, grad_attn_rows, preferred_element_type=jnp.float32)
        grad_mixed_heads = grad_mixed.reshape(seq_rows, heads_local, HEAD)

        def backward_block(carry, block_index):
            grad_keys, grad_values = carry
            row_start = block_index * block_rows
            block_query = lax.dynamic_slice_in_dim(queries, row_start, block_rows, 0)
            block_grad = lax.dynamic_slice_in_dim(grad_mixed_heads, row_start, block_rows, 0)
            block_logs = lax.dynamic_slice_in_dim(log_sums, row_start, block_rows, 0)
            soft_full = jnp.exp(block_scores(block_index, block_query) - block_logs[..., None])
            grad_soft = jnp.einsum(
                "rhe,se->rhs", block_grad, values_all, preferred_element_type=jnp.float32
            )
            inner = jnp.sum(soft_full * grad_soft, axis=-1, keepdims=True)
            grad_scores = (soft_full * (grad_soft - inner)).astype(jnp.bfloat16)
            grad_block_query = (
                jnp.einsum("rhs,se->rhe", grad_scores, keys_all, preferred_element_type=jnp.float32)
                * score_scale
            )
            grad_keys = (
                grad_keys
                + jnp.einsum(
                    "rhs,rhe->se", grad_scores, block_query, preferred_element_type=jnp.float32
                )
                * score_scale
            )
            grad_values = grad_values + jnp.einsum(
                "rhs,rhe->se",
                soft_full.astype(jnp.bfloat16),
                block_grad,
                preferred_element_type=jnp.float32,
            )
            return ((grad_keys, grad_values), grad_block_query)

        zero_keys = jnp.zeros((keyval_all.shape[0], HEAD), jnp.float32)
        (grad_keys, grad_values), grad_query_blocks = lax.scan(
            backward_block, (zero_keys, zero_keys), jnp.arange(block_count, dtype=jnp.int32)
        )
        grad_keyval_all = jnp.concatenate([grad_keys, grad_values], axis=1)
        grad_keyval_back = passed_along(
            grad_keyval_all[:seq_rows].astype(jnp.bfloat16), "ctx", -1
        ).astype(jnp.float32)
        grad_keyval_here = grad_keyval_all[seq_rows:] + grad_keyval_back
        grad_keyval = lax.psum(grad_keyval_here.astype(jnp.bfloat16), "tp").astype(jnp.float32)
        grad_key_lin = rotary(grad_keyval[:, None, :HEAD], positions, -1.0)[:, 0]
        grad_keyval_lin = jnp.concatenate([grad_key_lin, grad_keyval[:, HEAD:]], axis=1).astype(
            jnp.bfloat16
        )
        grad_query_heads = grad_query_blocks.reshape(seq_rows, heads_local, HEAD)
        grad_query_lin = (
            rotary(grad_query_heads, positions, -1.0)
            .reshape(seq_rows, heads_local * HEAD)
            .astype(jnp.bfloat16)
        )
        grad_wquery = jnp.dot(rows_attn.T, grad_query_lin, preferred_element_type=jnp.float32)
        grad_wkeyval = jnp.dot(rows_attn.T, grad_keyval_lin, preferred_element_type=jnp.float32)
        grad_normed_attn = sum_normed(
            jnp.dot(grad_query_lin, w_q_full.T, preferred_element_type=jnp.float32)
            + jnp.dot(grad_keyval_lin, w_kv_full.T, preferred_element_type=jnp.float32)
            * (1.0 / tp_count)
        )
        grad_input_norm, gain_attn_term = normalize_back(
            grad_normed_attn, scaled_attn, inverse_attn, gain_attn_f
        )
        grad_inputs = grad_hidden + grad_input_norm
        weight_terms = (
            lax.psum_scatter(grad_wquery, ("fsdp", "ctx"), scatter_dimension=0, tiled=True),
            lax.psum_scatter(grad_wkeyval, ("fsdp", "ctx"), scatter_dimension=0, tiled=True),
            lax.psum_scatter(grad_wout, ("fsdp", "ctx"), scatter_dimension=1, tiled=True),
            lax.psum_scatter(grad_wgateup, ("fsdp", "ctx"), scatter_dimension=1, tiled=True),
            lax.psum_scatter(grad_wdown, ("fsdp", "ctx"), scatter_dimension=1, tiled=True),
        )
        weight_totals, attn_gain_total, mlp_gain_total = totals
        weight_totals = jax.tree.map(jnp.add, weight_totals, weight_terms)
        new_totals = (
            weight_totals,
            attn_gain_total + gain_attn_term,
            mlp_gain_total + gain_mlp_term,
        )
        return (new_totals, (outputs, grad_inputs))

    grad_rows_count = D // group_count
    zero_weights = (
        jnp.zeros((grad_rows_count, w_query.shape[1]), jnp.float32),
        jnp.zeros((grad_rows_count, w_keyval.shape[1]), jnp.float32),
        jnp.zeros((w_out.shape[0], grad_rows_count), jnp.float32),
        jnp.zeros((2, grad_rows_count, w_gateup.shape[2]), jnp.float32),
        jnp.zeros((w_down.shape[0], grad_rows_count), jnp.float32),
    )
    zero_gain = jnp.zeros(gain_attn.shape, jnp.float32)
    totals, (outputs, grad_tokens) = lax.scan(
        slot_step, (zero_weights, zero_gain, zero_gain), (tokens_in, cot_in, lengths_in)
    )
    weight_totals, attn_gain_total, mlp_gain_total = totals
    gain_attn_grad, gain_mlp_grad = lax.psum((attn_gain_total, mlp_gain_total), ("fsdp", "ctx"))
    return (
        outputs,
        grad_tokens,
        weight_totals[0],
        weight_totals[1],
        weight_totals[2],
        weight_totals[3],
        weight_totals[4],
        gain_attn_grad,
        gain_mlp_grad,
    )


def solution(mesh):
    in_specs = (
        P("fsdp", "ctx", "tp"),
        P("fsdp"),
        P("fsdp", "tp"),
        P("fsdp", None),
        P("tp", "fsdp"),
        P(None, "fsdp", "tp"),
        P("tp", "fsdp"),
        P("tp"),
        P("tp"),
        P("fsdp", "ctx", "tp"),
    )
    out_specs = (
        P("fsdp", "ctx", "tp"),
        P("fsdp", "ctx", "tp"),
        P(("fsdp", "ctx"), "tp"),
        P(("fsdp", "ctx"), None),
        P("tp", ("fsdp", "ctx")),
        P(None, ("fsdp", "ctx"), "tp"),
        P("tp", ("fsdp", "ctx")),
        P("tp"),
        P("tp"),
    )
    return jax.shard_map(body, mesh=mesh, in_specs=in_specs, out_specs=out_specs, check_vma=False)
```

profile of v0, /device:TPU:0, one launch (start us, length us, event | category | flops | bytes accessed | tf_op | source)
XLA Modules:
  0.0 1806.8 jit_solution(14184233249694531120)
XLA Ops:
  9.7 1775.2 %while.101 = (s32[]{:T(128)}, f32[128,256]{1,0:T(8,128)}, f32[128,256]{1,0:T(8,128)}, f32[256,128]{1,0:T(8,128)}, f32[2,128,768]{2,1,0:T(8,128)}, /*index=5*/f32...) while((s32[]{:T(128)}, f32[128,256]{1,0:T(8,128)}, ...), condition=%wide.region_28.29_spmd.clone.clone.clone, body=%wide.region_0.28_spmd.clone.clone.clone.sunk | while | flops 23212412928 | bytes 608017280 | solution.py:265
  93.2 24.1 %while.102 = (s32[]{:T(128)}, bf16[2,512,2,128]{3,1,2,0:T(8,128)(2,1)}, f32[2,512,2]{1,2,0:T(2,128)S(1)}, s32[2048]{0:T(1024)S(1)}, s32[2]{0:T(128)S(1)}, /*inde...) while((s32[]{:T(128)}, ...), condition=%wide.region_6.6_spmd, body=%wide.region_3.5_spmd.sunk | while | flops 1106251776 | bytes 35455260 | solution.py:135
  126.0 47.4 %reduce-scatter.10.cloned.1.call-done = f32[1024,256]{1,0:T(8,128)} async-done(((f32[1024,1024]{1,0:T(8,128)}), f32[1024,256]{1,0:T(8,128)}) %reduce-scatter.10.cloned.1.call-update) | async-done | bytes 1048592 | tf_op jit(solution)/shard_map/while/body/eval_jaxpr/reduce_scatter | solution.py:79
  185.8 27.0 %all-gather.15.cloned.1.call-done = bf16[768,1024]{1,0:T(8,128)(2,1)} async-done(((bf16[768,256]{1,0:T(8,128)(2,1)}), bf16[768,1024]{1,0:T(8,128)(2,1)}) %all-gather.15.cloned.1.call-update) | async-done | bytes 1572880 | tf_op jit(solution)/shard_map/while/body/eval_jaxpr/all_gather | solution.py:99
  212.8 35.3 %all-gather.13.cloned.1.call-done = bf16[1024,1024]{1,0:T(8,128)(2,1)} async-done(((bf16[1024,256]{1,0:T(8,128)(2,1)}), bf16[1024,1024]{1,0:T(8,128)(2,1)}) %all-gather.13.cloned.1.call-update) | async-done | bytes 2097168 | tf_op jit(solution)/shard_map/while/body/eval_jaxpr/all_gather | solution.py:76
  253.6 59.5 %all-gather.11.cloned.1.call-done = bf16[2,1024,768]{2,1,0:T(8,128)(2,1)} async-done(((bf16[2,256,768]{2,1,0:T(8,128)(2,1)}), bf16[2,1024,768]{2,1,0:T(8,128)(2,1)}) %all-gather.11.cloned.1.call-update) | async-done | bytes 3145744 | tf_op jit(solution)/shard_map/while/body/eval_jaxpr/all_gather | solution.py:98
  313.1 35.7 %all-gather.9.cloned.1.call-done = bf16[1024,1024]{1,0:T(8,128)(2,1)} async-done(((bf16[1024,256]{1,0:T(8,128)(2,1)}), bf16[1024,1024]{1,0:T(8,128)(2,1)}) %all-gather.9.cloned.1.call-update) | async-done | bytes 2097168 | tf_op jit(solution)/shard_map/while/body/eval_jaxpr/all_gather | solution.py:73
  364.7 52.8 %reduce-scatter.12.cloned.1.call-done = f32[1024,256]{1,0:T(8,128)} async-done(((f32[1024,1024]{1,0:T(8,128)}), f32[1024,256]{1,0:T(8,128)}) %reduce-scatter.12.cloned.1.call-update) | async-done | bytes 1048592 | tf_op jit(solution)/shard_map/while/body/eval_jaxpr/reduce_scatter | solution.py:82
  431.9 34.7 %all-gather.17.cloned.1.call-done = bf16[1024,1024]{1,0:T(8,128)(2,1)} async-done(((bf16[1024,256]{1,0:T(8,128)(2,1)}), bf16[1024,1024]{1,0:T(8,128)(2,1)}) %all-gather.17.cloned.1.call-update) | async-done | bytes 2097168 | tf_op jit(solution)/shard_map/while/body/eval_jaxpr/all_gather | solution.py:76
  469.9 39.5 %while.103 = (s32[]{:T(128)}, f32[2048,128]{1,0:T(8,128)S(1)}, f32[2048,128]{1,0:T(8,128)}, f32[2,512,2,128]{3,1,0,2:T(8,128)}, s32[2048]{0:T(1024)S(1)}, /*inde...) while((s32[]{:T(128)}, f32[2048,128]{1,0:T(8,128)S(1)}, ...), condition=%wide.region_15.15_spmd.clone, body=%wide.region_13.14_spmd.clone.sunk | while | flops 2724597760 | bytes 87093640 | solution.py:210
  571.7 32.5 %reduce-scatter.22.cloned.1.call-done = f32[768,128]{1,0:T(8,128)} async-done(((f32[768,1024]{1,0:T(8,128)}), f32[768,128]{1,0:T(8,128)}) %reduce-scatter.22.cloned.1.call-update) | async-done | bytes 393232 | tf_op jit(solution)/shard_map/while/body/eval_jaxpr/reduce_scatter | solution.py:245
  605.4 53.8 %reduce-scatter.26.cloned.1.call-done = f32[1024,256]{1,0:T(8,128)} async-done(((f32[1024,1024]{1,0:T(8,128)}), f32[1024,256]{1,0:T(8,128)}) %reduce-scatter.26.cloned.1.call-update) | async-done | bytes 1048592 | tf_op jit(solution)/shard_map/while/body/eval_jaxpr/reduce_scatter | solution.py:79
  661.4 69.9 %reduce-scatter.20.cloned.1.call-done = f32[2,128,768]{2,1,0:T(8,128)} async-done(((f32[2,1024,768]{2,1,0:T(8,128)}), f32[2,128,768]{2,1,0:T(8,128)}) %reduce-scatter.20.cloned.1.call-update) | async-done | bytes 786448 | tf_op jit(solution)/shard_map/while/body/eval_jaxpr/reduce_scatter | solution.py:244
  732.6 31.7 %reduce-scatter.18.cloned.1.call-done = f32[256,128]{1,0:T(8,128)} async-done(((f32[256,1024]{1,0:T(8,128)}), f32[256,128]{1,0:T(8,128)}) %reduce-scatter.18.cloned.1.call-update) | async-done | bytes 131088 | tf_op jit(solution)/shard_map/while/body/eval_jaxpr/reduce_scatter | solution.py:243
  765.3 31.8 %reduce-scatter.14.cloned.1.call-done = f32[128,256]{1,0:T(8,128)} async-done(((f32[1024,256]{1,0:T(8,128)}), f32[128,256]{1,0:T(8,128)}) %reduce-scatter.14.cloned.1.call-update) | async-done | bytes 131088 | tf_op jit(solution)/shard_map/while/body/eval_jaxpr/reduce_scatter | solution.py:241
  798.6 31.1 %reduce-scatter.16.cloned.1.call-done = f32[128,256]{1,0:T(8,128)} async-done(((f32[1024,256]{1,0:T(8,128)}), f32[128,256]{1,0:T(8,128)}) %reduce-scatter.16.cloned.1.call-update) | async-done | bytes 131088 | tf_op jit(solution)/shard_map/while/body/eval_jaxpr/reduce_scatter | solution.py:242
  830.7 52.7 %reduce-scatter.24.cloned.1.call-done = f32[1024,256]{1,0:T(8,128)} async-done(((f32[1024,1024]{1,0:T(8,128)}), f32[1024,256]{1,0:T(8,128)}) %reduce-scatter.24.cloned.1.call-update) | async-done | bytes 1048592 | tf_op jit(solution)/shard_map/while/body/eval_jaxpr/reduce_scatter | solution.py:82
  1010.2 48.3 %reduce-scatter.10.cloned.1.call-done = f32[1024,256]{1,0:T(8,128)} async-done(((f32[1024,1024]{1,0:T(8,128)}), f32[1024,256]{1,0:T(8,128)}) %reduce-scatter.10.cloned.1.call-update) | async-done | bytes 1048592 | tf_op jit(solution)/shard_map/while/body/eval_jaxpr/reduce_scatter | solution.py:79
  1071.2 26.7 %all-gather.15.cloned.1.call-done = bf16[768,1024]{1,0:T(8,128)(2,1)} async-done(((bf16[768,256]{1,0:T(8,128)(2,1)}), bf16[768,1024]{1,0:T(8,128)(2,1)}) %all-gather.15.cloned.1.call-update) | async-done | bytes 1572880 | tf_op jit(solution)/shard_map/while/body/eval_jaxpr/all_gather | solution.py:99
  1097.9 35.2 %all-gather.13.cloned.1.call-done = bf16[1024,1024]{1,0:T(8,128)(2,1)} async-done(((bf16[1024,256]{1,0:T(8,128)(2,1)}), bf16[1024,1024]{1,0:T(8,128)(2,1)}) %all-gather.13.cloned.1.call-update) | async-done | bytes 2097168 | tf_op jit(solution)/shard_map/while/body/eval_jaxpr/all_gather | solution.py:76
  1138.6 59.7 %all-gather.11.cloned.1.call-done = bf16[2,1024,768]{2,1,0:T(8,128)(2,1)} async-done(((bf16[2,256,768]{2,1,0:T(8,128)(2,1)}), bf16[2,1024,768]{2,1,0:T(8,128)(2,1)}) %all-gather.11.cloned.1.call-update) | async-done | bytes 3145744 | tf_op jit(solution)/shard_map/while/body/eval_jaxpr/all_gather | solution.py:98
  1198.3 35.9 %all-gather.9.cloned.1.call-done = bf16[1024,1024]{1,0:T(8,128)(2,1)} async-done(((bf16[1024,256]{1,0:T(8,128)(2,1)}), bf16[1024,1024]{1,0:T(8,128)(2,1)}) %all-gather.9.cloned.1.call-update) | async-done | bytes 2097168 | tf_op jit(solution)/shard_map/while/body/eval_jaxpr/all_gather | solution.py:73
  1250.1 52.8 %reduce-scatter.12.cloned.1.call-done = f32[1024,256]{1,0:T(8,128)} async-done(((f32[1024,1024]{1,0:T(8,128)}), f32[1024,256]{1,0:T(8,128)}) %reduce-scatter.12.cloned.1.call-update) | async-done | bytes 1048592 | tf_op jit(solution)/shard_map/while/body/eval_jaxpr/reduce_scatter | solution.py:82
  1317.0 35.0 %all-gather.17.cloned.1.call-done = bf16[1024,1024]{1,0:T(8,128)(2,1)} async-done(((bf16[1024,256]{1,0:T(8,128)(2,1)}), bf16[1024,1024]{1,0:T(8,128)(2,1)}) %all-gather.17.cloned.1.call-update) | async-done | bytes 2097168 | tf_op jit(solution)/shard_map/while/body/eval_jaxpr/all_gather | solution.py:76
  1355.2 39.5 %while.103 = (s32[]{:T(128)}, f32[2048,128]{1,0:T(8,128)S(1)}, f32[2048,128]{1,0:T(8,128)}, f32[2,512,2,128]{3,1,0,2:T(8,128)}, s32[2048]{0:T(1024)S(1)}, /*inde...) while((s32[]{:T(128)}, f32[2048,128]{1,0:T(8,128)S(1)}, ...), condition=%wide.region_15.15_spmd.clone, body=%wide.region_13.14_spmd.clone.sunk | while | flops 2724597760 | bytes 87093640 | solution.py:210
  1457.1 32.5 %reduce-scatter.22.cloned.1.call-done = f32[768,128]{1,0:T(8,128)} async-done(((f32[768,1024]{1,0:T(8,128)}), f32[768,128]{1,0:T(8,128)}) %reduce-scatter.22.cloned.1.call-update) | async-done | bytes 393232 | tf_op jit(solution)/shard_map/while/body/eval_jaxpr/reduce_scatter | solution.py:245
  1490.8 53.7 %reduce-scatter.26.cloned.1.call-done = f32[1024,256]{1,0:T(8,128)} async-done(((f32[1024,1024]{1,0:T(8,128)}), f32[1024,256]{1,0:T(8,128)}) %reduce-scatter.26.cloned.1.call-update) | async-done | bytes 1048592 | tf_op jit(solution)/shard_map/while/body/eval_jaxpr/reduce_scatter | solution.py:79
  1546.6 70.0 %reduce-scatter.20.cloned.1.call-done = f32[2,128,768]{2,1,0:T(8,128)} async-done(((f32[2,1024,768]{2,1,0:T(8,128)}), f32[2,128,768]{2,1,0:T(8,128)}) %reduce-scatter.20.cloned.1.call-update) | async-done | bytes 786448 | tf_op jit(solution)/shard_map/while/body/eval_jaxpr/reduce_scatter | solution.py:244
  1618.0 31.5 %reduce-scatter.18.cloned.1.call-done = f32[256,128]{1,0:T(8,128)} async-done(((f32[256,1024]{1,0:T(8,128)}), f32[256,128]{1,0:T(8,128)}) %reduce-scatter.18.cloned.1.call-update) | async-done | bytes 131088 | tf_op jit(solution)/shard_map/while/body/eval_jaxpr/reduce_scatter | solution.py:243
  1650.5 31.8 %reduce-scatter.14.cloned.1.call-done = f32[128,256]{1,0:T(8,128)} async-done(((f32[1024,256]{1,0:T(8,128)}), f32[128,256]{1,0:T(8,128)}) %reduce-scatter.14.cloned.1.call-update) | async-done | bytes 131088 | tf_op jit(solution)/shard_map/while/body/eval_jaxpr/reduce_scatter | solution.py:241
  1683.9 31.2 %reduce-scatter.16.cloned.1.call-done = f32[128,256]{1,0:T(8,128)} async-done(((f32[1024,256]{1,0:T(8,128)}), f32[128,256]{1,0:T(8,128)}) %reduce-scatter.16.cloned.1.call-update) | async-done | bytes 131088 | tf_op jit(solution)/shard_map/while/body/eval_jaxpr/reduce_scatter | solution.py:242
  1716.1 53.1 %reduce-scatter.24.cloned.1.call-done = f32[1024,256]{1,0:T(8,128)} async-done(((f32[1024,1024]{1,0:T(8,128)}), f32[1024,256]{1,0:T(8,128)}) %reduce-scatter.24.cloned.1.call-update) | async-done | bytes 1048592 | tf_op jit(solution)/shard_map/while/body/eval_jaxpr/reduce_scatter | solution.py:82
  (551 shorter events, 614.4 us)
Async XLA Ops:
  10.2 69.1 %all-gather.7.cloned.1.call-start = ((), (), s32[]{:S(2)}) async-start(), calls=%async_computation.9 | async-start | bytes 2621440 | tf_op jit(solution)/shard_map/while/body/eval_jaxpr/all_gather | solution.py:73
  25.6 147.9 %reduce-scatter.10.cloned.1.call-start = ((), (), s32[]{:S(2)}) async-start(), calls=%async_computation.10 | async-start | bytes 5242880 | tf_op jit(solution)/shard_map/while/body/eval_jaxpr/reduce_scatter | solution.py:79
  121.8 91.0 %all-gather.15.cloned.1.call-start = ((), (), s32[]{:S(2)}) async-start(), calls=%async_computation.14 | async-start | bytes 1966080 | tf_op jit(solution)/shard_map/while/body/eval_jaxpr/all_gather | solution.py:99
  122.6 125.5 %all-gather.13.cloned.1.call-start = ((), (), s32[]{:S(2)}) async-start(), calls=%async_computation.13 | async-start | bytes 2621440 | tf_op jit(solution)/shard_map/while/body/eval_jaxpr/all_gather | solution.py:76
  125.4 187.7 %all-gather.11.cloned.1.call-start = ((), (), s32[]{:S(2)}) async-start(), calls=%async_computation.12 | async-start | bytes 3932160 | tf_op jit(solution)/shard_map/while/body/eval_jaxpr/all_gather | solution.py:98
  126.0 222.8 %all-gather.9.cloned.1.call-start = ((), (), s32[]{:S(2)}) async-start(), calls=%async_computation.11 | async-start | bytes 2621440 | tf_op jit(solution)/shard_map/while/body/eval_jaxpr/all_gather | solution.py:73
  185.5 231.9 %reduce-scatter.12.cloned.1.call-start = ((), (), s32[]{:S(2)}) async-start(), calls=%async_computation.15 | async-start | bytes 5242880 | tf_op jit(solution)/shard_map/while/body/eval_jaxpr/reduce_scatter | solution.py:82
  364.6 102.0 %all-gather.17.cloned.1.call-start = ((), (), s32[]{:S(2)}) async-start(), calls=%async_computation.16 | async-start | bytes 2621440 | tf_op jit(solution)/shard_map/while/body/eval_jaxpr/all_gather | solution.py:76
  431.4 130.3 %all-reduce.3.cloned.1.call-start = ((), (), s32[]{:S(2)}) async-start(), calls=%async_computation.18 | async-start | bytes 1048576 | tf_op jit(solution)/shard_map/while/body/eval_jaxpr/psum | solution.py:218
  516.2 88.1 %reduce-scatter.22.cloned.1.call-start = ((), (), s32[]{:S(2)}) async-start(), calls=%async_computation.22 | async-start | bytes 3538944 | tf_op jit(solution)/shard_map/while/body/eval_jaxpr/reduce_scatter | solution.py:245
  522.0 137.3 %reduce-scatter.26.cloned.1.call-start = ((), (), s32[]{:S(2)}) async-start(), calls=%async_computation.24 | async-start | bytes 5242880 | tf_op jit(solution)/shard_map/while/body/eval_jaxpr/reduce_scatter | solution.py:79
  528.7 202.6 %reduce-scatter.20.cloned.1.call-start = ((), (), s32[]{:S(2)}) async-start(), calls=%async_computation.21 | async-start | bytes 7077888 | tf_op jit(solution)/shard_map/while/body/eval_jaxpr/reduce_scatter | solution.py:244
  538.7 225.6 %reduce-scatter.18.cloned.1.call-start = ((), (), s32[]{:S(2)}) async-start(), calls=%async_computation.20 | async-start | bytes 1179648 | tf_op jit(solution)/shard_map/while/body/eval_jaxpr/reduce_scatter | solution.py:243
  543.1 253.9 %reduce-scatter.14.cloned.1.call-start = ((), (), s32[]{:S(2)}) async-start(), calls=%async_computation.17 | async-start | bytes 1179648 | tf_op jit(solution)/shard_map/while/body/eval_jaxpr/reduce_scatter | solution.py:241
  551.6 278.1 %reduce-scatter.16.cloned.1.call-start = ((), (), s32[]{:S(2)}) async-start(), calls=%async_computation.19 | async-start | bytes 1179648 | tf_op jit(solution)/shard_map/while/body/eval_jaxpr/reduce_scatter | solution.py:242
  566.5 316.9 %reduce-scatter.24.cloned.1.call-start = ((), (), s32[]{:S(2)}) async-start(), calls=%async_computation.23 | async-start | bytes 5242880 | tf_op jit(solution)/shard_map/while/body/eval_jaxpr/reduce_scatter | solution.py:82
  897.5 65.8 %all-gather.7.cloned.1.call-start = ((), (), s32[]{:S(2)}) async-start(), calls=%async_computation.9 | async-start | bytes 2621440 | tf_op jit(solution)/shard_map/while/body/eval_jaxpr/all_gather | solution.py:73
  910.3 148.2 %reduce-scatter.10.cloned.1.call-start = ((), (), s32[]{:S(2)}) async-start(), calls=%async_computation.10 | async-start | bytes 5242880 | tf_op jit(solution)/shard_map/while/body/eval_jaxpr/reduce_scatter | solution.py:79
  1005.9 92.0 %all-gather.15.cloned.1.call-start = ((), (), s32[]{:S(2)}) async-start(), calls=%async_computation.14 | async-start | bytes 1966080 | tf_op jit(solution)/shard_map/while/body/eval_jaxpr/all_gather | solution.py:99
  1006.6 126.5 %all-gather.13.cloned.1.call-start = ((), (), s32[]{:S(2)}) async-start(), calls=%async_computation.13 | async-start | bytes 2621440 | tf_op jit(solution)/shard_map/while/body/eval_jaxpr/all_gather | solution.py:76
  1009.4 188.9 %all-gather.11.cloned.1.call-start = ((), (), s32[]{:S(2)}) async-start(), calls=%async_computation.12 | async-start | bytes 3932160 | tf_op jit(solution)/shard_map/while/body/eval_jaxpr/all_gather | solution.py:98
  1010.2 224.0 %all-gather.9.cloned.1.call-start = ((), (), s32[]{:S(2)}) async-start(), calls=%async_computation.11 | async-start | bytes 2621440 | tf_op jit(solution)/shard_map/while/body/eval_jaxpr/all_gather | solution.py:73
  1070.6 232.2 %reduce-scatter.12.cloned.1.call-start = ((), (), s32[]{:S(2)}) async-start(), calls=%async_computation.15 | async-start | bytes 5242880 | tf_op jit(solution)/shard_map/while/body/eval_jaxpr/reduce_scatter | solution.py:82
  1250.0 102.0 %all-gather.17.cloned.1.call-start = ((), (), s32[]{:S(2)}) async-start(), calls=%async_computation.16 | async-start | bytes 2621440 | tf_op jit(solution)/shard_map/while/body/eval_jaxpr/all_gather | solution.py:76
  1316.8 130.3 %all-reduce.3.cloned.1.call-start = ((), (), s32[]{:S(2)}) async-start(), calls=%async_computation.18 | async-start | bytes 1048576 | tf_op jit(solution)/shard_map/while/body/eval_jaxpr/psum | solution.py:218
  1401.6 88.0 %reduce-scatter.22.cloned.1.call-start = ((), (), s32[]{:S(2)}) async-start(), calls=%async_computation.22 | async-start | bytes 3538944 | tf_op jit(solution)/shard_map/while/body/eval_jaxpr/reduce_scatter | solution.py:245
  1407.4 137.0 %reduce-scatter.26.cloned.1.call-start = ((), (), s32[]{:S(2)}) async-start(), calls=%async_computation.24 | async-start | bytes 5242880 | tf_op jit(solution)/shard_map/while/body/eval_jaxpr/reduce_scatter | solution.py:79
  1414.1 202.5 %reduce-scatter.20.cloned.1.call-start = ((), (), s32[]{:S(2)}) async-start(), calls=%async_computation.21 | async-start | bytes 7077888 | tf_op jit(solution)/shard_map/while/body/eval_jaxpr/reduce_scatter | solution.py:244
  1424.1 225.4 %reduce-scatter.18.cloned.1.call-start = ((), (), s32[]{:S(2)}) async-start(), calls=%async_computation.20 | async-start | bytes 1179648 | tf_op jit(solution)/shard_map/while/body/eval_jaxpr/reduce_scatter | solution.py:243
  1428.5 253.8 %reduce-scatter.14.cloned.1.call-start = ((), (), s32[]{:S(2)}) async-start(), calls=%async_computation.17 | async-start | bytes 1179648 | tf_op jit(solution)/shard_map/while/body/eval_jaxpr/reduce_scatter | solution.py:241
  1437.0 278.1 %reduce-scatter.16.cloned.1.call-start = ((), (), s32[]{:S(2)}) async-start(), calls=%async_computation.19 | async-start | bytes 1179648 | tf_op jit(solution)/shard_map/while/body/eval_jaxpr/reduce_scatter | solution.py:242
  1451.9 317.3 %reduce-scatter.24.cloned.1.call-start = ((), (), s32[]{:S(2)}) async-start(), calls=%async_computation.23 | async-start | bytes 5242880 | tf_op jit(solution)/shard_map/while/body/eval_jaxpr/reduce_scatter | solution.py:82
  (112 other events, 5692.1 us)
Sparse Core Ops, SparseCore 0:
  25.7 34.5 all-gather.6
  122.0 51.4 reduce-scatter.9
  175.1 37.6 all-gather.14
  214.6 33.3 all-gather.12
  249.6 63.4 all-gather.10
  314.9 33.8 all-gather.8
  364.8 52.6 reduce-scatter.11
  431.5 35.0 all-gather.16
  516.3 45.3 all-reduce.2
  563.9 40.3 reduce-scatter.21
  607.5 51.7 reduce-scatter.25
  661.4 69.7 reduce-scatter.19
  733.5 30.7 reduce-scatter.17
  766.4 30.5 reduce-scatter.13
  799.2 30.5 reduce-scatter.15
  832.6 50.8 reduce-scatter.23
  910.4 35.1 all-gather.6
  1006.0 52.5 reduce-scatter.9
  1060.2 37.6 all-gather.14
  1099.7 33.3 all-gather.12
  1134.8 63.4 all-gather.10
  1200.3 33.8 all-gather.8
  1250.1 52.6 reduce-scatter.11
  1316.9 35.0 all-gather.16
  1401.7 45.3 all-reduce.2
  1449.2 40.3 reduce-scatter.21
  1492.7 51.7 reduce-scatter.25
  1546.8 69.7 reduce-scatter.19
  1618.9 30.5 reduce-scatter.17
  1651.6 30.5 reduce-scatter.13
  1684.6 30.5 reduce-scatter.15
  1718.1 51.0 reduce-scatter.23
where the time goes:
time: 1810 us
  waiting for transfers between devices  1220 us (67%)
  blocking collectives  187 us (10%)
  matrix products  187 us (10%)
  other arithmetic  134 us (7%)
  local copies, waits for them, and re-layouts  44.2 us (2%)
    reduce_scatter x4, waiting for transfers between devices, sum_normed(): return lax.psum_scatter(values, 'tp', scatter_dimension=1, tiled=True)  211 us
    reduce_scatter x4, waiting for transfers between devices, sum_branch(): return lax.psum_scatter(values, 'tp', scatter_dimension=1, tiled=True)  203 us
    all_gather x4, waiting for transfers between devices, gather_grads(): return lax.all_gather(values, 'tp', axis=1, tiled=True)  140 us
    reduce_scatter x2, waiting for transfers between devices, slot_step(): lax.psum_scatter(grad_wgateup, ('fsdp', 'ctx'), scatter_dimension=1, tile...  140 us
    all_gather x2, waiting for transfers between devices, slot_step(): lax.all_gather(w_gateup, 'fsdp', axis=1, tiled=True)  119 us
    psum x8, blocking collectives, row_total(): return lax.psum(values, 'tp')  73.7 us
    all_gather x4, waiting for transfers between devices, gather_rows(): return lax.all_gather(values, 'tp', axis=1, tiled=True)  71.6 us
    reduce_scatter x2, waiting for transfers between devices, slot_step(): lax.psum_scatter(grad_wdown, ('fsdp', 'ctx'), scatter_dimension=1, tiled=...  65.1 us
  transfers between devices with their start and end apart: 36, of which 32 were waited for; matrix products, arithmetic and copies ran while one was open for 8% of the time, Pallas kernels for 0%

commit v1 on v0

v1 whole, which is shorter than its diff:
```python
import functools
import math

import jax
import jax.numpy as jnp
from jax import lax
from jax.experimental import pallas as pl
from jax.experimental.pallas import tpu as pltpu
from jax.sharding import Mesh
from jax.sharding import PartitionSpec as P

D = 1024
HEAD = 128
WINDOW = 1024
ROWS = 256
EPSILON = 1e-06
NEG = -1e30
LOG2E = math.log2(math.e)
BF = jnp.bfloat16
F32 = jnp.float32


def mm(a, b):
    return jnp.dot(a, b, preferred_element_type=F32)


def mm_nt(a, b):
    return lax.dot_general(a, b, (((1,), (1,)), ((), ())), preferred_element_type=F32)


def mm_tn(a, b):
    return lax.dot_general(a, b, (((0,), (0,)), ((), ())), preferred_element_type=F32)


def key_bias(step, start, length):
    span = WINDOW + ROWS
    row = lax.broadcasted_iota(jnp.int32, (ROWS, span), 0)
    col = lax.broadcasted_iota(jnp.int32, (ROWS, span), 1)
    pos = start - WINDOW + step * ROWS + col
    ahead = col - row - WINDOW
    inside = (ahead <= 0) & (ahead > -WINDOW) & (pos >= 0) & (pos < length)
    return jnp.where(inside | (ahead == 0), 0.0, NEG).astype(F32)


def attend_kernel(heads, where_ref, q_ref, kv_ref, mixed_ref, lse_ref, bias_ref):
    step = pl.program_id(0)
    span = WINDOW + ROWS
    bias_ref[...] = key_bias(step, where_ref[0], where_ref[1])
    keys = kv_ref[pl.ds(step * ROWS, span), :HEAD]
    values = kv_ref[pl.ds(step * ROWS, span), HEAD:]
    for h in range(heads):
        cols = slice(h * HEAD, (h + 1) * HEAD)
        s = mm_nt(q_ref[:, cols], keys) * (HEAD**-0.5 * LOG2E) + bias_ref[...]
        top = jnp.max(s, axis=1, keepdims=True)
        p = jnp.exp2(s - top)
        total = jnp.sum(p, axis=1, keepdims=True)
        mixed = mm(p.astype(BF), values) / total
        mixed_ref[:, cols] = mixed.astype(BF)
        lse_ref[:, h : h + 1] = top + jnp.log2(total)


def attend(q, kv, where):
    rows, width = q.shape
    heads = width // HEAD
    steps = rows // ROWS
    return pl.pallas_call(
        functools.partial(attend_kernel, heads),
        grid_spec=pltpu.PrefetchScalarGridSpec(
            num_scalar_prefetch=1,
            grid=(steps,),
            in_specs=[
                pl.BlockSpec((ROWS, width), lambda i, w: (i, 0)),
                pl.BlockSpec(kv.shape, lambda i, w: (0, 0)),
            ],
            out_specs=[
                pl.BlockSpec((ROWS, width), lambda i, w: (i, 0)),
                pl.BlockSpec((ROWS, heads), lambda i, w: (i, 0)),
            ],
            scratch_shapes=[pltpu.VMEM((ROWS, WINDOW + ROWS), F32)],
        ),
        out_shape=[
            jax.ShapeDtypeStruct((rows, width), BF),
            jax.ShapeDtypeStruct((rows, heads), F32),
        ],
        compiler_params=pltpu.CompilerParams(vmem_limit_bytes=40 << 20),
        cost_estimate=pl.CostEstimate(
            flops=4 * rows * width * (WINDOW + ROWS),
            bytes_accessed=2 * q.size * 2 + kv.size * 2,
            transcendentals=rows * heads * (WINDOW + ROWS),
        ),
        name="attend",
    )(where, q, kv)


def attend_back_kernel(
    heads, where_ref, q_ref, kv_ref, mixed_ref, lse_ref, gm_ref, gq_ref, gkv_ref, bias_ref
):
    step = pl.program_id(0)
    span = WINDOW + ROWS
    scale = HEAD**-0.5

    @pl.when(step == 0)
    def _():
        gkv_ref[...] = jnp.zeros_like(gkv_ref)

    bias_ref[...] = key_bias(step, where_ref[0], where_ref[1])
    here = pl.ds(step * ROWS, span)
    keys = kv_ref[here, :HEAD]
    values = kv_ref[here, HEAD:]
    for h in range(heads):
        cols = slice(h * HEAD, (h + 1) * HEAD)
        q = q_ref[:, cols]
        gm = gm_ref[:, cols]
        s = mm_nt(q, keys) * (scale * LOG2E) + bias_ref[...]
        p = jnp.exp2(s - lse_ref[:, h : h + 1])
        gp = mm_nt(gm, values)
        inner = jnp.sum(
            gm.astype(F32) * mixed_ref[:, cols].astype(F32), axis=1, keepdims=True
        )
        gs = (p * (gp - inner)).astype(BF)
        gq_ref[:, cols] = mm(gs, keys) * scale
        gkv_ref[here, :HEAD] += mm_tn(gs, q) * scale
        gkv_ref[here, HEAD:] += mm_tn(p.astype(BF), gm)


def attend_back(q, kv, mixed, lse, grad_mixed, where):
    rows, width = q.shape
    heads = width // HEAD
    steps = rows // ROWS
    block = pl.BlockSpec((ROWS, width), lambda i, w: (i, 0))
    whole = pl.BlockSpec(kv.shape, lambda i, w: (0, 0))
    return pl.pallas_call(
        functools.partial(attend_back_kernel, heads),
        grid_spec=pltpu.PrefetchScalarGridSpec(
            num_scalar_prefetch=1,
            grid=(steps,),
            in_specs=[
                block,
                whole,
                block,
                pl.BlockSpec((ROWS, heads), lambda i, w: (i, 0)),
                block,
            ],
            out_specs=[block, whole],
            scratch_shapes=[pltpu.VMEM((ROWS, WINDOW + ROWS), F32)],
        ),
        out_shape=[
            jax.ShapeDtypeStruct((rows, width), F32),
            jax.ShapeDtypeStruct(kv.shape, F32),
        ],
        compiler_params=pltpu.CompilerParams(vmem_limit_bytes=40 << 20),
        cost_estimate=pl.CostEstimate(
            flops=10 * rows * width * (WINDOW + ROWS),
            bytes_accessed=5 * q.size * 2 + kv.size * 6,
            transcendentals=rows * heads * (WINDOW + ROWS),
        ),
        name="attend_back",
    )(where, q, kv, mixed, lse, grad_mixed)


def swap(value, axis):
    return lax.ppermute(value, axis, [(0, 1), (1, 0)])


def swap_both(value):
    return lax.ppermute(value, ("ty", "tx"), [(i, i ^ 3) for i in range(4)])


def pick(flag, ones, zeros):
    return jnp.where(flag == 1, ones, zeros)


def pair(flag, own, other, axis):
    return jnp.concatenate([pick(flag, other, own), pick(flag, own, other)], axis=axis)


def half_at(value, index, axis):
    size = value.shape[axis] // 2
    return lax.dynamic_slice_in_dim(value, index * size, size, axis)


def along_fsdp(blocks, index):
    count = blocks.shape[0]
    total = lax.dynamic_index_in_dim(blocks, index, 0, False).astype(F32)
    if count > 4:
        return lax.psum_scatter(blocks, "fsdp", scatter_dimension=0, tiled=False).astype(F32)
    for step in range(1, count):
        block = lax.dynamic_index_in_dim(blocks, (index + step) % count, 0, False)
        came = lax.ppermute(block, "fsdp", [(i, (i + step) % count) for i in range(count)])
        total = total + came.astype(F32)
    return total


def body(
    tokens, lengths, w_query, w_keyval, w_out, w_gateup, w_down, gain_attn, gain_mlp, cotangent
):
    shards = lax.axis_size("fsdp")
    z, c = lax.axis_index("fsdp"), lax.axis_index("ctx")
    y, x = lax.axis_index("ty"), lax.axis_index("tx")
    seq_rows = tokens.shape[1]
    rows = seq_rows // 2
    feats = tokens.shape[2]
    depth = w_query.shape[0]
    sub = depth // 2
    eighth = depth // 8
    length = lax.dynamic_index_in_dim(lengths, y, 0, False)
    row_start = c * seq_rows + x * rows
    where = jnp.stack([row_start, length]).astype(jnp.int32)

    keyval_part = lax.dynamic_slice_in_dim(w_keyval, ((c * 2 + y) * 2 + x) * eighth, eighth, 0)
    qkv_part = jnp.concatenate([half_at(w_query, c, 0), keyval_part], axis=0)
    qkv_all = lax.all_gather(qkv_part, ("ty", "tx", "fsdp", "ctx"), axis=0, tiled=False)
    qkv_all = qkv_all.reshape(4, shards, 2, sub + eighth, feats)
    w_q = qkv_all[:, :, :, :sub].reshape(4, D, feats)
    w_q = w_q.transpose(1, 0, 2).reshape(D, 4 * feats)
    w_kv = qkv_all[:, :, :, sub:].transpose(1, 2, 0, 3, 4).reshape(D, feats)

    out_part = half_at(w_out, c, 0)
    out_all = lax.all_gather(out_part, ("ty", "tx", "ctx", "fsdp"), axis=0, tiled=False)
    w_o = out_all.reshape(8, shards, -1, depth).transpose(0, 2, 1, 3).reshape(-1, D)

    units = w_gateup.shape[2] // 2
    gateup_part = half_at(w_gateup, c, 2)
    down_part = half_at(w_down, c, 0)
    mlp_part = jnp.concatenate([gateup_part[0], gateup_part[1], down_part.T], axis=1)
    w_mlp = lax.all_gather(mlp_part, ("tx", "fsdp"), axis=0, tiled=False)
    w_mlp = w_mlp.reshape(2, D, 3 * units)

    gains = jnp.stack([gain_attn, gain_mlp])

    def piece(slot, half):
        block = lax.dynamic_index_in_dim(tokens, slot, 0, False)
        block = half_at(block, half, 0)
        return jnp.concatenate([block, gains, jnp.zeros((14, feats), BF)], axis=0)

    across_x = swap(piece(y, 1 - x), "tx")
    across_y = swap(piece(1 - y, x), "ty")
    across_both = swap_both(piece(1 - y, 1 - x))
    mine = piece(y, x)
    full = pair(
        y, pair(x, mine, across_x, 1), pair(x, across_y, across_both, 1), 1
    )
    resid = full[:rows].astype(F32)
    gain_a = full[rows].astype(F32)
    gain_m = full[rows + 1].astype(F32)

    t_local = c * seq_rows + jnp.arange(seq_rows, dtype=jnp.int32)
    cot = jnp.where((t_local[None, :] < lengths[:, None])[:, :, None], cotangent, 0)
    cot_x = swap(half_at(cot, 1 - x, 1), "tx")
    cot_pair = pair(x, half_at(cot, x, 1), cot_x, 2)
    cot_other = swap(cot_pair, "ty")
    cot_full = pair(y, cot_pair, cot_other, 2)
    cot_full = jnp.concatenate([pick(y, cot_full[1], cot_full[0]), pick(y, cot_full[0], cot_full[1])], axis=0)
    grad_rows = jnp.concatenate([cot_full, swap(cot_full, "ctx")], axis=0)
    grad_final = cot_full[:rows].astype(F32)

    inv_attn = lax.rsqrt(jnp.mean(resid * resid, axis=1, keepdims=True) + EPSILON)
    hat_attn = resid * inv_attn
    normed_attn = (hat_attn * gain_a).astype(BF)

    half_width = HEAD // 2
    freq = 10000.0 ** (-jnp.arange(half_width, dtype=F32) / half_width)
    angles = (row_start + jnp.arange(rows, dtype=jnp.int32)).astype(F32)[:, None] * freq[None, :]
    cosine, sine = jnp.cos(angles), jnp.sin(angles)
    cos_full = jnp.concatenate([cosine, cosine], axis=1)[:, None, :]
    sin_full = jnp.concatenate([-sine, sine], axis=1)[:, None, :]

    def rotate(value, direction):
        value = value.reshape(rows, -1, HEAD)
        turned = jnp.concatenate([value[..., half_width:], value[..., :half_width]], axis=2)
        return (value * cos_full + turned * (direction * sin_full)).reshape(rows, -1)

    q = rotate(mm(normed_attn, w_q), 1.0).astype(BF)
    keyval_lin = mm(normed_attn, w_kv)
    kv_own = jnp.concatenate([rotate(keyval_lin[:, :HEAD], 1.0), keyval_lin[:, HEAD:]], axis=1)
    kv_own = kv_own.astype(BF)
    kv_x = swap(kv_own, "tx")
    kv_c = swap(jnp.concatenate([kv_own, kv_x], axis=1), "ctx")
    kv_all = jnp.concatenate(
        [kv_c[:, :feats], pick(x, kv_x, kv_c[:, feats:]), kv_own], axis=0
    )
    mixed, lse = attend(q, kv_all, where)
    hidden = resid + mm(mixed, w_o)

    inv_mlp = lax.rsqrt(jnp.mean(hidden * hidden, axis=1, keepdims=True) + EPSILON)
    hat_mlp = hidden * inv_mlp
    normed_mlp = (hat_mlp * gain_m).astype(BF)
    two = jnp.concatenate([normed_mlp, swap(normed_mlp, "ty")], axis=0)
    mlp_rows = jnp.concatenate([two, swap(two, "ctx")], axis=0)

    grad_normed = 0.0
    branch = 0.0
    grad_parts = []
    for part in range(2):
        w_gu = w_mlp[part, :, : 2 * units]
        w_dt = w_mlp[part, :, 2 * units :]
        lin = mm(mlp_rows, w_gu)
        gate, up = lin[:, :units], lin[:, units:]
        grad_active = mm(grad_rows, w_dt)
        inner = math.sqrt(2 / math.pi) * (gate + 0.044715 * gate * gate * gate)
        tanh = jnp.tanh(inner)
        gelu = 0.5 * gate * (1.0 + tanh)
        slope = 0.5 * (1.0 + tanh) + 0.5 * gate * (1.0 - tanh * tanh) * math.sqrt(
            2 / math.pi
        ) * (1.0 + 3 * 0.044715 * gate * gate)
        active = (gelu * up).astype(BF)
        grad_gu = jnp.concatenate(
            [(grad_active * up * slope).astype(BF), (grad_active * gelu).astype(BF)], axis=1
        )
        grad_normed = grad_normed + mm_nt(grad_gu, w_gu)
        branch = branch + mm_nt(active, w_dt)
        grad_parts.append(
            jnp.concatenate(
                [mm_tn(mlp_rows, grad_gu).astype(BF), mm_tn(grad_rows, active).astype(BF)], axis=1
            )
        )

    group = 2 * rows
    grad_normed = grad_normed.astype(BF)
    grad_normed = grad_normed[:group].astype(F32) + swap(grad_normed[group:], "ctx").astype(F32)
    grad_normed = grad_normed[:rows] + swap(grad_normed[rows:].astype(BF), "ty").astype(F32)

    branch = branch.astype(BF)
    partial = branch[:group].astype(F32) + swap(branch[group:], "ctx").astype(F32)
    partial = partial.reshape(2, rows, D)
    partial = jnp.stack([partial[0] + hidden, partial[1]]).astype(BF)
    came = swap(half_at(partial, 1 - y, 2), "ty")
    summed = half_at(partial, y, 2).astype(F32) + came[::-1].astype(F32)
    summed = summed.astype(BF)
    summed = jnp.stack([pick(y, summed[1], summed[0]), pick(y, summed[0], summed[1])])
    outputs = pair(x, half_at(summed, x, 2), swap(half_at(summed, 1 - x, 2), "tx"), 1)

    mlp_grads = jnp.stack(grad_parts).reshape(2 * shards, depth, 3 * units)
    mlp_grads = lax.psum_scatter(mlp_grads, ("tx", "fsdp"), scatter_dimension=0, tiled=False)
    mlp_other = swap(half_at(mlp_grads, 1 - c, 0), "ctx")
    mlp_own = half_at(mlp_grads, c, 0)

    def units_of(at):
        cut = slice(at * units, (at + 1) * units)
        return pair(c, mlp_own[:, cut], mlp_other[:, cut], 1).astype(F32)

    grad_gateup = jnp.stack([units_of(0), units_of(1)])
    grad_down = units_of(2).T

    def norm_back(grad, hat, inv, gain):
        g = grad * gain
        dots = jnp.mean(g * hat, axis=1, keepdims=True)
        return inv * (g - hat * dots), jnp.sum(grad * hat, axis=0)

    back, grad_gain_mlp = norm_back(grad_normed, hat_mlp, inv_mlp, gain_m)
    grad_hidden = grad_final + back
    grad_hidden_low = grad_hidden.astype(BF)
    grad_mixed = mm_nt(grad_hidden_low, w_o).astype(BF)
    grad_wout = mm_tn(mixed, grad_hidden_low).astype(BF)
    grad_wout = grad_wout.reshape(4, -1, shards, 2, sub).transpose(0, 2, 3, 1, 4)
    grad_wout = grad_wout.reshape((-1,) + grad_wout.shape[3:])
    grad_output_proj = lax.psum_scatter(
        grad_wout, ("ty", "tx", "fsdp", "ctx"), scatter_dimension=0, tiled=False
    ).astype(F32)

    grad_q, grad_kv = attend_back(q, kv_all, mixed, lse, grad_mixed, where)
    kv_far, kv_near, kv_here = grad_kv[:rows], grad_kv[rows : 2 * rows], grad_kv[2 * rows :]
    near = swap(kv_near.astype(BF), "tx").astype(F32)
    sent = swap((kv_far + pick(x, near, 0.0)).astype(BF), "ctx").astype(F32)
    grad_kv = kv_here + pick(x, 0.0, near) + sent
    grad_kv_lin = jnp.concatenate(
        [rotate(grad_kv[:, :HEAD], -1.0), grad_kv[:, HEAD:]], axis=1
    ).astype(BF)
    grad_q_lin = rotate(grad_q, -1.0).astype(BF)
    grad_wq = mm_tn(normed_attn, grad_q_lin).astype(BF)
    grad_wkv = mm_tn(normed_attn, grad_kv_lin).astype(BF)
    grad_normed_a = mm_nt(grad_q_lin, w_q) + mm_nt(grad_kv_lin, w_kv)
    back, grad_gain_attn = norm_back(grad_normed_a, hat_attn, inv_attn, gain_a)
    grad_row = (grad_hidden + back).astype(BF)

    blocks = grad_row.reshape(rows, 4, feats)
    me = y * 2 + x

    def block_for(other):
        return lax.dynamic_index_in_dim(blocks, other, 1, False)

    from_x = swap(block_for(me ^ 1), "tx")
    from_y = swap(block_for(me ^ 2), "ty")
    from_both = swap_both(block_for(me ^ 3))
    slot_own = pair(x, block_for(me), from_x, 0)
    slot_other = pair(x, from_y, from_both, 0)
    grad_tokens = jnp.stack(
        [pick(y, slot_other, slot_own), pick(y, slot_own, slot_other)]
    ).astype(F32)

    gain_grads = jnp.stack([grad_gain_attn, grad_gain_mlp])
    gain_high = gain_grads.astype(BF)
    gain_low = (gain_grads - gain_high.astype(F32)).astype(BF)
    gain_rows = jnp.concatenate([gain_high, gain_low, jnp.zeros((12, D), BF)], axis=0)
    wq_blocks = grad_wq.reshape(shards, 2, sub, 4, feats)
    wkv_blocks = grad_wkv.reshape(shards, 2, 4, eighth, feats).transpose(0, 1, 3, 2, 4)
    all_blocks = jnp.concatenate([wq_blocks, wkv_blocks], axis=2)
    all_blocks = all_blocks.transpose(1, 3, 0, 2, 4).reshape(2, 4, shards * (sub + eighth), feats)
    gain_blocks = gain_rows.reshape(16, 4, feats).transpose(1, 0, 2)
    all_blocks = jnp.concatenate(
        [all_blocks, jnp.broadcast_to(gain_blocks, (2,) + gain_blocks.shape)], axis=2
    )
    send_c = lax.dynamic_index_in_dim(all_blocks, 1 - c, 0, False)
    keep_c = lax.dynamic_index_in_dim(all_blocks, c, 0, False)
    chip = (keep_c.astype(F32) + swap(send_c, "ctx").astype(F32)).astype(BF)

    def chip_for(other):
        return lax.dynamic_index_in_dim(chip, other, 0, False)

    plane = (
        chip_for(me).astype(F32)
        + swap(chip_for(me ^ 1), "tx").astype(F32)
        + swap(chip_for(me ^ 2), "ty").astype(F32)
        + swap_both(chip_for(me ^ 3)).astype(F32)
    ).astype(BF)
    gain_part = jnp.broadcast_to(plane[-16:], (shards, 16, feats))
    plane = plane[:-16].reshape(shards, sub + eighth, feats)
    total = along_fsdp(jnp.concatenate([plane, gain_part], axis=1), z)
    grad_query = total[:sub]
    kv_total = total[sub : sub + eighth].astype(BF)
    gain_total = total[sub + eighth :]
    gain_sums = gain_total[:2] + gain_total[2:4]
    kv_pair = pair(x, kv_total, swap(kv_total, "tx"), 0)
    grad_keyval = pair(y, kv_pair, swap(kv_pair, "ty"), 0).astype(F32)

    return (
        outputs,
        grad_tokens,
        grad_query,
        grad_keyval,
        grad_output_proj,
        grad_gateup,
        grad_down,
        gain_sums[0],
        gain_sums[1],
    )


def solution(mesh):
    names = dict(zip(mesh.axis_names, mesh.devices.shape))
    grid = mesh.devices.reshape(names["fsdp"], names["ctx"], 2, names["tp"] // 2)
    split = Mesh(grid, ("fsdp", "ctx", "ty", "tx"))
    tp = ("ty", "tx")
    in_specs = (
        P("fsdp", "ctx", tp),
        P("fsdp"),
        P("fsdp", tp),
        P("fsdp", None),
        P(tp, "fsdp"),
        P(None, "fsdp", tp),
        P(tp, "fsdp"),
        P(tp),
        P(tp),
        P("fsdp", "ctx", tp),
    )
    out_specs = (
        P("fsdp", "ctx", tp),
        P("fsdp", "ctx", tp),
        P(("fsdp", "ctx"), tp),
        P(("fsdp", "ctx"), None),
        P(tp, ("fsdp", "ctx")),
        P(None, ("fsdp", "ctx"), tp),
        P(tp, ("fsdp", "ctx")),
        P(tp),
        P(tp),
    )
    return jax.shard_map(body, mesh=split, in_specs=in_specs, out_specs=out_specs, check_vma=False)
```

time: 1810 us -> 569 us (0.31)
  waiting for transfers between devices: 1220 us -> 265 us
  blocking collectives: 187 us -> 0 us
  matrix products: 187 us -> 78.5 us
  other arithmetic: 134 us -> 54.2 us
  local copies, waits for them, and re-layouts: 44.2 us -> 87.8 us
  Pallas kernels: 0 us -> 27.9 us
  starting transfers between devices: 10.7 us -> 30.7 us
    reduce_scatter x18 -> x2, waiting for transfers between devices: 809 us -> 72.9 us  [the longest x1 72.8 us: body(): lax.psum_scatter(grad_wout, ('ty', 'tx', 'fsdp', 'ctx'), scatter_dimensio...]
    all_gather x12 -> x3, waiting for transfers between devices: 385 us -> 93.3 us  [the longest x1 56.1 us: body(): lax.all_gather(qkv_part, ('ty', 'tx', 'fsdp', 'ctx'), axis=0, tiled=False)]
    dot_general x64 -> x21, matrix products: 187 us -> 78.5 us  [the longest x7 35.4 us: mm(): return jnp.dot(a, b, preferred_element_type=F32)]
    all_gather x6 -> x0, blocking collectives: 97.8 us -> none  [the longest x2 36.3 us: slot_step(): lax.all_gather(w_out, 'fsdp', axis=1, tiled=True)]
    ppermute x4 -> x30, waiting for transfers between devices: 5.01 us -> 98.4 us  [the longest x24 88.2 us: swap(): return lax.ppermute(value, axis, [(0, 1), (1, 0)])]
    psum x9 -> x0, blocking collectives: 88.7 us -> none  [the longest x8 73.7 us: row_total(): return lax.psum(values, 'tp')]
    pallas_call x0 -> x2, Pallas kernels: none -> 27.9 us  [the longest x1 17.6 us: attend_back(): pl.pallas_call(functools.partial(attend_back_kernel, heads), grid_spec=pl...]
    while x228 -> x0, local copies, waits for them, and re-layouts: 27.2 us -> none
  transfers between devices with their start and end apart: 36 -> 35, of which waited for: 32 -> 18; matrix products, arithmetic and copies ran while one was open for 8% -> 31% of each run, Pallas kernels for 0% -> 5%
where the time goes in v1:
time: 569 us; the launch traced here: 559 us
  waiting for transfers between devices  265 us (47%)
  local copies, waits for them, and re-layouts  87.8 us (15%)
  matrix products  78.5 us (14%)
  other arithmetic  54.2 us (10%)
  starting transfers between devices  30.7 us (5%)
  Pallas kernels  27.9 us (5%)
  between operations  15.1 us (3%)
    ppermute x24, waiting for transfers between devices, swap(): return lax.ppermute(value, axis, [(0, 1), (1, 0)])  88.2 us
    reduce_scatter x1, waiting for transfers between devices, body(): lax.psum_scatter(grad_wout, ('ty', 'tx', 'fsdp', 'ctx'), scatter_dimensio...  72.8 us
    all_gather x1, waiting for transfers between devices, body(): lax.all_gather(qkv_part, ('ty', 'tx', 'fsdp', 'ctx'), axis=0, tiled=False)  56.1 us
    all_gather x1, waiting for transfers between devices, body(): lax.all_gather(out_part, ('ty', 'tx', 'ctx', 'fsdp'), axis=0, tiled=False)  37.2 us
    dot_general x7, matrix products, mm(): return jnp.dot(a, b, preferred_element_type=F32)  35.4 us
    dot_general x7, matrix products, mm_tn(): lax.dot_general(a, b, (((0,), (0,)), ((), ())), preferred_element_type=F32)  23 us
    ppermute x24, starting transfers between devices, swap(): return lax.ppermute(value, axis, [(0, 1), (1, 0)])  20.5 us
    dot_general x7, matrix products, mm_nt(): lax.dot_general(a, b, (((1,), (1,)), ((), ())), preferred_element_type=F32)  20.1 us
  transfers between devices with their start and end apart: 35, of which 18 were waited for; matrix products, arithmetic and copies ran while one was open for 31% of the time, Pallas kernels for 5%

profile of v1, /device:TPU:0, one launch (start us, length us, event | category | flops | bytes accessed | tf_op | source)
XLA Modules:
  0.0 558.8 jit_solution(6033568647369065254)
XLA Ops:
  15.0 3.9 collective-permute-start
  35.1 37.2 %all-gather.9.cloned.1.call-done = bf16[4096,256]{1,0:T(8,128)(2,1)} async-done(((bf16[128,256]{1,0:T(8,128)(2,1)}), bf16[4096,256]{1,0:T(8,128)(2,1)}) %all-gather.9.cloned.1.call-update) | async-done | bytes 2097168 | tf_op jit(solution)/shard_map/all_gather | solution.py:219
  72.3 4.3 copy.84
  76.6 56.1 %all-gather.7.cloned.1.call-done = bf16[5120,256]{1,0:T(8,128)(2,1)} async-done(((bf16[160,256]{1,0:T(8,128)(2,1)}), bf16[5120,256]{1,0:T(8,128)(2,1)}) %all-gather.7.cloned.1.call-update) | async-done | bytes 2621456 | tf_op jit(solution)/shard_map/all_gather | solution.py:212
  146.2 3.6 collective-permute-done.3
  156.9 10.3 %attend.1 = (bf16[512,1024]{1,0:T(8,128)(2,1)S(1)}, f32[512,8]{1,0:T(8,128)S(1)}) custom-call(s32[2]{0:T(128)S(1)} %pad_add_fusion.where_ref, bf16[512,1024]{1,0:T(8,128)(2,1)S(1)} %copy.102.q_ref, bf16[1536,256]{1,0:T(8,128)(2,1)S(1)} %maximum_maximum_fusion.kv_ref), custom_call_target="tpu_custom_call" | custom-call | flops 2684354560 | bytes 2883584 | tf_op jit(solution)/shard_map/attend/pallas_call | solution.py:66
  173.6 21.5 %collective-permute-done.5 = bf16[512,1024]{1,0:T(8,128)(2,1)S(1)} collective-permute-done((bf16[512,1024]{1,0:T(8,128)(2,1)S(1)}, bf16[512,1024]{1,0:T(8,128)(2,1)S(1)}, u32[]{:S(2)}, u32[]{:S(2)}) %collective-permute-start.5) | collective-permute-done | bytes 1048608 | tf_op jit(solution)/shard_map/ppermute | solution.py:162
  196.7 19.6 %collective-permute-done.11 = bf16[2,512,512]{2,1,0:T(8,128)(2,1)S(1)} collective-permute-done((bf16[2,512,512]{2,1,0:T(8,128)(2,1)S(1)}, bf16[2,512,512]{2,1,0:T(8,128)(2,1)S(1)}, u32[]{:S(2)}, u32[]{:S(2)}) %collective-permute-start.11) | collective-permute-done | bytes 1048608 | tf_op jit(solution)/shard_map/ppermute | solution.py:162
  219.0 6.8 %copy.86 = bf16[2048,1152]{1,0:T(8,128)(2,1)} copy(bf16[2048,1152]{0,1:T(8,128)(2,1)} %all-gather.11.cloned.1.call-done) | data formatting | bytes 9437184 | tf_op jit(solution)/shard_map/all_gather | solution.py:226
  225.8 6.3 %fusion.47 = f32[2048,768]{0,1:T(8,128)S(1)} fusion(bf16[2,1024,1152]{2,1,0:T(8,128)(2,1)} %bitcast.202, bf16[1024,1024]{1,0:T(8,128)(2,1)} %collective-permute-done.6, bf16[512,1024]{1,0:T(8,128)(2,1)} %copy-done.50, bf16[512,1024]{1,0:T(8,128)(2,1)} %copy-done.29), kind=kOutput, calls=%fused_computation.101 | convolution fusion | flops 3233808384 | bytes 12058624 | tf_op jit(solution)/shard_map/dot_general | solution.py:24
  232.1 6.9 %fusion.8 = (bf16[2048,384]{0,1:T(8,128)(2,1)S(1)}, bf16[2048,384]{0,1:T(8,128)(2,1)S(1)}, bf16[2048,384]{0,1:T(8,128)(2,1)S(1)}) fusion(f32[2048,768]{0,1:T(8,128)S(1)} %fusion.47, bf16[2,1024,1152]{2,1,0:T(8,128)(2,1)S(1)} %bitcast.203, bf16[1024,1024]{1,0:T(8,128)(2,1)} %collective-permute-done.12, bf16[512,1024]{1,0:T(8,128)(2,1)S(1)} %copy-done.25, ...), kind=kOutput, calls=%fused_computation.21 | convolution fusion | flops 1642856448 | bytes 15990784 | tf_op jit(solution)/shard_map/dot_general | solution.py:24
  241.7 7.7 %fusion.48 = f32[2048,768]{0,1:T(8,128)} fusion(bf16[2,1024,1152]{2,1,0:T(8,128)(2,1)S(1)} %bitcast.205, bf16[1024,1024]{1,0:T(8,128)(2,1)} %collective-permute-done.6, bf16[512,1024]{1,0:T(8,128)(2,1)S(1)} %copy-done.51, bf16[512,1024]{1,0:T(8,128)(2,1)S(1)} %copy-done.30), kind=kOutput, calls=%fused_computation.102 | convolution fusion | flops 3233808384 | bytes 12058624 | tf_op jit(solution)/shard_map/dot_general | solution.py:24
  249.4 9.5 %fusion.13 = (bf16[2048,384]{0,1:T(8,128)(2,1)}, bf16[2048,384]{0,1:T(8,128)(2,1)}, bf16[2048,384]{0,1:T(8,128)(2,1)S(1)}) fusion(f32[2048,768]{0,1:T(8,128)} %fusion.48, bf16[2,1024,1152]{2,1,0:T(8,128)(2,1)S(1)} %bitcast.206, bf16[1024,1024]{1,0:T(8,128)(2,1)} %collective-permute-done.12, bf16[512,1024]{1,0:T(8,128)(2,1)S(1)} %copy-done.25, ...), kind=kOutput, calls=%fused_computation.26 | convolution fusion | flops 1642856448 | bytes 15990784 | tf_op jit(solution)/shard_map/dot_general | solution.py:24
  263.6 6.0 %fusion.37 = f32[2048,1024]{1,0:T(8,128)} fusion(bf16[2048,384]{0,1:T(8,128)(2,1)S(1)} %get-tuple-element.64, bf16[2048,384]{0,1:T(8,128)(2,1)S(1)} %get-tuple-element.63, bf16[2,1024,1152]{2,1,0:T(8,128)(2,1)S(1)} %bitcast.208), kind=kOutput, calls=%fused_computation.88 | convolution fusion | flops 3227516928 | bytes 13107200 | tf_op jit(solution)/shard_map/dot_general | solution.py:28
  269.6 6.0 %add_convert_fusion = bf16[2048,1024]{1,0:T(8,128)(2,1)S(1)} fusion(f32[2048,1024]{1,0:T(8,128)} %fusion.37, bf16[2048,384]{0,1:T(8,128)(2,1)S(1)} %copy-done.58, bf16[2048,384]{0,1:T(8,128)(2,1)S(1)} %copy-done.57, bf16[2,1024,1152]{2,1,0:T(8,128)(2,1)S(1)} %bitcast.209), kind=kOutput, calls=%fused_computation | convolution fusion | flops 3231711232 | bytes 17301504 | tf_op jit(solution)/shard_map/dot_general | solution.py:28
  278.2 5.2 fusion.41
  283.5 5.0 fusion.40
  288.5 3.4 convolution_convert_fusion.2
  291.9 3.4 convolution_convert_fusion.3
  298.6 6.7 %copy.97 = bf16[2,1024,1152]{2,1,0:T(8,128)(2,1)} copy(bf16[2,1024,1152]{1,2,0:T(8,128)(2,1)} %pad_maximum_fusion) | data formatting | bytes 9437184 | tf_op jit(solution)/shard_map/stack | solution.py:333
  317.8 3.3 convert_add_fusion.1
  322.3 15.4 %collective-permute-done.14 = bf16[512,1024]{1,0:T(8,128)(2,1)} collective-permute-done((bf16[512,1024]{1,0:T(8,128)(2,1)}, bf16[512,1024]{1,0:T(8,128)(2,1)}, u32[]{:S(2)}, u32[]{:S(2)}) %collective-permute-start.14) | collective-permute-done | bytes 1048608 | tf_op jit(solution)/shard_map/ppermute | solution.py:162
  345.1 17.6 %attend_back.1 = (f32[512,1024]{1,0:T(8,128)S(1)}, f32[1536,256]{1,0:T(8,128)S(1)}) custom-call(s32[2]{0:T(128)S(1)} %pad_add_fusion.where_ref, bf16[512,1024]{1,0:T(8,128)(2,1)S(1)} %copy.102.q_ref, bf16[1536,256]{1,0:T(8,128)(2,1)S(1)} %maximum_maximum_fusion.kv_ref, bf16[512,1024]{1,0:T(8,128)(2,1)S(1)} %copy-done.3, f32[512,8]{1,0:T(8,128)S(1)} %copy-done.6, ...), custom_call_target="tpu_custom_call" | custom-call | flops 6710886400 | bytes 7602176 | tf_op jit(solution)/shard_map/attend_back/pallas_call | solution.py:132
  372.9 4.5 reshape.410
  393.3 5.5 constant_dynamic-slice_fusion.4
  404.2 4.5 reshape.414
  408.6 3.4 copy.96
  417.9 4.8 collective-permute-done.19
  433.4 8.6 %collective-permute-done.9 = bf16[2,512,256]{2,1,0:T(8,128)(2,1)S(1)} collective-permute-done((bf16[2,512,256]{2,1,0:T(8,128)(2,1)S(1)}, bf16[2,512,256]{2,1,0:T(8,128)(2,1)S(1)}, u32[]{:S(2)}, u32[]{:S(2)}) %collective-permute-start.9) | collective-permute-done | bytes 524320 | tf_op jit(solution)/shard_map/ppermute | solution.py:162
  442.2 7.6 %collective-permute-done.21 = bf16[656,256]{1,0:T(8,128)(2,1)S(1)} collective-permute-done((bf16[656,256]{1,0:T(8,128)(2,1)S(1)}, bf16[656,256]{1,0:T(8,128)(2,1)S(1)}, u32[]{:S(2)}, u32[]{:S(2)}) %collective-permute-start.21) | collective-permute-done | bytes 335904 | tf_op jit(solution)/shard_map/ppermute | solution.py:162
  449.8 5.6 %collective-permute-done.23 = bf16[656,256]{1,0:T(8,128)(2,1)S(1)} collective-permute-done((bf16[656,256]{1,0:T(8,128)(2,1)S(1)}, bf16[656,256]{1,0:T(8,128)(2,1)S(1)}, u32[]{:S(2)}, u32[]{:S(2)}) %collective-permute-start.23) | collective-permute-done | bytes 335904 | tf_op jit(solution)/shard_map/ppermute | solution.py:166
  475.8 72.8 %reduce-scatter.3.cloned.1.call-done = bf16[1,256,128]{2,1,0:T(8,128)(2,1)} async-done(((bf16[32,256,128]{2,1,0:T(8,128)(2,1)}), bf16[1,256,128]{2,1,0:T(8,128)(2,1)}) %reduce-scatter.3.cloned.1.call-update) | async-done | bytes 65552 | tf_op jit(solution)/shard_map/reduce_scatter | solution.py:357
  (319 shorter events, 160.7 us)
Async XLA Ops:
  7.2 65.1 %all-gather.9.cloned.1.call-start = ((), (), s32[]{:S(2)}) async-start(), calls=%async_computation.5 | async-start | bytes 2162688 | tf_op jit(solution)/shard_map/all_gather | solution.py:219
  8.8 123.9 %all-gather.7.cloned.1.call-start = ((), (), s32[]{:S(2)}) async-start(), calls=%async_computation.4 | async-start | bytes 2703360 | tf_op jit(solution)/shard_map/all_gather | solution.py:212
  11.2 207.8 %all-gather.11.cloned.1.call-start = ((), (), s32[]{:S(2)}) async-start(), calls=%async_computation.6 | async-start | bytes 5308416 | tf_op jit(solution)/shard_map/all_gather | solution.py:226
  15.0 15.9 %collective-permute-start = (bf16[528,256]{1,0:T(8,128)(2,1)}, bf16[528,256]{1,0:T(8,128)(2,1)}, u32[]{:S(2)}, u32[]{:S(2)}) collective-permute-start(bf16[528,256]{1,0:T(8,128)(2,1)} %get-tuple-element.133), channel_id=1, source_target_pairs={{0,3},{1,2},{2,1},{3,0},{4,7},{5,6},{6,5},{7,4},{8,11},{9,10},{10,... | collective-permute-start | bytes 811016 | tf_op jit(solution)/shard_map/ppermute | solution.py:166
  18.9 13.0 %collective-permute-start.1 = (bf16[528,256]{1,0:T(8,128)(2,1)S(1)}, bf16[528,256]{1,0:T(8,128)(2,1)}, u32[]{:S(2)}, u32[]{:S(2)}) collective-permute-start(bf16[528,256]{1,0:T(8,128)(2,1)S(1)} %get-tuple-element.134), channel_id=1, source_target_pairs={{0,2},{2,0},{1,3},{3,1},{4,6},{6,4},{5,7},{7,5},{8,10},{10,8},{9,1... | collective-permute-start | bytes 811016 | tf_op jit(solution)/shard_map/ppermute | solution.py:162
  19.4 14.0 %collective-permute-start.2 = (bf16[528,256]{1,0:T(8,128)(2,1)S(1)}, bf16[528,256]{1,0:T(8,128)(2,1)}, u32[]{:S(2)}, u32[]{:S(2)}) collective-permute-start(bf16[528,256]{1,0:T(8,128)(2,1)S(1)} %get-tuple-element.135), channel_id=1, source_target_pairs={{0,1},{1,0},{2,3},{3,2},{4,5},{5,4},{6,7},{7,6},{8,9},{9,8},{10,11... | collective-permute-start | bytes 811016 | tf_op jit(solution)/shard_map/ppermute | solution.py:162
  21.8 148.7 %collective-permute-start.10 = (bf16[2,512,256]{2,1,0:T(8,128)(2,1)}, bf16[2,512,256]{2,1,0:T(8,128)(2,1)}, u32[]{:S(2)}, u32[]{:S(2)}) collective-permute-start(bf16[2,512,256]{2,1,0:T(8,128)(2,1)} %constant_dynamic-slice_fusion.5), channel_id=1, source_target_pairs={{0,1},{1,0},{2,3},{3,2},{4,5},{5,4},{6,7},{7,6},{8,9},{9,8},{10,11... | collective-permute-start | bytes 1572872 | tf_op jit(solution)/shard_map/ppermute | solution.py:162
  26.1 447.8 %reduce-scatter.5.cloned.1.call-start = ((), (), s32[]{:S(2)}) async-start(), calls=%async_computation.3 | async-start | bytes 5308416 | tf_op jit(solution)/shard_map/reduce_scatter | solution.py:334
  138.4 11.4 %collective-permute-start.3 = (bf16[512,256]{1,0:T(8,128)(2,1)}, bf16[512,256]{1,0:T(8,128)(2,1)}, u32[]{:S(2)}, u32[]{:S(2)}) collective-permute-start(bf16[512,256]{1,0:T(8,128)(2,1)} %pad_maximum_fusion.35), channel_id=1, source_target_pairs={{0,1},{1,0},{2,3},{3,2},{4,5},{5,4},{6,7},{7,6},{8,9},{9,8},{10,11... | collective-permute-start | bytes 786440 | tf_op jit(solution)/shard_map/ppermute | solution.py:162
  168.9 26.1 %collective-permute-start.5 = (bf16[512,1024]{1,0:T(8,128)(2,1)S(1)}, bf16[512,1024]{1,0:T(8,128)(2,1)S(1)}, u32[]{:S(2)}, u32[]{:S(2)}) collective-permute-start(bf16[512,1024]{1,0:T(8,128)(2,1)S(1)} %multiply_convert_fusion.4), channel_id=1, source_target_pairs={{0,2},{2,0},{1,3},{3,1},{4,6},{6,4},{5,7},{7,5},{8,10},{10,8},{9,1... | collective-permute-start | bytes 3145736 | tf_op jit(solution)/shard_map/ppermute | solution.py:162
  172.0 44.4 %collective-permute-start.11 = (bf16[2,512,512]{2,1,0:T(8,128)(2,1)S(1)}, bf16[2,512,512]{2,1,0:T(8,128)(2,1)S(1)}, u32[]{:S(2)}, u32[]{:S(2)}) collective-permute-start(bf16[2,512,512]{2,1,0:T(8,128)(2,1)S(1)} %pad_maximum_fusion.18), channel_id=1, source_target_pairs={{0,2},{2,0},{1,3},{3,1},{4,6},{6,4},{5,7},{7,5},{8,10},{10,8},{9,1... | collective-permute-start | bytes 3145736 | tf_op jit(solution)/shard_map/ppermute | solution.py:162
  196.7 29.0 %collective-permute-start.6 = (bf16[1024,1024]{1,0:T(8,128)(2,1)}, bf16[1024,1024]{1,0:T(8,128)(2,1)}, u32[]{:S(2)}, u32[]{:S(2)}) collective-permute-start(bf16[1024,1024]{1,0:T(8,128)(2,1)} %pad_maximum_fusion.6), channel_id=1, source_target_pairs={{0,4},{4,0},{1,5},{5,1},{2,6},{6,2},{3,7},{7,3},{8,12},{12,8},{9,1... | collective-permute-start | bytes 6291464 | tf_op jit(solution)/shard_map/ppermute | solution.py:162
  219.0 13.1 %collective-permute-start.12 = (bf16[1024,1024]{1,0:T(8,128)(2,1)}, bf16[1024,1024]{1,0:T(8,128)(2,1)}, u32[]{:S(2)}, u32[]{:S(2)}) collective-permute-start(bf16[1024,1024]{1,0:T(8,128)(2,1)} %pad_maximum_fusion.7), channel_id=1, source_target_pairs={{0,4},{4,0},{1,5},{5,1},{2,6},{6,2},{3,7},{7,3},{8,12},{12,8},{9,1... | collective-permute-start | bytes 6291464 | tf_op jit(solution)/shard_map/ppermute | solution.py:162
  263.0 54.8 %collective-permute-start.7 = (bf16[1024,1024]{1,0:T(8,128)(2,1)}, bf16[1024,1024]{1,0:T(8,128)(2,1)}, u32[]{:S(2)}, u32[]{:S(2)}) collective-permute-start(bf16[1024,1024]{1,0:T(8,128)(2,1)} %slice.273), channel_id=1, source_target_pairs={{0,4},{4,0},{1,5},{5,1},{2,6},{6,2},{3,7},{7,3},{8,12},{12,8},{9,1... | collective-permute-start | bytes 6291464 | tf_op jit(solution)/shard_map/ppermute | solution.py:162
  278.2 27.2 %collective-permute-start.13 = (bf16[1024,1024]{1,0:T(8,128)(2,1)}, bf16[1024,1024]{1,0:T(8,128)(2,1)}, u32[]{:S(2)}, u32[]{:S(2)}) collective-permute-start(bf16[1024,1024]{1,0:T(8,128)(2,1)} %slice.281), channel_id=1, source_target_pairs={{0,4},{4,0},{1,5},{5,1},{2,6},{6,2},{3,7},{7,3},{8,12},{12,8},{9,1... | collective-permute-start | bytes 6291464 | tf_op jit(solution)/shard_map/ppermute | solution.py:162
  305.4 243.3 %reduce-scatter.3.cloned.1.call-start = ((), (), s32[]{:S(2)}) async-start(), calls=%async_computation.2 | async-start | bytes 2162688 | tf_op jit(solution)/shard_map/reduce_scatter | solution.py:357
  311.8 26.0 %collective-permute-start.14 = (bf16[512,1024]{1,0:T(8,128)(2,1)}, bf16[512,1024]{1,0:T(8,128)(2,1)}, u32[]{:S(2)}, u32[]{:S(2)}) collective-permute-start(bf16[512,1024]{1,0:T(8,128)(2,1)} %slice.425), channel_id=1, source_target_pairs={{0,2},{2,0},{1,3},{3,1},{4,6},{6,4},{5,7},{7,5},{8,10},{10,8},{9,1... | collective-permute-start | bytes 3145736 | tf_op jit(solution)/shard_map/ppermute | solution.py:162
  362.7 18.2 %collective-permute-start.15 = (bf16[512,256]{1,0:T(8,128)(2,1)S(1)}, bf16[512,256]{1,0:T(8,128)(2,1)S(1)}, u32[]{:S(2)}, u32[]{:S(2)}) collective-permute-start(bf16[512,256]{1,0:T(8,128)(2,1)S(1)} %slice.426), channel_id=1, source_target_pairs={{0,1},{1,0},{2,3},{3,2},{4,5},{5,4},{6,7},{7,6},{8,9},{9,8},{10,11... | collective-permute-start | bytes 786440 | tf_op jit(solution)/shard_map/ppermute | solution.py:162
  380.6 43.2 %collective-permute-start.8 = (bf16[2,512,512]{2,1,0:T(8,128)(2,1)}, bf16[2,512,512]{2,1,0:T(8,128)(2,1)}, u32[]{:S(2)}, u32[]{:S(2)}) collective-permute-start(bf16[2,512,512]{2,1,0:T(8,128)(2,1)} %fusion.57), channel_id=1, source_target_pairs={{0,2},{2,0},{1,3},{3,1},{4,6},{6,4},{5,7},{7,5},{8,10},{10,8},{9,1... | collective-permute-start | bytes 3145736 | tf_op jit(solution)/shard_map/ppermute | solution.py:162
  387.7 38.9 %collective-permute-start.20 = (bf16[4,656,256]{2,1,0:T(8,128)(2,1)}, bf16[4,656,256]{2,1,0:T(8,128)(2,1)}, u32[]{:S(2)}, u32[]{:S(2)}) collective-permute-start(bf16[4,656,256]{2,1,0:T(8,128)(2,1)} %fusion.50), channel_id=1, source_target_pairs={{0,4},{4,0},{1,5},{5,1},{2,6},{6,2},{3,7},{7,3},{8,12},{12,8},{9,1... | collective-permute-start | bytes 4030472 | tf_op jit(solution)/shard_map/ppermute | solution.py:162
  398.9 16.6 %collective-permute-start.17 = (bf16[512,256]{1,0:T(8,128)(2,1)S(1)}, bf16[512,256]{1,0:T(8,128)(2,1)}, u32[]{:S(2)}, u32[]{:S(2)}) collective-permute-start(bf16[512,256]{1,0:T(8,128)(2,1)S(1)} %bitcast.231), channel_id=1, source_target_pairs={{0,3},{1,2},{2,1},{3,0},{4,7},{5,6},{6,5},{7,4},{8,11},{9,10},{10,... | collective-permute-start | bytes 786440 | tf_op jit(solution)/shard_map/ppermute | solution.py:166
  400.4 16.5 %collective-permute-start.18 = (bf16[512,256]{1,0:T(8,128)(2,1)}, bf16[512,256]{1,0:T(8,128)(2,1)}, u32[]{:S(2)}, u32[]{:S(2)}) collective-permute-start(bf16[512,256]{1,0:T(8,128)(2,1)} %bitcast.195), channel_id=1, source_target_pairs={{0,2},{2,0},{1,3},{3,1},{4,6},{6,4},{5,7},{7,5},{8,10},{10,8},{9,1... | collective-permute-start | bytes 786440 | tf_op jit(solution)/shard_map/ppermute | solution.py:162
  413.9 8.8 %collective-permute-start.19 = (bf16[512,256]{1,0:T(8,128)(2,1)}, bf16[512,256]{1,0:T(8,128)(2,1)}, u32[]{:S(2)}, u32[]{:S(2)}) collective-permute-start(bf16[512,256]{1,0:T(8,128)(2,1)} %bitcast.194), channel_id=1, source_target_pairs={{0,1},{1,0},{2,3},{3,2},{4,5},{5,4},{6,7},{7,6},{8,9},{9,8},{10,11... | collective-permute-start | bytes 786440 | tf_op jit(solution)/shard_map/ppermute | solution.py:162
  425.7 16.3 %collective-permute-start.9 = (bf16[2,512,256]{2,1,0:T(8,128)(2,1)S(1)}, bf16[2,512,256]{2,1,0:T(8,128)(2,1)S(1)}, u32[]{:S(2)}, u32[]{:S(2)}) collective-permute-start(bf16[2,512,256]{2,1,0:T(8,128)(2,1)S(1)} %fusion.72), channel_id=1, source_target_pairs={{0,1},{1,0},{2,3},{3,2},{4,5},{5,4},{6,7},{7,6},{8,9},{9,8},{10,11... | collective-permute-start | bytes 1572872 | tf_op jit(solution)/shard_map/ppermute | solution.py:162
  428.4 21.4 %collective-permute-start.21 = (bf16[656,256]{1,0:T(8,128)(2,1)S(1)}, bf16[656,256]{1,0:T(8,128)(2,1)S(1)}, u32[]{:S(2)}, u32[]{:S(2)}) collective-permute-start(bf16[656,256]{1,0:T(8,128)(2,1)S(1)} %get-tuple-element.81), channel_id=1, source_target_pairs={{0,1},{1,0},{2,3},{3,2},{4,5},{5,4},{6,7},{7,6},{8,9},{9,8},{10,11... | collective-permute-start | bytes 1007624 | tf_op jit(solution)/shard_map/ppermute | solution.py:162
  429.5 20.3 %collective-permute-start.22 = (bf16[656,256]{1,0:T(8,128)(2,1)S(1)}, bf16[656,256]{1,0:T(8,128)(2,1)S(1)}, u32[]{:S(2)}, u32[]{:S(2)}) collective-permute-start(bf16[656,256]{1,0:T(8,128)(2,1)S(1)} %get-tuple-element.83), channel_id=1, source_target_pairs={{0,2},{2,0},{1,3},{3,1},{4,6},{6,4},{5,7},{7,5},{8,10},{10,8},{9,1... | collective-permute-start | bytes 1007624 | tf_op jit(solution)/shard_map/ppermute | solution.py:162
  430.5 25.0 %collective-permute-start.23 = (bf16[656,256]{1,0:T(8,128)(2,1)S(1)}, bf16[656,256]{1,0:T(8,128)(2,1)S(1)}, u32[]{:S(2)}, u32[]{:S(2)}) collective-permute-start(bf16[656,256]{1,0:T(8,128)(2,1)S(1)} %get-tuple-element.82), channel_id=1, source_target_pairs={{0,3},{1,2},{2,1},{3,0},{4,7},{5,6},{6,5},{7,4},{8,11},{9,10},{10,... | collective-permute-start | bytes 1007624 | tf_op jit(solution)/shard_map/ppermute | solution.py:166
  455.7 7.6 %collective-permute-start.24 = (bf16[176,256]{1,0:T(8,128)(2,1)S(1)}, bf16[176,256]{1,0:T(8,128)(2,1)S(1)}, u32[]{:S(2)}, u32[]{:S(2)}) collective-permute-start(bf16[176,256]{1,0:T(8,128)(2,1)S(1)} %get-tuple-element.120), channel_id=1, source_target_pairs={{0,8},{8,16},{16,24},{24,0},{1,9},{9,17},{17,25},{25,1},{2,10},{10... | collective-permute-start | bytes 270344 | tf_op jit(solution)/shard_map/ppermute | solution.py:189
  455.8 9.3 %collective-permute-start.25 = (bf16[176,256]{1,0:T(8,128)(2,1)S(1)}, bf16[176,256]{1,0:T(8,128)(2,1)S(1)}, u32[]{:S(2)}, u32[]{:S(2)}) collective-permute-start(bf16[176,256]{1,0:T(8,128)(2,1)S(1)} %get-tuple-element.121), channel_id=1, source_target_pairs={{0,16},{8,24},{16,0},{24,8},{1,17},{9,25},{17,1},{25,9},{2,18},{10... | collective-permute-start | bytes 270344 | tf_op jit(solution)/shard_map/ppermute | solution.py:189
  457.8 7.3 %collective-permute-start.26 = (bf16[176,256]{1,0:T(8,128)(2,1)S(1)}, bf16[176,256]{1,0:T(8,128)(2,1)S(1)}, u32[]{:S(2)}, u32[]{:S(2)}) collective-permute-start(bf16[176,256]{1,0:T(8,128)(2,1)S(1)} %get-tuple-element.122), channel_id=1, source_target_pairs={{0,24},{8,0},{16,8},{24,16},{1,25},{9,1},{17,9},{25,17},{2,26},{10... | collective-permute-start | bytes 270344 | tf_op jit(solution)/shard_map/ppermute | solution.py:189
  465.2 4.6 collective-permute-start.27
  475.1 75.1 %collective-permute-start.29 = (bf16[128,1152]{1,0:T(8,128)(2,1)S(1)}, bf16[128,1152]{1,0:T(8,128)(2,1)S(1)}, u32[]{:S(2)}, u32[]{:S(2)}) collective-permute-start(bf16[128,1152]{1,0:T(8,128)(2,1)S(1)} %get-tuple-element.110), channel_id=1, source_target_pairs={{0,4},{4,0},{1,5},{5,1},{2,6},{6,2},{3,7},{7,3},{8,12},{12,8},{9,1... | collective-permute-start | bytes 884744 | tf_op jit(solution)/shard_map/ppermute | solution.py:162
  (62 other events, 645.3 us)
Sparse Core Ops, SparseCore 0:
  11.5 60.6 all-gather.8
  75.7 56.9 all-gather.6
  135.3 82.0 all-gather.10
  305.5 99.0 reduce-scatter.4
  412.2 136.4 reduce-scatter.2

commit v2 on v1

v2 whole, which is shorter than its diff:
```python
import functools
import math

import jax
import jax.numpy as jnp
from jax import lax
from jax.experimental import pallas as pl
from jax.experimental.pallas import tpu as pltpu
from jax.sharding import Mesh
from jax.sharding import PartitionSpec as P

D = 1024
HEAD = 128
WINDOW = 1024
ROWS = 256
SPAN = WINDOW + ROWS
WIDE = 256
EPSILON = 1e-06
NEG = -1e30
LOG2E = math.log2(math.e)
SCALE = HEAD**-0.5
BF = jnp.bfloat16
F32 = jnp.float32
LIMIT = 24 << 20
COST = 1 / 16


def mm(a, b):
    return jnp.dot(a, b, preferred_element_type=F32)


def mm_nt(a, b):
    return lax.dot_general(a, b, (((1,), (1,)), ((), ())), preferred_element_type=F32)


def mm_tn(a, b):
    return lax.dot_general(a, b, (((0,), (0,)), ((), ())), preferred_element_type=F32)


def out(shape, kind):
    return jax.ShapeDtypeStruct(shape, kind)


def cost(flops, nbytes, exps=0):
    flops, nbytes, exps = (int(v * COST) for v in (flops, nbytes, exps))
    return pl.CostEstimate(flops=flops, bytes_accessed=nbytes, transcendentals=exps)


ROW_START, CORE, HALF, ME, SLOT, LENGTHS = 0, 1, 2, 3, 4, 5


def place(info, k):
    return pl.ds(pl.multiple_of((info[ME] ^ k) * WIDE, WIDE), WIDE)


def by_rows(width, rows=ROWS):
    return pl.BlockSpec((rows, width), lambda i, s: (i, 0))


def whole(shape):
    return pl.BlockSpec(shape, lambda i, s: (0,) * len(shape))


def kernel(body, name, grid, args, in_specs, out_specs, outs, work, scratch=(), limit=LIMIT):
    call = pl.pallas_call(
        body,
        grid_spec=pltpu.PrefetchScalarGridSpec(
            num_scalar_prefetch=1,
            grid=(grid,),
            in_specs=[s or whole(a.shape) for s, a in zip(in_specs, args[1:])],
            out_specs=[s or whole(o.shape) for s, o in zip(out_specs, outs)],
            scratch_shapes=scratch,
        ),
        out_shape=outs,
        compiler_params=pltpu.CompilerParams(vmem_limit_bytes=limit),
        cost_estimate=work,
        name=name,
    )
    return call(*args)


def turn(value, cosine, sine):
    return value * cosine + pltpu.roll(value, HEAD // 2, 1) * sine


def prepare_kernel(info, *refs):
    tok_ref, cot_ref, ga_ref, gm_ref, wq_ref, wkv_ref, wo_ref, wgu_ref, wd_ref = refs[:9]
    pieces, cots, qkv_ref, mlp_ref = refs[9:13], refs[13:15], *refs[15:]
    gains = jnp.concatenate(
        [r[...].astype(F32).reshape(1, WIDE) for r in (ga_ref, gm_ref)]
        + [jnp.zeros((14, WIDE), F32)],
        axis=0,
    ).astype(BF)
    rows = tok_ref.shape[1] // 2
    c, x, y = info[CORE], info[HALF], info[SLOT]
    units = wd_ref.shape[0] // 2
    column = pl.ds(pl.multiple_of(c * HEAD, HEAD), HEAD)
    qkv_ref[0] = wq_ref[:, column]
    qkv_ref[1] = wkv_ref[:, column]
    qkv_ref[2] = wo_ref[pl.ds(pl.multiple_of(c * HEAD, HEAD), HEAD), :].T
    for k in range(4):
        half = pl.ds(pl.multiple_of((x ^ (k & 1)) * rows, rows), rows)
        pieces[k][:rows, :] = tok_ref[y ^ (k >> 1), half, :]
        pieces[k][rows:, :] = gains
    for k in range(2):
        half = pl.ds(pl.multiple_of((x ^ k) * rows, rows), rows)
        for slot in range(2):
            time = lax.broadcasted_iota(jnp.int32, (rows, WIDE), 0)
            time = time + info[ROW_START] + ((x ^ k) - x) * rows
            value = cot_ref[y ^ slot, half, :]
            cots[k][slot] = jnp.where(
                time < info[LENGTHS + (y ^ slot)], value.astype(F32), 0.0
            ).astype(BF)
    unit = pl.ds(pl.multiple_of(c * units, HEAD), units)
    mlp_ref[:, :units] = wgu_ref[0, :, unit]
    mlp_ref[:, units : 2 * units] = wgu_ref[1, :, unit]
    mlp_ref[:, 2 * units :] = wd_ref[unit, :].T


def prepare(info, tokens, cotangent, gain_attn, gain_mlp, w_query, w_keyval, w_out, w_gateup, w_down):
    rows = tokens.shape[1] // 2
    depth = w_query.shape[0]
    outs = [out((rows + 16, WIDE), BF)] * 4 + [out((2, rows, WIDE), BF)] * 2
    outs += [
        out((3, depth, HEAD), BF),
        out((depth, 3 * w_down.shape[0] // 2), BF),
    ]
    args = (info, tokens, cotangent, gain_attn, gain_mlp, w_query, w_keyval, w_out, w_gateup, w_down)
    return kernel(
        prepare_kernel, "prepare", 1, args, [None] * 9, [None] * 8, outs, cost(0, 6 << 20), (), 60 << 20
    )


def assemble_kernel(info, *refs):
    for k in range(4):
        for slot in range(2):
            refs[4 + slot][:, place(info, k)] = refs[k][slot ^ (k >> 1)]


def assemble(info, parts):
    rows = parts[0].shape[1]
    return kernel(
        assemble_kernel,
        "assemble",
        1,
        (info, *parts),
        [None] * 4,
        [None] * 2,
        [out((rows, D), BF)] * 2,
        cost(0, 8 << 20),
    )


def project_kernel(info, *refs):
    pieces, (wq_own, wq_core, kv_near, kv_core) = refs[:4], refs[4:8]
    cos_ref, sin_ref, x_ref, gain_ref, normed_ref, q_ref, kv_ref, wkv_ref = refs[8:]
    rows = x_ref.shape[0]
    for k in range(4):
        x_ref[:, place(info, k)] = pieces[k][:rows, :]
        gain_ref[:, place(info, k)] = pieces[k][rows:, :]
    resid = x_ref[...].astype(F32)
    inv = lax.rsqrt(jnp.mean(resid * resid, axis=1, keepdims=True) + EPSILON)
    normed = (resid * inv * gain_ref[0:1, :].astype(F32)).astype(BF)
    normed_ref[...] = normed
    cosine, sine = cos_ref[...], sin_ref[...]
    own_first = info[CORE] == 0
    wkv_ref[:, :HEAD] = jnp.where(own_first, kv_near[1], kv_core[...])
    wkv_ref[:, HEAD:] = jnp.where(own_first, kv_core[...], kv_near[1])
    lin = mm(normed, wkv_ref[...])
    kv_ref[:, :HEAD] = turn(lin[:, :HEAD], cosine, sine).astype(BF)
    kv_ref[:, HEAD:] = lin[:, HEAD:].astype(BF)
    for j in range(4):
        lin = mm(normed, two_heads(wq_own if j < 2 else wq_core, j % 2))
        for i in range(2):
            head = turn(lin[:, i * HEAD : (i + 1) * HEAD], cosine, sine)
            q_ref[:, (2 * j + i) * HEAD : (2 * j + i + 1) * HEAD] = head.astype(BF)


def two_heads(ref, j):
    return jnp.concatenate([ref[2 * j], ref[2 * j + 1]], axis=1)


def project(info, pieces, w_q, w_kv, cosine, sine):
    rows = pieces[0].shape[0] - 16
    return kernel(
        project_kernel,
        "project",
        1,
        (info, *pieces, *w_q, *w_kv, cosine, sine),
        [None] * 10,
        [None] * 6,
        [
            out((rows, D), BF),
            out((16, D), BF),
            out((rows, D), BF),
            out((rows, 8 * HEAD), BF),
            out((rows, 2 * HEAD), BF),
            out((D, 2 * HEAD), BF),
        ],
        cost(2 * rows * D * 10 * HEAD, 8 << 20),
    )


def fill_bias(bias_ref, info, step):
    row = lax.broadcasted_iota(jnp.int32, (ROWS, SPAN), 0)
    col = lax.broadcasted_iota(jnp.int32, (ROWS, SPAN), 1)
    pos = info[ROW_START] - WINDOW + step * ROWS + col
    ahead = col - row - WINDOW
    inside = (ahead <= 0) & (ahead > -WINDOW) & (pos >= 0) & (pos < info[LENGTHS + info[SLOT]])
    bias_ref[...] = jnp.where(inside | (ahead == 0), 0.0, NEG).astype(F32)


def attend_kernel(info, *refs):
    q_ref, far_ref, near_ref, own_ref = refs[:4]
    mixed_ref, lse_ref, kv_ref, bias_ref = refs[4:]
    step = pl.program_id(0)
    rows = own_ref.shape[0]

    @pl.when(step == 0)
    def _():
        kv_ref[:rows, :] = far_ref[...]
        kv_ref[rows : 2 * rows, :] = near_ref[...]
        kv_ref[2 * rows :, :] = own_ref[...]

    fill_bias(bias_ref, info, step)
    here = pl.ds(step * ROWS, SPAN)
    keys = kv_ref[here, :HEAD]
    values = kv_ref[here, HEAD:]
    for h in range(8):
        cols = slice(h * HEAD, (h + 1) * HEAD)
        s = mm_nt(q_ref[:, cols], keys) * (SCALE * LOG2E) + bias_ref[...]
        top = jnp.max(s, axis=1, keepdims=True)
        p = jnp.exp2(s - top)
        total = jnp.sum(p, axis=1, keepdims=True)
        mixed_ref[:, cols] = (mm(p.astype(BF), values) / total).astype(BF)
        lse_ref[:, h : h + 1] = top + jnp.log2(total)


def attend(info, q, far, near, own):
    rows = q.shape[0]
    return kernel(
        attend_kernel,
        "attend",
        rows // ROWS,
        (info, q, far, near, own),
        [by_rows(8 * HEAD)] + [None] * 3,
        [by_rows(8 * HEAD), by_rows(8), None],
        [
            out((rows, 8 * HEAD), BF),
            out((rows, 8), F32),
            out((3 * rows, 2 * HEAD), BF),
        ],
        cost(4 * rows * D * SPAN, 5 << 20, rows * 8 * SPAN),
        [pltpu.VMEM((ROWS, SPAN), F32)],
    )


def project_out_kernel(info, *refs):
    mixed_ref, x_ref, gain_ref, w_o = *refs[:3], refs[3:5]
    hidden_ref, normed_ref = refs[5:]
    hidden = x_ref[...].astype(F32)
    for j in range(4):
        mixed = mixed_ref[:, 2 * j * HEAD : 2 * (j + 1) * HEAD]
        hidden = hidden + mm_nt(mixed, two_heads(w_o[j // 2], j % 2))
    hidden_ref[...] = hidden
    inv = lax.rsqrt(jnp.mean(hidden * hidden, axis=1, keepdims=True) + EPSILON)
    normed_ref[...] = (hidden * inv * gain_ref[1:2, :].astype(F32)).astype(BF)


def project_out(info, mixed, x, gains, w_o):
    rows = x.shape[0]
    return kernel(
        project_out_kernel,
        "project_out",
        rows // ROWS,
        (info, mixed, x, gains, *w_o),
        [by_rows(8 * HEAD), by_rows(D)] + [None] * 3,
        [by_rows(D), by_rows(D)],
        [out((rows, D), F32), out((rows, D), BF)],
        cost(2 * rows * D * D, 7 << 20),
    )


def norm_back_kernel(info, *refs):
    own_ref, cot_ref, hidden_ref, gain_ref, *came_refs = refs[:6]
    gh_ref, ghl_ref, gg_ref = refs[6:]

    @pl.when(pl.program_id(0) == 0)
    def _():
        gg_ref[...] = jnp.zeros_like(gg_ref)

    came = jnp.where(pl.program_id(0) == 0, came_refs[0][...], came_refs[1][...])
    grad = own_ref[...].astype(F32) + came.astype(F32)
    hidden = hidden_ref[...]
    inv = lax.rsqrt(jnp.mean(hidden * hidden, axis=1, keepdims=True) + EPSILON)
    hat = hidden * inv
    gg_ref[0:1, :] += jnp.sum(grad * hat, axis=0, keepdims=True)
    g = grad * gain_ref[1:2, :].astype(F32)
    dots = jnp.mean(g * hat, axis=1, keepdims=True)
    grad_hidden = cot_ref[...].astype(F32) + inv * (g - hat * dots)
    gh_ref[...] = grad_hidden
    ghl_ref[...] = grad_hidden.astype(BF)


def norm_back(info, own, came, cot, hidden, gains):
    rows = hidden.shape[0]
    return kernel(
        norm_back_kernel,
        "norm_back",
        rows // ROWS,
        (info, own, cot, hidden, gains, *came),
        [by_rows(D)] * 3 + [None] * 3,
        [by_rows(D), by_rows(D), None],
        [out((rows, D), F32), out((rows, D), BF), out((8, D), F32)],
        cost(20 * rows * D, 10 << 20),
    )


def attend_back_kernel(info, *refs):
    low_ref, cos_ref, sin_ref, q_ref, kv_ref, mixed_ref, lse_ref = refs[:7]
    w_o = refs[7:9]
    gq_ref, far_ref, near_ref, here_ref, gkv_ref, bias_ref = refs[9:]
    step = pl.program_id(0)
    rows = here_ref.shape[0]

    @pl.when(step == 0)
    def _():
        gkv_ref[...] = jnp.zeros_like(gkv_ref)

    low = low_ref[...]
    fill_bias(bias_ref, info, step)
    here = pl.ds(step * ROWS, SPAN)
    keys = kv_ref[here, :HEAD]
    values = kv_ref[here, HEAD:]
    for j in range(4):
        two = mm(low, two_heads(w_o[j // 2], j % 2))
        for i in range(2):
            h = 2 * j + i
            cols = slice(h * HEAD, (h + 1) * HEAD)
            q = q_ref[:, cols]
            gm = two[:, i * HEAD : (i + 1) * HEAD].astype(BF)
            s = mm_nt(q, keys) * (SCALE * LOG2E) + bias_ref[...]
            p = jnp.exp2(s - lse_ref[:, h : h + 1])
            gp = mm_nt(gm, values)
            inner = jnp.sum(
                gm.astype(F32) * mixed_ref[:, cols].astype(F32), axis=1, keepdims=True
            )
            gs = (p * (gp - inner)).astype(BF)
            gq = mm(gs, keys) * SCALE
            gq_ref[:, cols] = turn(gq, cos_ref[...], -sin_ref[...]).astype(BF)
            gkv_ref[here, :HEAD] += mm_tn(gs, q) * SCALE
            gkv_ref[here, HEAD:] += mm_tn(p.astype(BF), gm)

    @pl.when(step == pl.num_programs(0) - 1)
    def _():
        far_ref[...] = gkv_ref[:rows, :].astype(BF)
        near_ref[...] = gkv_ref[rows : 2 * rows, :].astype(BF)
        here_ref[...] = gkv_ref[2 * rows :, :]


def attend_back(info, low, cosine, sine, q, kv, mixed, lse, w_o):
    rows = q.shape[0]
    wide = by_rows(8 * HEAD)
    return kernel(
        attend_back_kernel,
        "attend_back",
        rows // ROWS,
        (info, low, cosine, sine, q, kv, mixed, lse, *w_o),
        [by_rows(D), by_rows(HEAD), by_rows(HEAD), wide, None, wide, by_rows(8), None, None],
        [wide] + [None] * 3,
        [out((rows, 8 * HEAD), BF)] + [out((rows, 2 * HEAD), k) for k in (BF, BF, F32)],
        cost(10 * rows * D * (SPAN + HEAD), 12 << 20, rows * 8 * SPAN),
        [pltpu.VMEM(kv.shape, F32), pltpu.VMEM((ROWS, SPAN), F32)],
        60 << 20,
    )


def project_back_kernel(info, *refs):
    gq_ref, here_ref, near_ref, far_ref, cos_ref, sin_ref, x_ref, gain_ref, gh_ref = refs[:9]
    wq_own, wq_core, wkv_ref = refs[9:12]
    gkv_ref, gg_ref, *piece_refs = refs[12:18]
    buffer_ref = refs[18]

    @pl.when(pl.program_id(0) == 0)
    def _():
        gg_ref[...] = jnp.zeros_like(gg_ref)

    grad = here_ref[...] + near_ref[...].astype(F32) + far_ref[...].astype(F32)
    gkv_ref[:, :HEAD] = turn(grad[:, :HEAD], cos_ref[...], -sin_ref[...]).astype(BF)
    gkv_ref[:, HEAD:] = grad[:, HEAD:].astype(BF)
    normed_grad = mm_nt(gkv_ref[...], wkv_ref[...])
    for j in range(4):
        weights = two_heads(wq_own if j < 2 else wq_core, j % 2)
        normed_grad = normed_grad + mm_nt(gq_ref[:, 2 * j * HEAD : 2 * (j + 1) * HEAD], weights)
    resid = x_ref[...].astype(F32)
    inv = lax.rsqrt(jnp.mean(resid * resid, axis=1, keepdims=True) + EPSILON)
    hat = resid * inv
    gg_ref[0:1, :] += jnp.sum(normed_grad * hat, axis=0, keepdims=True)
    g = normed_grad * gain_ref[0:1, :].astype(F32)
    dots = jnp.mean(g * hat, axis=1, keepdims=True)
    buffer_ref[...] = gh_ref[...] + inv * (g - hat * dots)
    for k in range(4):
        piece_refs[k][...] = buffer_ref[:, place(info, k)].astype(BF)


def project_back(info, gq, grad_kv, near, far, cosine, sine, x, gains, grad_hidden, w_q, w_kv):
    rows = gq.shape[0]
    steps = rows // ROWS
    pair_rows = by_rows(2 * HEAD)
    return kernel(
        project_back_kernel,
        "project_back",
        steps,
        (info, gq, grad_kv, near, far, cosine, sine, x, gains, grad_hidden, *w_q, w_kv),
        [
            by_rows(8 * HEAD),
            pair_rows,
            pair_rows,
            pair_rows,
            by_rows(HEAD),
            by_rows(HEAD),
            by_rows(D),
            None,
            by_rows(D),
            None,
            None,
            None,
        ],
        [pair_rows, None] + [by_rows(WIDE)] * 4,
        [out((rows, 2 * HEAD), BF), out((8, D), F32)] + [out((rows, WIDE), BF)] * 4,
        cost(2 * rows * D * 10 * HEAD, 10 << 20),
        [pltpu.VMEM((ROWS, D), F32)],
    )


def halves(ref, info, shards, core):
    sub = D // shards // 2
    at_core = info[CORE] ^ core
    return jnp.concatenate(
        [
            ref[:, pl.ds(pl.multiple_of(d * 2 * sub + at_core * sub, HEAD), sub)]
            for d in range(shards)
        ],
        axis=1,
    )


def head_grads_kernel(shards, info, *refs):
    sub = D // shards // 2
    for at_pair in range(2):
        left_ref, right_ref = refs[2 * at_pair : 2 * at_pair + 2]
        for core in range(2):
            mine = halves(left_ref, info, shards, core)
            for j in range(2):
                cols = []
                for k in (2 * j, 2 * j + 1):
                    for kc in (core, 1 - core):
                        cols.append(right_ref[:, (kc * 4 + k) * HEAD : (kc * 4 + k + 1) * HEAD])
                grad = mm_tn(mine, jnp.concatenate(cols, axis=1)).astype(BF)
                for i in range(2):
                    part = grad[:, i * WIDE : (i + 1) * WIDE].reshape(shards, sub, WIDE)
                    refs[4 + core][2 * j + i, :, at_pair * sub : (at_pair + 1) * sub, :] = part


def key_grads_kernel(shards, info, *refs):
    normed_ref, gkv_ref, ga_ref, gm_ref = refs[:4]
    sub = D // shards // 2
    gains = [r[0:1, k * WIDE : (k + 1) * WIDE] for r in (ga_ref, gm_ref) for k in range(4)]
    gains = jnp.concatenate(gains + [jnp.zeros((8, WIDE), F32)], axis=0).astype(BF)
    for core in range(2):
        grad = mm_tn(halves(normed_ref, info, shards, core), gkv_ref[...]).astype(BF)
        for d in range(shards):
            refs[4 + core][d, :sub, :] = grad[d * sub : (d + 1) * sub, :]
            refs[4 + core][d, sub:, :] = gains


def key_grads(info, c, shards, normed, gkv, ga, gm):
    sub = D // shards // 2
    if sub % HEAD:
        keys = mm_tn(normed, gkv).astype(BF).reshape(shards, 2, sub, WIDE)
        gains = jnp.concatenate([ga[0].reshape(4, WIDE), gm[0].reshape(4, WIDE)])
        gains = jnp.concatenate([gains, jnp.zeros((8, WIDE), F32)]).astype(BF)
        gains = jnp.broadcast_to(gains, (shards, 16, WIDE))
        return [jnp.concatenate([at(keys, c ^ core, 1), gains], axis=1) for core in range(2)]
    return kernel(
        functools.partial(key_grads_kernel, shards),
        "key_grads",
        1,
        (info, normed, gkv, ga, gm),
        [None] * 4,
        [None] * 2,
        [out((shards, sub + 16, WIDE), BF)] * 2,
        cost(2 * normed.shape[0] * D * WIDE, 2 << 20),
    )


def head_grads(info, c, shards, pairs):
    rows = pairs[0].shape[0]
    sub = D // shards // 2
    if sub % HEAD:
        parts = [[], []]
        for left, right in (pairs[:2], pairs[2:]):
            grad = mm_tn(left, right).astype(BF).reshape(shards, 2, sub, 2, 4, HEAD)
            for core in range(2):
                mine = at(grad, c ^ core, 1)
                mine = mine[:, :, ::-1] if core else mine
                mine = mine.transpose(3, 0, 1, 2, 4).reshape(4, shards, sub, WIDE)
                parts[core].append(mine)
        return [jnp.concatenate(p, axis=2) for p in parts]
    return kernel(
        functools.partial(head_grads_kernel, shards),
        "head_grads",
        1,
        (info, *pairs),
        [None] * 4,
        [None] * 2,
        [out((4, shards, 2 * sub, WIDE), BF)] * 2,
        cost(4 * rows * D * D, 10 << 20),
    )


def sum_parts_kernel(info, *refs):
    for k in range(4):
        refs[2 + k][...] = (refs[0][k].astype(F32) + refs[1][k].astype(F32)).astype(BF)


def sum_parts(info, mine, other):
    return kernel(
        sum_parts_kernel,
        "sum_parts",
        1,
        (info, mine, other),
        [None] * 2,
        [None] * 4,
        [out(mine.shape[1:], BF)] * 4,
        cost(0, 6 << 20),
    )


def mlp_kernel(units, first, cut_up, info, *refs):
    rows, cot = refs[0][...], refs[1][...]
    weights = refs[2:4]
    active_ref, ggu_ref, branch_ref, *gn_refs = refs[4 if first else 6 :]
    root = math.sqrt(2 / math.pi)
    grad_normed = 0.0 if first else refs[4][...].astype(F32)
    branch = 0.0 if first else refs[5][...].astype(F32)
    for part in range(2):
        w_gu = weights[part][:, : 2 * units]
        w_dt = weights[part][:, 2 * units :]
        lin = mm(rows, w_gu)
        gate, up = lin[:, :units], lin[:, units:]
        grad_active = mm(cot, w_dt)
        square = gate * gate
        tanh = jnp.tanh(root * gate * (1.0 + 0.044715 * square))
        side = 0.5 * (1.0 + tanh)
        gelu = gate * side
        slope = side + gelu * (1.0 - tanh) * (root + 3 * 0.044715 * root * square)
        active = (gelu * up).astype(BF)
        grad_gu = jnp.concatenate(
            [(grad_active * up * slope).astype(BF), (grad_active * gelu).astype(BF)], axis=1
        )
        active_ref[:, part * units : (part + 1) * units] = active
        ggu_ref[:, part * 2 * units : (part + 1) * 2 * units] = grad_gu
        grad_normed = grad_normed + mm_nt(grad_gu, w_gu)
        branch = branch + mm_nt(active, w_dt)
    branch_ref[...] = branch.astype(BF)
    if not cut_up:
        gn_refs[0][...] = grad_normed.astype(BF)
    else:
        for i in range(2):

            @pl.when(pl.program_id(0) == i)
            def _():
                gn_refs[i][...] = grad_normed.astype(BF)


def mlp(info, rows, cot, weights, before=(), cut_up=False):
    count = rows.shape[0]
    units = weights[0].shape[1] // 3
    widths = (2 * units, 4 * units, D)
    outs = [out((count, w), BF) for w in widths]
    outs += [out((ROWS, D), BF)] * 2 if cut_up else [out((count, D), BF)]
    return kernel(
        functools.partial(mlp_kernel, units, not before, cut_up),
        "mlp",
        count // ROWS,
        (info, rows, cot, *weights, *before),
        [by_rows(D)] * 2 + [None] * 2 + [by_rows(D)] * len(before),
        [by_rows(w) for w in widths] + ([None] * 2 if cut_up else [by_rows(D)]),
        outs,
        cost(24 * count * D * units, 14 << 20, count * 2 * units),
    )


def unit_grads_kernel(info, *refs):
    rows_refs, cot_refs, gu_refs, act_refs, out_refs = (refs[i : i + 2] for i in range(0, 10, 2))
    units = act_refs[0].shape[1] // 2
    for part in range(2):
        gu = slice(part * 2 * units, (part + 1) * 2 * units)
        act = slice(part * units, (part + 1) * units)
        up = mm_tn(rows_refs[0][...], gu_refs[0][:, gu]) + mm_tn(rows_refs[1][...], gu_refs[1][:, gu])
        down = mm_tn(cot_refs[0][...], act_refs[0][:, act]) + mm_tn(cot_refs[1][...], act_refs[1][:, act])
        out_refs[part][:, : 2 * units] = up.astype(BF)
        out_refs[part][:, 2 * units :] = down.astype(BF)


def unit_grads(info, rows, cots, grads, actives):
    count = rows[0].shape[0]
    units = actives[0].shape[1] // 2
    columns = pl.BlockSpec((count, WIDE), lambda i, s: (0, i))
    return kernel(
        unit_grads_kernel,
        "unit_grads",
        D // WIDE,
        (info, *rows, *cots, *grads, *actives),
        [columns] * 4 + [None] * 4,
        [pl.BlockSpec((WIDE, 3 * units), lambda i, s: (i, 0))] * 2,
        [out((D, 3 * units), BF)] * 2,
        cost(24 * count * D * units, 14 << 20),
    )


def split_kernel(info, *refs):
    own_ref, hidden_ref, far_ref = refs[:3]
    pieces, buffer_ref = refs[3:7], refs[7]
    for slot in range(2):
        total = own_ref[...].astype(F32) + hidden_ref[...] if slot == 0 else far_ref[...].astype(F32)
        buffer_ref[...] = total
        for k in range(4):
            pieces[k][slot ^ (k >> 1)] = buffer_ref[:, place(info, k)].astype(BF)


def split(info, own, hidden, far):
    rows = own.shape[0]
    return kernel(
        split_kernel,
        "split",
        1,
        (info, own, hidden, far),
        [None] * 3,
        [None] * 4,
        [out((2, rows, WIDE), BF)] * 4,
        cost(0, 8 << 20),
        [pltpu.VMEM((rows, D), F32)],
    )


def swap(value, axis):
    return lax.ppermute(value, axis, [(0, 1), (1, 0)])


def swap_both(value):
    return lax.ppermute(value, ("ty", "tx"), [(i, i ^ 3) for i in range(4)])


def to_next(value, back=False):
    pairs = [(0, 1), (1, 2), (2, 3), (3, 0)]
    return lax.ppermute(value, ("ctx", "tx"), [p[::-1] for p in pairs] if back else pairs)


def exchange(parts):
    return [parts[0], swap(parts[1], "tx"), swap(parts[2], "ty"), swap_both(parts[3])]


def after(value, *others):
    return lax.optimization_barrier((value, others))[0]


def pick(flag, ones, zeros):
    return jnp.where(flag == 1, ones, zeros)


def pair(flag, own, other, axis):
    return jnp.concatenate([pick(flag, other, own), pick(flag, own, other)], axis=axis)


def half_at(value, index, axis):
    size = value.shape[axis] // 2
    return lax.dynamic_slice_in_dim(value, index * size, size, axis)


def at(value, index, axis=0):
    return lax.dynamic_index_in_dim(value, index, axis, False)


def add(*values):
    return sum(v.astype(F32) for v in values)


DIRECT = 4


def to_shard(value, step):
    shards = lax.axis_size("fsdp")
    return lax.ppermute(value, "fsdp", [(i, (i + step) % shards) for i in range(shards)])


def fsdp_gather(part, axis):
    shards = lax.axis_size("fsdp")
    if shards > DIRECT:
        return lax.all_gather(part, "fsdp", axis=axis, tiled=True)
    size = part.shape[axis]
    z = lax.axis_index("fsdp")
    shape = part.shape[:axis] + (shards * size,) + part.shape[axis + 1 :]
    full = lax.dynamic_update_slice_in_dim(jnp.zeros(shape, part.dtype), part, z * size, axis)
    for step in range(1, shards):
        origin = (z - step) % shards
        full = lax.dynamic_update_slice_in_dim(full, to_shard(part, step), origin * size, axis)
    return full


def fsdp_scatter(parts):
    shards = lax.axis_size("fsdp")
    if shards > DIRECT:
        return lax.psum_scatter(parts, "fsdp", scatter_dimension=0, tiled=False).astype(F32)
    z = lax.axis_index("fsdp")
    came = [to_shard(at(parts, (z + step) % shards), step) for step in range(1, shards)]
    return add(at(parts, z), *came)


def fsdp_halve(parts):
    shards = lax.axis_size("fsdp")
    if shards > DIRECT:
        return lax.psum_scatter(parts, "fsdp", scatter_dimension=0, tiled=False)
    z = lax.axis_index("fsdp")
    count = shards // 2
    while count:
        parts = parts.reshape((2, count) + parts.shape[1:])
        side = (z // count) % 2
        came = lax.ppermute(at(parts, 1 - side), "fsdp", [(i, i ^ count) for i in range(shards)])
        parts = add(at(parts, side), came).astype(BF)
        count //= 2
    return parts[0]


def body(
    tokens, lengths, w_query, w_keyval, w_out, w_gateup, w_down, gain_attn, gain_mlp, cotangent
):
    shards = lax.axis_size("fsdp")
    z, c = lax.axis_index("fsdp"), lax.axis_index("ctx")
    y, x = lax.axis_index("ty"), lax.axis_index("tx")
    me = 2 * y + x
    seq_rows = tokens.shape[1]
    rows = seq_rows // 2
    depth = w_query.shape[0]
    sub = depth // 2
    units = w_gateup.shape[2] // 2
    row_start = c * seq_rows + x * rows
    info = jnp.stack(
        [row_start, c, x, me, y, lengths[0], lengths[1]]
    ).astype(jnp.int32)

    *sends, qkv_part, mlp_part = prepare(
        info, tokens, cotangent, gain_attn, gain_mlp, w_query, w_keyval, w_out, w_gateup, w_down
    )

    qkv = fsdp_gather(qkv_part, 1)
    pieces = exchange(sends[:4])
    own_cot, x_cot = sends[4:]
    qkv, mlp_part = after([qkv, mlp_part], pieces)
    w_near = lax.all_gather(mlp_part, "fsdp", axis=0, tiled=True)
    w_q = jnp.stack(exchange([qkv[0]] * 4))
    w_q = [w_q, swap(w_q, "ctx")]
    w_kv = [qkv, swap(qkv[1], "ctx")]
    qkv_late, own_cot, x_cot = after([qkv, own_cot, x_cot], w_q[0])
    cot_x, cot_y = swap(x_cot, "tx"), swap(own_cot, "ty")

    half_width = HEAD // 2
    freq = 10000.0 ** (-jnp.arange(half_width, dtype=F32) / half_width)
    angles = (row_start + jnp.arange(rows, dtype=jnp.int32)).astype(F32)[:, None] * freq[None, :]
    cosine, sine = jnp.cos(angles), jnp.sin(angles)
    cosine = jnp.concatenate([cosine, cosine], axis=1)
    sine = jnp.concatenate([-sine, sine], axis=1)

    x_rows, gain_rows, normed_attn, q, kv_own, w_kv = project(
        info, pieces, w_q, w_kv, cosine, sine
    )
    kv_near, kv_far = to_next(kv_own), swap(kv_own, "ctx")
    w_o = exchange([after(qkv_late[2], kv_own)] * 4)
    q, cot_x, cot_y = after([q, cot_x, cot_y], kv_near)
    cot_both = swap(cot_x, "ty")
    mixed, lse, kv = attend(info, q, kv_far, kv_near, kv_own)
    w_o, w_near, cot_both, mixed = after([w_o, w_near, cot_both, mixed])
    w_o = jnp.stack(w_o)
    w_o = [w_o, swap(w_o, "ctx")]
    w_far = swap(w_near, "tx")
    w_near = [w_near, swap(w_near, "ctx")]
    hidden, normed_mlp = project_out(info, mixed, x_rows, gain_rows, w_o)
    cot_parts = after([own_cot, cot_x, cot_y, cot_both], normed_mlp)
    cots = assemble(info, cot_parts)

    far = swap(normed_mlp, "ty")
    near_act, near_gu, *near_sums = mlp(info, normed_mlp, cots[0], w_near)
    far = after(far, near_act)
    far_act, far_gu, *far_sums = mlp(info, far, cots[1], w_near)
    mlp_rows = [normed_mlp, far]

    def over_cores(grads):
        return add(grads[0], swap(grads[1], "ctx")).astype(BF)

    def over_fsdp(grads):
        return lax.psum_scatter(grads, "fsdp", scatter_dimension=0, tiled=True)

    own_grads = unit_grads(info, mlp_rows, cots, [near_gu, far_gu], [near_act, far_act])
    w_far, own_grads = after([w_far, own_grads])
    w_far = [w_far, swap(w_far, "ctx")]
    own_grads, w_far = after([over_cores(own_grads), w_far])
    own_sums = over_fsdp(own_grads)
    far_act, far_gu, far_branch, *gn_y = mlp(
        info, far, cots[1], w_far, [far_sums[1], far_sums[0]], True
    )
    near_sums = after(near_sums, gn_y)
    gn_y = [swap(g, "ty") for g in gn_y]
    near_act, near_gu, branch, gn = mlp(
        info, normed_mlp, cots[0], w_far, [near_sums[1], near_sums[0]]
    )
    out_parts = split(info, branch, hidden, after(far_branch, gn))
    gn_y[0], near_act = after([gn_y[0], near_act], out_parts)
    other_grads = unit_grads(info, mlp_rows, cots, [near_gu, far_gu], [near_act, far_act])
    gn_y = after(gn_y, other_grads)

    grad_hidden, grad_low, gg_mlp = norm_back(
        info, gn, gn_y, cots[0], hidden, gain_rows
    )

    other_grads, grad_low = after([over_cores(after(other_grads, gn_y)), grad_low])
    other_sums = over_fsdp(other_grads)
    out_came = exchange(after(out_parts, gn_y))
    grad_q, kv_far, kv_near, kv_here = attend_back(
        info, grad_low, cosine, sine, q, kv, mixed, lse, w_o
    )
    kv_near, kv_far = to_next(kv_near, True), swap(kv_far, "ctx")
    grad_q, out_came, own_sums = after([grad_q, out_came, own_sums])
    mine, other = head_grads(
        info, c, shards, after([normed_attn, grad_q, grad_low, mixed], kv_near)
    )
    chip = sum_parts(info, mine, swap(other, "ctx"))
    plane = exchange(chip)
    kv_here = after(kv_here, chip)
    grad_kv, gg_attn, *grad_pieces = project_back(
        info,
        grad_q,
        kv_here,
        kv_near,
        kv_far,
        cosine,
        sine,
        x_rows,
        gain_rows,
        grad_hidden,
        w_q,
        w_kv,
    )
    mine, other = key_grads(info, c, shards, normed_attn, grad_kv, gg_attn, gg_mlp)
    keys = add(mine, swap(other, "ctx")).astype(BF)
    keys, other_sums, grad_pieces, plane = after([keys, other_sums, grad_pieces, plane])
    grad_came = exchange(grad_pieces)
    plane = add(*plane).astype(BF)
    keys, other_sums, grad_came[1], grad_came[2] = after(
        [keys, other_sums, grad_came[1], grad_came[2]], plane
    )
    total = fsdp_scatter(plane)
    from_x = swap(other_sums, "tx")
    keys = fsdp_halve(keys)
    keys = add(keys, swap(keys, "tx")).astype(BF)
    keys = add(keys, swap(keys, "ty"))
    total = [pair(c, g[:, :HEAD], g[:, HEAD:], 1) for g in (total[:sub], total[sub:])]
    grad_query, grad_output_proj = total[0], total[1].T
    grad_keyval = keys[:sub]
    gain_sums = [at(keys[sub + 4 * i : sub + 4 * i + 4], me) for i in range(2)]

    came = grad_came
    slot_own = pair(x, came[0], came[1], 0)
    slot_other = pair(x, came[2], came[3], 0)
    grad_tokens = jnp.stack(
        [pick(y, slot_other, slot_own), pick(y, slot_own, slot_other)]
    ).astype(F32)

    halves_out = [add(out_came[0], out_came[2]), add(out_came[1], out_came[3])]
    outputs = pair(x, *(h.astype(BF) for h in halves_out), 1)
    outputs = jnp.stack([pick(y, outputs[1], outputs[0]), pick(y, outputs[0], outputs[1])])

    mlp_grads = add(own_sums, from_x).astype(BF)
    mlp_other = swap(half_at(mlp_grads, 1 - c, 0), "ctx")
    mlp_own = half_at(mlp_grads, c, 0)

    def units_of(i):
        span = slice(i * units, (i + 1) * units)
        return pair(c, mlp_own[:, span], mlp_other[:, span], 1).astype(F32)

    grad_gateup = jnp.stack([units_of(0), units_of(1)])
    grad_down = units_of(2).T

    return (
        outputs,
        grad_tokens,
        grad_query,
        grad_keyval,
        grad_output_proj,
        grad_gateup,
        grad_down,
        gain_sums[0],
        gain_sums[1],
    )


def solution(mesh):
    names = dict(zip(mesh.axis_names, mesh.devices.shape))
    grid = mesh.devices.reshape(names["fsdp"], names["ctx"], 2, names["tp"] // 2)
    split = Mesh(grid, ("fsdp", "ctx", "ty", "tx"))
    tp = ("ty", "tx")
    in_specs = (
        P("fsdp", "ctx", tp),
        P("fsdp"),
        P("fsdp", tp),
        P("fsdp", None),
        P(tp, "fsdp"),
        P(None, "fsdp", tp),
        P(tp, "fsdp"),
        P(tp),
        P(tp),
        P("fsdp", "ctx", tp),
    )
    out_specs = (
        P("fsdp", "ctx", tp),
        P("fsdp", "ctx", tp),
        P(("fsdp", "ctx"), tp),
        P(("fsdp", "ctx"), None),
        P(tp, ("fsdp", "ctx")),
        P(None, ("fsdp", "ctx"), tp),
        P(tp, ("fsdp", "ctx")),
        P(tp),
        P(tp),
    )
    return jax.shard_map(body, mesh=split, in_specs=in_specs, out_specs=out_specs, check_vma=False)
```

time: 569 us -> 345 us (0.61)
  waiting for transfers between devices: 265 us -> 124 us
  matrix products: 78.5 us -> 0 us
  Pallas kernels: 27.9 us -> 104 us
  local copies, waits for them, and re-layouts: 87.8 us -> 26.2 us
  other arithmetic: 54.2 us -> 17.3 us
  starting transfers between devices: 30.7 us -> 52.7 us
    all_gather x3 -> x1, waiting for transfers between devices: 93.3 us -> 0.01 us  [body(): w_near = lax.all_gather(mlp_part, 'fsdp', axis=0, tiled=True)]
    dot_general x21 -> x0, matrix products: 78.5 us -> none  [the longest x7 35.4 us: mm(): return jnp.dot(a, b, preferred_element_type=F32)]
    pallas_call x2 -> x18, Pallas kernels: 27.9 us -> 104 us  [kernel(): return call(*args)]
    reduce_scatter x2, waiting for transfers between devices: 72.9 us -> 0.01 us  [over_fsdp(): return lax.psum_scatter(grads, 'fsdp', scatter_dimension=0, tiled=True)]
    ppermute x3 -> x10, waiting for transfers between devices: 4.51 us -> 31.6 us  [the longest x6 14.5 us: to_shard(): lax.ppermute(value, 'fsdp', [(i, (i + step) % shards) for i in range(shar...]
    reshape x8 -> x0, local copies, waits for them, and re-layouts: 18.2 us -> none  [the longest x2 6.61 us: body(): wq_blocks = grad_wq.reshape(shards, 2, sub, 4, feats)]
    ppermute x3 -> x10, starting transfers between devices: 3.87 us -> 14.1 us  [the longest x6 9.93 us: to_shard(): lax.ppermute(value, 'fsdp', [(i, (i + step) % shards) for i in range(shar...]
    slice x16 -> x2, local copies, waits for them, and re-layouts: 10.6 us -> 0.67 us  [the longest x1 0.66 us: body(): grad_keyval = keys[:sub]]
  transfers between devices with their start and end apart: 35 -> 53, of which waited for: 18 -> 29; matrix products, arithmetic and copies ran while one was open for 31% -> 5% of each run, Pallas kernels for 5% -> 29%
where the time goes in v2:
time: 345 us; the launch traced here: 340 us
  waiting for transfers between devices  124 us (36%)
  Pallas kernels  104 us (30%)
  starting transfers between devices  52.7 us (15%)
  local copies, waits for them, and re-layouts  26.2 us (8%)
  other arithmetic  17.3 us (5%)
  between operations  15 us (4%)
    pallas_call x18, Pallas kernels, kernel(): return call(*args)  104 us
    ppermute x34, waiting for transfers between devices, swap(): return lax.ppermute(value, axis, [(0, 1), (1, 0)])  85.9 us
    ppermute x34, starting transfers between devices, swap(): return lax.ppermute(value, axis, [(0, 1), (1, 0)])  28.3 us
    unnamed x150, local copies, waits for them, and re-layouts  22.3 us
    ppermute x6, waiting for transfers between devices, to_shard(): lax.ppermute(value, 'fsdp', [(i, (i + step) % shards) for i in range(shar...  14.5 us
    ppermute x2, waiting for transfers between devices, to_next(): lax.ppermute(value, ('ctx', 'tx'), [p[::-1] for p in pairs] if back else...  10.3 us
    ppermute x6, starting transfers between devices, swap_both(): return lax.ppermute(value, ('ty', 'tx'), [(i, i ^ 3) for i in range(4)])  10.1 us
    ppermute x6, starting transfers between devices, to_shard(): lax.ppermute(value, 'fsdp', [(i, (i + step) % shards) for i in range(shar...  9.93 us
  transfers between devices with their start and end apart: 53, of which 29 were waited for; matrix products, arithmetic and copies ran while one was open for 5% of the time, Pallas kernels for 29%

profile of v2, /device:TPU:0, one launch (start us, length us, event | category | flops | bytes accessed | tf_op | source)
XLA Modules:
  0.0 339.5 jit_solution(11626558934024627649)
XLA Ops:
  8.5 4.5 %prepare.1 = (bf16[528,256]{1,0:T(8,128)(2,1)}, bf16[528,256]{1,0:T(8,128)(2,1)}, bf16[528,256]{1,0:T(8,128)(2,1)}, bf16[528,256]{1,0:T(8,128)(2,1)}, bf16[2,512...) custom-call(s32[7]{0:T(128)} %stack.68.info, ...), custom_call_target="tpu_custom_call" | custom-call | bytes 393216 | tf_op jit(solution)/shard_map/prepare/pallas_call | solution.py:79
  13.0 3.0 collective-permute-start
  26.8 9.0 %collective-permute-done.1 = bf16[3,256,128]{2,1,0:T(8,128)(2,1)S(1)} collective-permute-done((bf16[3,256,128]{2,1,0:T(8,128)(2,1)}, bf16[3,256,128]{2,1,0:T(8,128)(2,1)S(1)}, u32[]{:S(2)}, u32[]{:S(2)}) %collective-permute-start.1) | collective-permute-done | bytes 196640 | tf_op jit(solution)/shard_map/ppermute | solution.py:695
  40.5 6.6 %collective-permute-done.8 = bf16[1024,128]{1,0:T(8,128)(2,1)S(1)} collective-permute-done((bf16[1024,128]{1,0:T(8,128)(2,1)S(1)}, bf16[1024,128]{1,0:T(8,128)(2,1)S(1)}, u32[]{:S(2)}, u32[]{:S(2)}) %collective-permute-start.8) | collective-permute-done | bytes 262176 | tf_op jit(solution)/shard_map/ppermute | solution.py:653
  47.1 4.6 %collective-permute-done.7 = bf16[1024,128]{1,0:T(8,128)(2,1)S(1)} collective-permute-done((bf16[1024,128]{1,0:T(8,128)(2,1)S(1)}, bf16[1024,128]{1,0:T(8,128)(2,1)S(1)}, u32[]{:S(2)}, u32[]{:S(2)}) %collective-permute-start.7) | collective-permute-done | bytes 262176 | tf_op jit(solution)/shard_map/ppermute | solution.py:649
  63.5 4.2 %collective-permute-done.14.refs_1_ = bf16[2,512,256]{2,1,0:T(8,128)(2,1)S(1)} collective-permute-done((bf16[2,512,256]{2,1,0:T(8,128)(2,1)}, bf16[2,512,256]{2,1,0:T(8,128)(2,1)S(1)}, u32[]{:S(2)}, u32[]{:S(2)}) %collective-permute-start.14) | collective-permute-done | bytes 524320 | tf_op jit(solution)/shard_map/ppermute | solution.py:649
  68.7 2.9 collective-permute-done.16.refs_2_
  77.4 10.4 %attend.1 = (bf16[512,1024]{1,0:T(8,128)(2,1)S(1)}, f32[512,8]{1,0:T(8,128)S(1)}, bf16[1536,256]{1,0:T(8,128)(2,1)S(1)}) custom-call(s32[7]{0:T(128)S(1)} %copy-done.59, bf16[512,1024]{1,0:T(8,128)(2,1)S(1)} %get-tuple-element.160.refs_0_.refs_3_, bf16[512,256]{1,0:T(8,128)(2,1)S(1)} %collective-permute-done.18.refs_1_, ...), custom_call_target="tpu_custom_call" | custom-call | flops 167772160 | bytes 327680 | tf_op jit(solution)/shard_map/attend/pallas_call | solution.py:79
  90.5 7.0 %collective-permute-done.12 = bf16[1024,128]{1,0:T(8,128)(2,1)S(1)} collective-permute-done((bf16[1024,128]{1,0:T(8,128)(2,1)S(1)}, bf16[1024,128]{1,0:T(8,128)(2,1)S(1)}, u32[]{:S(2)}, u32[]{:S(2)}) %collective-permute-start.12) | collective-permute-done | bytes 262176 | tf_op jit(solution)/shard_map/ppermute | solution.py:649
  101.4 3.5 %collective-permute-done.19.refs_4_.refs_8_ = bf16[4,1024,128]{2,1,0:T(8,128)(2,1)S(1)} collective-permute-done((bf16[4,1024,128]{2,1,0:T(8,128)(2,1)S(1)}, bf16[4,1024,128]{2,1,0:T(8,128)(2,1)S(1)}, u32[]{:S(2)}, u32[]{:S(2)}) %collective-permute-start.19) | collective-permute-done | bytes 1048608 | tf_op jit(solution)/shard_map/ppermute | solution.py:649
  110.8 6.8 %mlp.4 = (bf16[512,768]{1,0:T(8,128)(2,1)S(1)}, bf16[512,1536]{1,0:T(8,128)(2,1)S(1)}, bf16[512,1024]{1,0:T(8,128)(2,1)S(1)}, bf16[512,1024]{1,0:T(8,128)(2,1)S(1)}) custom-call(s32[7]{0:T(128)S(1)} %copy-done.59, bf16[512,1024]{1,0:T(8,128)(2,1)S(1)} %get-tuple-element.169.refs_0_, bf16[512,1024]{1,0:T(8,128)(2,1)S(1)} %get-tuple-element.176.refs_1_.refs_2_, ...), custom_call_target="tpu_custom_call" | custom-call | flops 301989888 | bytes 917504 | tf_op jit(solution)/shard_map/mlp/pallas_call | solution.py:79
  118.6 14.0 %collective-permute-done.20.refs_0_.refs_1_ = bf16[512,1024]{1,0:T(8,128)(2,1)S(1)} collective-permute-done((bf16[512,1024]{1,0:T(8,128)(2,1)S(1)}, bf16[512,1024]{1,0:T(8,128)(2,1)S(1)}, u32[]{:S(2)}, u32[]{:S(2)}) %collective-permute-start.20) | collective-permute-done | bytes 1048608 | tf_op jit(solution)/shard_map/ppermute | solution.py:649
  132.6 6.8 %mlp.5 = (bf16[512,768]{1,0:T(8,128)(2,1)S(1)}, bf16[512,1536]{1,0:T(8,128)(2,1)S(1)}, bf16[512,1024]{1,0:T(8,128)(2,1)S(1)}, bf16[512,1024]{1,0:T(8,128)(2,1)S(1)}) custom-call(s32[7]{0:T(128)S(1)} %copy-done.59, bf16[512,1024]{1,0:T(8,128)(2,1)S(1)} %collective-permute-done.20.refs_0_.refs_1_, bf16[512,1024]{1,0:T(8,128)(2,1)S(1)} %get-tuple-element.180.refs_1_.refs_3_, ...), custom_call_target="tpu_custom_call" | custom-call | flops 301989888 | bytes 917504 | tf_op jit(solution)/shard_map/mlp/pallas_call | solution.py:79
  141.3 7.7 %unit_grads.2 = (bf16[1024,1152]{1,0:T(8,128)(2,1)S(1)}, bf16[1024,1152]{1,0:T(8,128)(2,1)S(1)}) custom-call(s32[7]{0:T(128)S(1)} %copy-done.59, bf16[512,1024]{1,0:T(8,128)(2,1)S(1)} %get-tuple-element.169.refs_0_, bf16[512,1024]{1,0:T(8,128)(2,1)S(1)} %collective-permute-done.20.refs_0_.refs_1_, bf16[512,1024]{1,0:T(8,128)(2,1)S(1)} %get-tuple-element.176.refs_1_.refs_2_, ...), custom_call_target="tpu_custom_call" | custom-call | flops 301989888 | bytes 917504 | tf_op jit(solution)/shard_map/unit_grads/pallas_call | solution.py:79
  149.0 3.9 %collective-permute-done.22.refs_2_ = bf16[1024,1152]{1,0:T(8,128)(2,1)} collective-permute-done((bf16[1024,1152]{1,0:T(8,128)(2,1)}, bf16[1024,1152]{1,0:T(8,128)(2,1)}, u32[]{:S(2)}, u32[]{:S(2)}) %collective-permute-start.22) | collective-permute-done | bytes 2359328 | tf_op jit(solution)/shard_map/ppermute | solution.py:649
  153.4 7.4 %collective-permute-done.23 = bf16[1024,1152]{1,0:T(8,128)(2,1)S(1)} collective-permute-done((bf16[1024,1152]{1,0:T(8,128)(2,1)S(1)}, bf16[1024,1152]{1,0:T(8,128)(2,1)S(1)}, u32[]{:S(2)}, u32[]{:S(2)}) %collective-permute-start.23) | collective-permute-done | bytes 2359328 | tf_op jit(solution)/shard_map/ppermute | solution.py:649
  166.6 9.3 %mlp.6 = (bf16[512,768]{1,0:T(8,128)(2,1)S(1)}, bf16[512,1536]{1,0:T(8,128)(2,1)S(1)}, bf16[512,1024]{1,0:T(8,128)(2,1)S(1)}, bf16[256,1024]{1,0:T(8,128)(2,1)S(1)}, bf16[256,1024]{1,0:T(8,128)(2,1)S(1)}) custom-call(s32[7]{0:T(128)S(1)} %copy-done.59, bf16[512,1024]{1,0:T(8,128)(2,1)S(1)} %collective-permute-done.20.refs_0_.refs_1_, ...), custom_call_target="tpu_custom_call" | custom-call | flops 301989888 | bytes 917504 | tf_op jit(solution)/shard_map/mlp/pallas_call | solution.py:79
  178.0 9.0 %mlp.7 = (bf16[512,768]{1,0:T(8,128)(2,1)S(1)}, bf16[512,1536]{1,0:T(8,128)(2,1)S(1)}, bf16[512,1024]{1,0:T(8,128)(2,1)S(1)}, bf16[512,1024]{1,0:T(8,128)(2,1)S(1)}) custom-call(s32[7]{0:T(128)S(1)} %copy-done.59, bf16[512,1024]{1,0:T(8,128)(2,1)S(1)} %get-tuple-element.169.refs_0_, bf16[512,1024]{1,0:T(8,128)(2,1)S(1)} %get-tuple-element.176.refs_1_.refs_2_, ...), custom_call_target="tpu_custom_call" | custom-call | flops 301989888 | bytes 917504 | tf_op jit(solution)/shard_map/mlp/pallas_call | solution.py:79
  190.7 7.4 %unit_grads.3 = (bf16[1024,1152]{1,0:T(8,128)(2,1)S(1)}, bf16[1024,1152]{1,0:T(8,128)(2,1)S(1)}) custom-call(s32[7]{0:T(128)S(1)} %copy-done.59, bf16[512,1024]{1,0:T(8,128)(2,1)S(1)} %get-tuple-element.169.refs_0_, bf16[512,1024]{1,0:T(8,128)(2,1)S(1)} %collective-permute-done.20.refs_0_.refs_1_, bf16[512,1024]{1,0:T(8,128)(2,1)S(1)} %get-tuple-element.176.refs_1_.refs_2_, ...), custom_call_target="tpu_custom_call" | custom-call | flops 301989888 | bytes 917504 | tf_op jit(solution)/shard_map/unit_grads/pallas_call | solution.py:79
  198.1 3.1 collective-permute-done.26.refs_5_
  211.4 22.7 %attend_back.1 = (bf16[512,1024]{1,0:T(8,128)(2,1)}, bf16[512,256]{1,0:T(8,128)(2,1)}, bf16[512,256]{1,0:T(8,128)(2,1)}, f32[512,256]{1,0:T(8,128)}) custom-call(s32[7]{0:T(128)} %stack.68.info, bf16[512,1024]{1,0:T(8,128)(2,1)} %copy-done.24, f32[512,128]{1,0:T(8,128)} %copy-done.19, f32[512,128]{1,0:T(8,128)} %copy-done.17, bf16[512,1024]{1,0:T(8,128)(2,1)} %copy-done.26, ...), custom_call_target="tpu_custom_call" | custom-call | flops 461373440 | bytes 786432 | tf_op jit(solution)/shard_map/attend_back/pallas_call | solution.py:79
  234.4 7.4 %collective-permute-done.31.refs_2_ = bf16[512,256]{1,0:T(8,128)(2,1)S(1)} collective-permute-done((bf16[512,256]{1,0:T(8,128)(2,1)}, bf16[512,256]{1,0:T(8,128)(2,1)S(1)}, u32[]{:S(2)}, u32[]{:S(2)}) %collective-permute-start.31) | collective-permute-done | bytes 262176 | tf_op jit(solution)/shard_map/ppermute | solution.py:658
  243.1 3.0 head_grads.1
  246.7 3.6 %collective-permute-done.32.refs_1_ = bf16[4,4,256,256]{3,2,1,0:T(8,128)(2,1)S(1)} collective-permute-done((bf16[4,4,256,256]{3,2,1,0:T(8,128)(2,1)S(1)}, bf16[4,4,256,256]{3,2,1,0:T(8,128)(2,1)S(1)}, u32[]{:S(2)}, u32[]{:S(2)}) %collective-permute-start.32) | collective-permute-done | bytes 2097184 | tf_op jit(solution)/shard_map/ppermute | solution.py:649
  252.4 3.3 project_back.1
  261.3 11.5 %collective-permute-done.35 = bf16[4,256,256]{2,1,0:T(8,128)(2,1)} collective-permute-done((bf16[4,256,256]{2,1,0:T(8,128)(2,1)}, bf16[4,256,256]{2,1,0:T(8,128)(2,1)}, u32[]{:S(2)}, u32[]{:S(2)}) %collective-permute-start.35) | collective-permute-done | bytes 524320 | tf_op jit(solution)/shard_map/ppermute | solution.py:649
  272.8 12.1 %collective-permute-done.36 = bf16[4,256,256]{2,1,0:T(8,128)(2,1)} collective-permute-done((bf16[4,256,256]{2,1,0:T(8,128)(2,1)}, bf16[4,256,256]{2,1,0:T(8,128)(2,1)}, u32[]{:S(2)}, u32[]{:S(2)}) %collective-permute-start.36) | collective-permute-done | bytes 524320 | tf_op jit(solution)/shard_map/ppermute | solution.py:649
  286.7 3.8 %collective-permute-start.43 = (bf16[256,256]{1,0:T(8,128)(2,1)S(1)}, bf16[256,256]{1,0:T(8,128)(2,1)S(1)}, u32[]{:S(2)}, u32[]{:S(2)}) collective-permute-start(bf16[256,256]{1,0:T(8,128)(2,1)S(1)} %get-tuple-element.302), channel_id=1, source_target_pairs={{0,24},{8,0},{16,8},{24,16},{1,25},{9,1},{17,9},{25,17},{2,26},{10... | collective-permute-start | bytes 393224 | tf_op jit(solution)/shard_map/ppermute | solution.py:695
  296.2 4.5 %collective-permute-done.42 = bf16[256,256]{1,0:T(8,128)(2,1)S(1)} collective-permute-done((bf16[256,256]{1,0:T(8,128)(2,1)S(1)}, bf16[256,256]{1,0:T(8,128)(2,1)S(1)}, u32[]{:S(2)}, u32[]{:S(2)}) %collective-permute-start.42) | collective-permute-done | bytes 131104 | tf_op jit(solution)/shard_map/ppermute | solution.py:695
  311.5 2.9 collective-permute-done.44
  314.9 4.0 %collective-permute-done.45 = bf16[1,144,256]{2,1,0:T(8,128)(2,1)S(1)} collective-permute-done((bf16[1,144,256]{2,1,0:T(8,128)(2,1)S(1)}, bf16[1,144,256]{2,1,0:T(8,128)(2,1)S(1)}, u32[]{:S(2)}, u32[]{:S(2)}) %collective-permute-start.45) | collective-permute-done | bytes 73760 | tf_op jit(solution)/shard_map/ppermute | solution.py:730
  325.4 2.8 collective-permute-done.47
  (288 shorter events, 111.8 us)
Async XLA Ops:
  7.2 91.7 %all-gather.2.cloned.1.call-start = ((), (), s32[]{:S(2)}) async-start(), calls=%async_computation.2 | async-start | bytes 2949120 | tf_op jit(solution)/shard_map/all_gather | solution.py:761
  13.0 11.0 %collective-permute-start = (bf16[3,256,128]{2,1,0:T(8,128)(2,1)}, bf16[3,256,128]{2,1,0:T(8,128)(2,1)S(1)}, u32[]{:S(2)}, u32[]{:S(2)}) collective-permute-start(bf16[3,256,128]{2,1,0:T(8,128)(2,1)} %get-tuple-element.143), channel_id=1, source_target_pairs={{0,8},{8,16},{16,24},{24,0},{1,9},{9,17},{17,25},{25,1},{2,10},{10... | collective-permute-start | bytes 589832 | tf_op jit(solution)/shard_map/ppermute | solution.py:695
  16.1 19.8 %collective-permute-start.2 = (bf16[3,256,128]{2,1,0:T(8,128)(2,1)}, bf16[3,256,128]{2,1,0:T(8,128)(2,1)S(1)}, u32[]{:S(2)}, u32[]{:S(2)}) collective-permute-start(bf16[3,256,128]{2,1,0:T(8,128)(2,1)} %get-tuple-element.143), channel_id=1, source_target_pairs={{0,24},{8,0},{16,8},{24,16},{1,25},{9,1},{17,9},{25,17},{2,26},{10... | collective-permute-start | bytes 589832 | tf_op jit(solution)/shard_map/ppermute | solution.py:695
  18.1 17.7 %collective-permute-start.1 = (bf16[3,256,128]{2,1,0:T(8,128)(2,1)}, bf16[3,256,128]{2,1,0:T(8,128)(2,1)S(1)}, u32[]{:S(2)}, u32[]{:S(2)}) collective-permute-start(bf16[3,256,128]{2,1,0:T(8,128)(2,1)} %get-tuple-element.143), channel_id=1, source_target_pairs={{0,16},{8,24},{16,0},{24,8},{1,17},{9,25},{17,1},{25,9},{2,18},{10... | collective-permute-start | bytes 589832 | tf_op jit(solution)/shard_map/ppermute | solution.py:695
  19.1 16.8 %collective-permute-start.3 = (bf16[528,256]{1,0:T(8,128)(2,1)}, bf16[528,256]{1,0:T(8,128)(2,1)S(1)}, u32[]{:S(2)}, u32[]{:S(2)}) collective-permute-start(bf16[528,256]{1,0:T(8,128)(2,1)} %get-tuple-element.146), channel_id=1, source_target_pairs={{0,1},{1,0},{2,3},{3,2},{4,5},{5,4},{6,7},{7,6},{8,9},{9,8},{10,11... | collective-permute-start | bytes 811016 | tf_op jit(solution)/shard_map/ppermute | solution.py:649
  20.6 15.3 %collective-permute-start.4 = (bf16[528,256]{1,0:T(8,128)(2,1)}, bf16[528,256]{1,0:T(8,128)(2,1)S(1)}, u32[]{:S(2)}, u32[]{:S(2)}) collective-permute-start(bf16[528,256]{1,0:T(8,128)(2,1)} %get-tuple-element.147), channel_id=1, source_target_pairs={{0,2},{2,0},{1,3},{3,1},{4,6},{6,4},{5,7},{7,5},{8,10},{10,8},{9,1... | collective-permute-start | bytes 811016 | tf_op jit(solution)/shard_map/ppermute | solution.py:649
  24.1 11.9 %collective-permute-start.5 = (bf16[528,256]{1,0:T(8,128)(2,1)}, bf16[528,256]{1,0:T(8,128)(2,1)S(1)}, u32[]{:S(2)}, u32[]{:S(2)}) collective-permute-start(bf16[528,256]{1,0:T(8,128)(2,1)} %get-tuple-element.148), channel_id=1, source_target_pairs={{0,3},{1,2},{2,1},{3,0},{4,7},{5,6},{6,5},{7,4},{8,11},{9,10},{10,... | collective-permute-start | bytes 811016 | tf_op jit(solution)/shard_map/ppermute | solution.py:653
  36.8 197.7 %reduce-scatter.3.cloned.1.call-start = ((), (), s32[]{:S(2)}) async-start(), calls=%async_computation.3 | async-start | bytes 2949120 | tf_op jit(solution)/shard_map/reduce_scatter | solution.py:802
  39.5 12.3 %collective-permute-start.7 = (bf16[1024,128]{1,0:T(8,128)(2,1)S(1)}, bf16[1024,128]{1,0:T(8,128)(2,1)S(1)}, u32[]{:S(2)}, u32[]{:S(2)}) collective-permute-start(bf16[1024,128]{1,0:T(8,128)(2,1)S(1)} %get-tuple-element.299), channel_id=1, source_target_pairs={{0,2},{2,0},{1,3},{3,1},{4,6},{6,4},{5,7},{7,5},{8,10},{10,8},{9,1... | collective-permute-start | bytes 786440 | tf_op jit(solution)/shard_map/ppermute | solution.py:649
  40.0 11.9 %collective-permute-start.6 = (bf16[1024,128]{1,0:T(8,128)(2,1)S(1)}, bf16[1024,128]{1,0:T(8,128)(2,1)S(1)}, u32[]{:S(2)}, u32[]{:S(2)}) collective-permute-start(bf16[1024,128]{1,0:T(8,128)(2,1)S(1)} %get-tuple-element.299), channel_id=1, source_target_pairs={{0,1},{1,0},{2,3},{3,2},{4,5},{5,4},{6,7},{7,6},{8,9},{9,8},{10,11... | collective-permute-start | bytes 786440 | tf_op jit(solution)/shard_map/ppermute | solution.py:649
  52.7 15.0 %collective-permute-start.14 = (bf16[2,512,256]{2,1,0:T(8,128)(2,1)}, bf16[2,512,256]{2,1,0:T(8,128)(2,1)S(1)}, u32[]{:S(2)}, u32[]{:S(2)}) collective-permute-start(bf16[2,512,256]{2,1,0:T(8,128)(2,1)} %get-tuple-element.157), channel_id=1, source_target_pairs={{0,1},{1,0},{2,3},{3,2},{4,5},{5,4},{6,7},{7,6},{8,9},{9,8},{10,11... | collective-permute-start | bytes 1572872 | tf_op jit(solution)/shard_map/ppermute | solution.py:649
  54.2 13.6 %collective-permute-start.15 = (bf16[2,512,256]{2,1,0:T(8,128)(2,1)S(1)}, bf16[2,512,256]{2,1,0:T(8,128)(2,1)S(1)}, u32[]{:S(2)}, u32[]{:S(2)}) collective-permute-start(bf16[2,512,256]{2,1,0:T(8,128)(2,1)S(1)} %copy-done.38), channel_id=1, source_target_pairs={{0,2},{2,0},{1,3},{3,1},{4,6},{6,4},{5,7},{7,5},{8,10},{10,8},{9,1... | collective-permute-start | bytes 1572872 | tf_op jit(solution)/shard_map/ppermute | solution.py:649
  71.6 27.3 %collective-permute-start.17 = (bf16[2,512,256]{2,1,0:T(8,128)(2,1)S(1)}, bf16[2,512,256]{2,1,0:T(8,128)(2,1)S(1)}, u32[]{:S(2)}, u32[]{:S(2)}) collective-permute-start(bf16[2,512,256]{2,1,0:T(8,128)(2,1)S(1)} %collective-permute-done.14.refs_1_), channel_id=1, source_target_pairs={{0,2},{2,0},{1,3},{3,1},{4,6},{6,4},{5,7},{7,5},{8,10},{10,8},{9,1... | collective-permute-start | bytes 1572872 | tf_op jit(solution)/shard_map/ppermute | solution.py:649
  73.9 16.6 %collective-permute-start.13 = (bf16[1024,128]{1,0:T(8,128)(2,1)S(1)}, bf16[1024,128]{1,0:T(8,128)(2,1)S(1)}, u32[]{:S(2)}, u32[]{:S(2)}) collective-permute-start(bf16[1024,128]{1,0:T(8,128)(2,1)S(1)} %slice_bitcast_fusion.1), channel_id=1, source_target_pairs={{0,3},{1,2},{2,1},{3,0},{4,7},{5,6},{6,5},{7,4},{8,11},{9,10},{10,... | collective-permute-start | bytes 786440 | tf_op jit(solution)/shard_map/ppermute | solution.py:653
  75.5 22.0 %collective-permute-start.12 = (bf16[1024,128]{1,0:T(8,128)(2,1)S(1)}, bf16[1024,128]{1,0:T(8,128)(2,1)S(1)}, u32[]{:S(2)}, u32[]{:S(2)}) collective-permute-start(bf16[1024,128]{1,0:T(8,128)(2,1)S(1)} %slice_bitcast_fusion.1), channel_id=1, source_target_pairs={{0,2},{2,0},{1,3},{3,1},{4,6},{6,4},{5,7},{7,5},{8,10},{10,8},{9,1... | collective-permute-start | bytes 786440 | tf_op jit(solution)/shard_map/ppermute | solution.py:649
  76.2 21.3 %collective-permute-start.11 = (bf16[1024,128]{1,0:T(8,128)(2,1)S(1)}, bf16[1024,128]{1,0:T(8,128)(2,1)S(1)}, u32[]{:S(2)}, u32[]{:S(2)}) collective-permute-start(bf16[1024,128]{1,0:T(8,128)(2,1)S(1)} %slice_bitcast_fusion.1), channel_id=1, source_target_pairs={{0,1},{1,0},{2,3},{3,2},{4,5},{5,4},{6,7},{7,6},{8,9},{9,8},{10,11... | collective-permute-start | bytes 786440 | tf_op jit(solution)/shard_map/ppermute | solution.py:649
  98.9 11.9 %collective-permute-start.21 = (bf16[1024,1152]{1,0:T(8,128)(2,1)}, bf16[1024,1152]{1,0:T(8,128)(2,1)S(1)}, u32[]{:S(2)}, u32[]{:S(2)}) collective-permute-start(bf16[1024,1152]{1,0:T(8,128)(2,1)} %all-gather.2.cloned.1.call-done.refs_2_), channel_id=1, source_target_pairs={{0,4},{4,0},{1,5},{5,1},{2,6},{6,2},{3,7},{7,3},{8,12},{12,8},{9,1... | collective-permute-start | bytes 7077896 | tf_op jit(solution)/shard_map/ppermute | solution.py:649
  99.0 53.9 %collective-permute-start.22 = (bf16[1024,1152]{1,0:T(8,128)(2,1)}, bf16[1024,1152]{1,0:T(8,128)(2,1)}, u32[]{:S(2)}, u32[]{:S(2)}) collective-permute-start(bf16[1024,1152]{1,0:T(8,128)(2,1)} %all-gather.2.cloned.1.call-done.refs_2_), channel_id=1, source_target_pairs={{0,1},{1,0},{2,3},{3,2},{4,5},{5,4},{6,7},{7,6},{8,9},{9,8},{10,11... | collective-permute-start | bytes 7077896 | tf_op jit(solution)/shard_map/ppermute | solution.py:649
  107.3 25.3 %collective-permute-start.20 = (bf16[512,1024]{1,0:T(8,128)(2,1)S(1)}, bf16[512,1024]{1,0:T(8,128)(2,1)S(1)}, u32[]{:S(2)}, u32[]{:S(2)}) collective-permute-start(bf16[512,1024]{1,0:T(8,128)(2,1)S(1)} %get-tuple-element.169.refs_0_), channel_id=1, source_target_pairs={{0,2},{2,0},{1,3},{3,1},{4,6},{6,4},{5,7},{7,5},{8,10},{10,8},{9,1... | collective-permute-start | bytes 3145736 | tf_op jit(solution)/shard_map/ppermute | solution.py:649
  162.9 122.0 %reduce-scatter.5.cloned.1.call-start = ((), (), s32[]{:S(2)}) async-start(), calls=%async_computation.4 | async-start | bytes 2949120 | tf_op jit(solution)/shard_map/reduce_scatter | solution.py:802
  175.9 14.8 %collective-permute-start.25 = (bf16[256,1024]{1,0:T(8,128)(2,1)S(1)}, bf16[256,1024]{1,0:T(8,128)(2,1)S(1)}, u32[]{:S(2)}, u32[]{:S(2)}) collective-permute-start(bf16[256,1024]{1,0:T(8,128)(2,1)S(1)} %get-tuple-element.195), channel_id=1, source_target_pairs={{0,2},{2,0},{1,3},{3,1},{4,6},{6,4},{5,7},{7,5},{8,10},{10,8},{9,1... | collective-permute-start | bytes 1572872 | tf_op jit(solution)/shard_map/ppermute | solution.py:649
  177.6 23.6 %collective-permute-start.26 = (bf16[256,1024]{1,0:T(8,128)(2,1)S(1)}, bf16[256,1024]{1,0:T(8,128)(2,1)S(1)}, u32[]{:S(2)}, u32[]{:S(2)}) collective-permute-start(bf16[256,1024]{1,0:T(8,128)(2,1)S(1)} %get-tuple-element.196), channel_id=1, source_target_pairs={{0,2},{2,0},{1,3},{3,1},{4,6},{6,4},{5,7},{7,5},{8,10},{10,8},{9,1... | collective-permute-start | bytes 1572872 | tf_op jit(solution)/shard_map/ppermute | solution.py:649
  207.8 26.3 %collective-permute-start.28 = (bf16[2,512,256]{2,1,0:T(8,128)(2,1)}, bf16[2,512,256]{2,1,0:T(8,128)(2,1)}, u32[]{:S(2)}, u32[]{:S(2)}) collective-permute-start(bf16[2,512,256]{2,1,0:T(8,128)(2,1)} %get-tuple-element.226), channel_id=1, source_target_pairs={{0,1},{1,0},{2,3},{3,2},{4,5},{5,4},{6,7},{7,6},{8,9},{9,8},{10,11... | collective-permute-start | bytes 1572872 | tf_op jit(solution)/shard_map/ppermute | solution.py:649
  208.9 25.3 %collective-permute-start.29 = (bf16[2,512,256]{2,1,0:T(8,128)(2,1)}, bf16[2,512,256]{2,1,0:T(8,128)(2,1)}, u32[]{:S(2)}, u32[]{:S(2)}) collective-permute-start(bf16[2,512,256]{2,1,0:T(8,128)(2,1)} %get-tuple-element.227), channel_id=1, source_target_pairs={{0,2},{2,0},{1,3},{3,1},{4,6},{6,4},{5,7},{7,5},{8,10},{10,8},{9,1... | collective-permute-start | bytes 1572872 | tf_op jit(solution)/shard_map/ppermute | solution.py:649
  209.8 24.6 %collective-permute-start.30 = (bf16[2,512,256]{2,1,0:T(8,128)(2,1)}, bf16[2,512,256]{2,1,0:T(8,128)(2,1)}, u32[]{:S(2)}, u32[]{:S(2)}) collective-permute-start(bf16[2,512,256]{2,1,0:T(8,128)(2,1)} %get-tuple-element.228), channel_id=1, source_target_pairs={{0,3},{1,2},{2,1},{3,0},{4,7},{5,6},{6,5},{7,4},{8,11},{9,10},{10,... | collective-permute-start | bytes 1572872 | tf_op jit(solution)/shard_map/ppermute | solution.py:653
  257.7 15.1 %collective-permute-start.35 = (bf16[4,256,256]{2,1,0:T(8,128)(2,1)}, bf16[4,256,256]{2,1,0:T(8,128)(2,1)}, u32[]{:S(2)}, u32[]{:S(2)}) collective-permute-start(bf16[4,256,256]{2,1,0:T(8,128)(2,1)} %get-tuple-element.245), channel_id=1, source_target_pairs={{0,1},{1,0},{2,3},{3,2},{4,5},{5,4},{6,7},{7,6},{8,9},{9,8},{10,11... | collective-permute-start | bytes 1572872 | tf_op jit(solution)/shard_map/ppermute | solution.py:649
  259.4 25.5 %collective-permute-start.36 = (bf16[4,256,256]{2,1,0:T(8,128)(2,1)}, bf16[4,256,256]{2,1,0:T(8,128)(2,1)}, u32[]{:S(2)}, u32[]{:S(2)}) collective-permute-start(bf16[4,256,256]{2,1,0:T(8,128)(2,1)} %get-tuple-element.246), channel_id=1, source_target_pairs={{0,2},{2,0},{1,3},{3,1},{4,6},{6,4},{5,7},{7,5},{8,10},{10,8},{9,1... | collective-permute-start | bytes 1572872 | tf_op jit(solution)/shard_map/ppermute | solution.py:649
  260.9 24.0 %collective-permute-start.37 = (bf16[4,256,256]{2,1,0:T(8,128)(2,1)}, bf16[4,256,256]{2,1,0:T(8,128)(2,1)}, u32[]{:S(2)}, u32[]{:S(2)}) collective-permute-start(bf16[4,256,256]{2,1,0:T(8,128)(2,1)} %get-tuple-element.247), channel_id=1, source_target_pairs={{0,3},{1,2},{2,1},{3,0},{4,7},{5,6},{6,5},{7,4},{8,11},{9,10},{10,... | collective-permute-start | bytes 1572872 | tf_op jit(solution)/shard_map/ppermute | solution.py:653
  292.2 18.2 %collective-permute-start.38 = (bf16[512,256]{1,0:T(8,128)(2,1)S(1)}, bf16[512,256]{1,0:T(8,128)(2,1)}, u32[]{:S(2)}, u32[]{:S(2)}) collective-permute-start(bf16[512,256]{1,0:T(8,128)(2,1)S(1)} %copy-done.62), channel_id=1, source_target_pairs={{0,3},{1,2},{2,1},{3,0},{4,7},{5,6},{6,5},{7,4},{8,11},{9,10},{10,... | collective-permute-start | bytes 786440 | tf_op jit(solution)/shard_map/ppermute | solution.py:653
  293.6 11.1 %collective-permute-start.39 = (bf16[512,256]{1,0:T(8,128)(2,1)S(1)}, bf16[512,256]{1,0:T(8,128)(2,1)}, u32[]{:S(2)}, u32[]{:S(2)}) collective-permute-start(bf16[512,256]{1,0:T(8,128)(2,1)S(1)} %copy-done.66), channel_id=1, source_target_pairs={{0,1},{1,0},{2,3},{3,2},{4,5},{5,4},{6,7},{7,6},{8,9},{9,8},{10,11... | collective-permute-start | bytes 786440 | tf_op jit(solution)/shard_map/ppermute | solution.py:649
  295.0 10.7 %collective-permute-start.40 = (bf16[512,256]{1,0:T(8,128)(2,1)S(1)}, bf16[512,256]{1,0:T(8,128)(2,1)S(1)}, u32[]{:S(2)}, u32[]{:S(2)}) collective-permute-start(bf16[512,256]{1,0:T(8,128)(2,1)S(1)} %copy-done.64), channel_id=1, source_target_pairs={{0,2},{2,0},{1,3},{3,1},{4,6},{6,4},{5,7},{7,5},{8,10},{10,8},{9,1... | collective-permute-start | bytes 786440 | tf_op jit(solution)/shard_map/ppermute | solution.py:649
  308.3 20.6 %collective-permute-start.48 = (bf16[256,1152]{1,0:T(8,128)(2,1)}, bf16[256,1152]{1,0:T(8,128)(2,1)S(1)}, u32[]{:S(2)}, u32[]{:S(2)}) collective-permute-start(bf16[256,1152]{1,0:T(8,128)(2,1)} %reduce-scatter.5.cloned.1.call-done), channel_id=1, source_target_pairs={{0,1},{1,0},{2,3},{3,2},{4,5},{5,4},{6,7},{7,6},{8,9},{9,8},{10,11... | collective-permute-start | bytes 1769480 | tf_op jit(solution)/shard_map/ppermute | solution.py:649
  (95 other events, 863.0 us)
Sparse Core Ops, SparseCore 0:
  36.9 54.0 all-gather.1
  163.0 46.0 reduce-scatter.2
  211.3 47.5 reduce-scatter.4

commit v3 on v2

--- a/solution.py
+++ b/solution.py
@@ -319,7 +319,7 @@
 def attend_back_kernel(info, *refs):
     low_ref, cos_ref, sin_ref, q_ref, kv_ref, mixed_ref, lse_ref = refs[:7]
     w_o = refs[7:9]
-    gq_ref, far_ref, near_ref, here_ref, gkv_ref, bias_ref = refs[9:]
+    gq_ref, far_ref, near_ref, here_ref, gkv_ref, bias_ref, gm_ref, inner_ref, p_ref, gs_ref = refs[9:]
     step = pl.program_id(0)
     rows = here_ref.shape[0]
 
@@ -327,35 +327,57 @@
     def _():
         gkv_ref[...] = jnp.zeros_like(gkv_ref)
 
+    col = lax.broadcasted_iota(jnp.int32, (SPAN, ROWS), 0)
+    row = lax.broadcasted_iota(jnp.int32, (SPAN, ROWS), 1)
+    pos = info[ROW_START] - WINDOW + step * ROWS + col
+    ahead = col - row - WINDOW
+    inside = (ahead <= 0) & (ahead > -WINDOW) & (pos >= 0)
+    inside = inside & (pos < info[LENGTHS + info[SLOT]])
+    bias_ref[...] = jnp.where(inside | (ahead == 0), 0.0, NEG).astype(F32)
+
     low = low_ref[...]
-    fill_bias(bias_ref, info, step)
+    for j in range(4):
+        two = mm(low, two_heads(w_o[j // 2], j % 2)).astype(BF)
+        gm_ref[:, 2 * j * HEAD : 2 * (j + 1) * HEAD] = two
+        for i in range(2):
+            h = 2 * j + i
+            mixed = mixed_ref[:, h * HEAD : (h + 1) * HEAD].astype(F32)
+            gm = two[:, i * HEAD : (i + 1) * HEAD].astype(F32)
+            inner_ref[:, h : h + 1] = jnp.sum(gm * mixed, axis=1, keepdims=True)
+    inner = inner_ref[...].T
+    lse = lse_ref[...].T
     here = pl.ds(step * ROWS, SPAN)
-    keys = kv_ref[here, :HEAD]
-    values = kv_ref[here, HEAD:]
+    keys_t = kv_ref[here, :HEAD].T
     for j in range(4):
-        two = mm(low, two_heads(w_o[j // 2], j % 2))
         for i in range(2):
             h = 2 * j + i
             cols = slice(h * HEAD, (h + 1) * HEAD)
-            q = q_ref[:, cols]
-            gm = two[:, i * HEAD : (i + 1) * HEAD].astype(BF)
-            s = mm_nt(q, keys) * (SCALE * LOG2E) + bias_ref[...]
-            p = jnp.exp2(s - lse_ref[:, h : h + 1])
-            gp = mm_nt(gm, values)
-            inner = jnp.sum(
-                gm.astype(F32) * mixed_ref[:, cols].astype(F32), axis=1, keepdims=True
+            q, gm = q_ref[:, cols], gm_ref[:, cols]
+            for block in range(0, SPAN, ROWS):
+                part = slice(block, block + ROWS)
+                there = pl.ds(step * ROWS + block, ROWS)
+                s = mm_nt(kv_ref[there, :HEAD], q) * (SCALE * LOG2E) + bias_ref[part, :]
+                p = jnp.exp2(s - lse[h : h + 1, :])
+                gp = mm_nt(kv_ref[there, HEAD:], gm)
+                p_ref[part, i * ROWS : (i + 1) * ROWS] = p.astype(BF)
+                gs_ref[part, i * ROWS : (i + 1) * ROWS] = (p * (gp - inner[h : h + 1, :])).astype(BF)
+            gq = (mm(keys_t, gs_ref[:, i * ROWS : (i + 1) * ROWS]) * SCALE).T
+            gq_ref[:, cols] = turn(gq, cos_ref[...], -sin_ref[...]).astype(BF)
+
+        def stacked(ref):
+            return jnp.concatenate(
+                [ref[:, h * HEAD : (h + 1) * HEAD] for h in (2 * j, 2 * j + 1)], axis=0
             )
-            gs = (p * (gp - inner)).astype(BF)
-            gq = mm(gs, keys) * SCALE
-            gq_ref[:, cols] = turn(gq, cos_ref[...], -sin_ref[...]).astype(BF)
-            gkv_ref[here, :HEAD] += mm_tn(gs, q) * SCALE
-            gkv_ref[here, HEAD:] += mm_tn(p.astype(BF), gm)
+
+        gkv_ref[here, :HEAD] += mm(gs_ref[...], stacked(q_ref))
+        gkv_ref[here, HEAD:] += mm(p_ref[...], stacked(gm_ref))
 
     @pl.when(step == pl.num_programs(0) - 1)
     def _():
-        far_ref[...] = gkv_ref[:rows, :].astype(BF)
-        near_ref[...] = gkv_ref[rows : 2 * rows, :].astype(BF)
-        here_ref[...] = gkv_ref[2 * rows :, :]
+        for i, ref in enumerate((far_ref, near_ref, here_ref)):
+            block = slice(i * rows, (i + 1) * rows)
+            ref[:, :HEAD] = (gkv_ref[block, :HEAD] * SCALE).astype(ref.dtype)
+            ref[:, HEAD:] = gkv_ref[block, HEAD:].astype(ref.dtype)
 
 
 def attend_back(info, low, cosine, sine, q, kv, mixed, lse, w_o):
@@ -370,7 +392,14 @@
         [wide] + [None] * 3,
         [out((rows, 8 * HEAD), BF)] + [out((rows, 2 * HEAD), k) for k in (BF, BF, F32)],
         cost(10 * rows * D * (SPAN + HEAD), 12 << 20, rows * 8 * SPAN),
-        [pltpu.VMEM(kv.shape, F32), pltpu.VMEM((ROWS, SPAN), F32)],
+        [
+            pltpu.VMEM(kv.shape, F32),
+            pltpu.VMEM((SPAN, ROWS), F32),
+            pltpu.VMEM((ROWS, 8 * HEAD), BF),
+            pltpu.VMEM((ROWS, 8), F32),
+            pltpu.VMEM((SPAN, 2 * ROWS), BF),
+            pltpu.VMEM((SPAN, 2 * ROWS), BF),
+        ],
         60 << 20,
     )
 
@@ -852,19 +881,16 @@
         w_kv,
     )
     mine, other = key_grads(info, c, shards, normed_attn, grad_kv, gg_attn, gg_mlp)
-    keys = add(mine, swap(other, "ctx")).astype(BF)
-    keys, other_sums, grad_pieces, plane = after([keys, other_sums, grad_pieces, plane])
-    grad_came = exchange(grad_pieces)
+    keys = swap(other, "ctx")
+    plane, mine = after([plane, mine])
     plane = add(*plane).astype(BF)
-    keys, other_sums, grad_came[1], grad_came[2] = after(
-        [keys, other_sums, grad_came[1], grad_came[2]], plane
-    )
-    total = fsdp_scatter(plane)
+    keys, other_sums, grad_pieces = after([keys, other_sums, grad_pieces], plane)
+    keys = add(mine, keys).astype(BF)
+    total = fsdp_scatter(jnp.concatenate([plane, keys], axis=1))
+    grad_came = after(exchange(grad_pieces), total)
     from_x = swap(other_sums, "tx")
-    keys = fsdp_halve(keys)
-    keys = add(keys, swap(keys, "tx")).astype(BF)
-    keys = add(keys, swap(keys, "ty"))
-    total = [pair(c, g[:, :HEAD], g[:, HEAD:], 1) for g in (total[:sub], total[sub:])]
+    keys = add(*exchange([total[2 * sub :].astype(BF)] * 4))
+    total = [pair(c, g[:, :HEAD], g[:, HEAD:], 1) for g in (total[:sub], total[sub : 2 * sub])]
     grad_query, grad_output_proj = total[0], total[1].T
     grad_keyval = keys[:sub]
     gain_sums = [at(keys[sub + 4 * i : sub + 4 * i + 4], me) for i in range(2)]

time: 345 us -> 331 us (0.959)
  the two profiles are of different devices: /device:TPU:0 before, /device:TPU:9 now
where the time goes in v3:
time: 331 us; the launch traced here: 326 us
  waiting for transfers between devices  112 us (34%)
  Pallas kernels  101 us (31%)
  starting transfers between devices  56.6 us (17%)
  local copies, waits for them, and re-layouts  24 us (7%)
  other arithmetic  17.5 us (5%)
  between operations  14.9 us (5%)
    pallas_call x18, Pallas kernels, kernel(): return call(*args)  101 us
    ppermute x34, waiting for transfers between devices, swap(): return lax.ppermute(value, axis, [(0, 1), (1, 0)])  63.2 us
    ppermute x34, starting transfers between devices, swap(): return lax.ppermute(value, axis, [(0, 1), (1, 0)])  36 us
    ppermute x6, waiting for transfers between devices, to_shard(): lax.ppermute(value, 'fsdp', [(i, (i + step) % shards) for i in range(shar...  20.5 us
    unnamed x142, local copies, waits for them, and re-layouts  20.1 us
    ppermute x7, waiting for transfers between devices, swap_both(): return lax.ppermute(value, ('ty', 'tx'), [(i, i ^ 3) for i in range(4)])  18.8 us
    ppermute x2, waiting for transfers between devices, to_next(): lax.ppermute(value, ('ctx', 'tx'), [p[::-1] for p in pairs] if back else...  9.72 us
    ppermute x7, starting transfers between devices, swap_both(): return lax.ppermute(value, ('ty', 'tx'), [(i, i ^ 3) for i in range(4)])  8.86 us
  transfers between devices with their start and end apart: 52, of which 26 were waited for; matrix products, arithmetic and copies ran while one was open for 6% of the time, Pallas kernels for 30%

profile of v3, /device:TPU:9, one launch (start us, length us, event | category | flops | bytes accessed | tf_op | source)
XLA Modules:
  0.0 326.3 jit_solution(11141027946606793499)
XLA Ops:
  8.5 4.5 %prepare.1 = (bf16[528,256]{1,0:T(8,128)(2,1)}, bf16[528,256]{1,0:T(8,128)(2,1)}, bf16[528,256]{1,0:T(8,128)(2,1)}, bf16[528,256]{1,0:T(8,128)(2,1)}, bf16[2,512...) custom-call(s32[7]{0:T(128)} %stack.68.info, ...), custom_call_target="tpu_custom_call" | custom-call | bytes 393216 | tf_op jit(solution)/shard_map/prepare/pallas_call | solution.py:79
  21.2 9.6 %collective-permute-done.1 = bf16[3,256,128]{2,1,0:T(8,128)(2,1)S(1)} collective-permute-done((bf16[3,256,128]{2,1,0:T(8,128)(2,1)}, bf16[3,256,128]{2,1,0:T(8,128)(2,1)S(1)}, u32[]{:S(2)}, u32[]{:S(2)}) %collective-permute-start.1) | collective-permute-done | bytes 196640 | tf_op jit(solution)/shard_map/ppermute | solution.py:724
  34.7 4.4 %collective-permute-done.8 = bf16[1024,128]{1,0:T(8,128)(2,1)S(1)} collective-permute-done((bf16[1024,128]{1,0:T(8,128)(2,1)S(1)}, bf16[1024,128]{1,0:T(8,128)(2,1)S(1)}, u32[]{:S(2)}, u32[]{:S(2)}) %collective-permute-start.8) | collective-permute-done | bytes 262176 | tf_op jit(solution)/shard_map/ppermute | solution.py:682
  39.1 2.7 collective-permute-done.7
  42.1 7.1 %collective-permute-start.9 = (bf16[4,1024,128]{2,1,0:T(8,128)(2,1)S(1)}, bf16[4,1024,128]{2,1,0:T(8,128)(2,1)S(1)}, u32[]{:S(2)}, u32[]{:S(2)}) collective-permute-start(bf16[4,1024,128]{2,1,0:T(8,128)(2,1)S(1)} %pad_maximum_fusion.refs_4_.refs_9_), channel_id=1, source_target_pairs={{0,4},{4,0},{1,5},{5,1},{2,6},{6,2},{3,7},{7,3},{8,12},{12,8},{9,1... | collective-permute-start | bytes 3145736 | tf_op jit(solution)/shard_map/ppermute | solution.py:678
  54.5 2.8 project.1
  59.3 3.4 %collective-permute-done.14.refs_1_ = bf16[2,512,256]{2,1,0:T(8,128)(2,1)S(1)} collective-permute-done((bf16[2,512,256]{2,1,0:T(8,128)(2,1)}, bf16[2,512,256]{2,1,0:T(8,128)(2,1)S(1)}, u32[]{:S(2)}, u32[]{:S(2)}) %collective-permute-start.14) | collective-permute-done | bytes 524320 | tf_op jit(solution)/shard_map/ppermute | solution.py:678
  64.2 4.6 %collective-permute-done.16.refs_2_ = bf16[512,256]{1,0:T(8,128)(2,1)S(1)} collective-permute-done((bf16[512,256]{1,0:T(8,128)(2,1)S(1)}, bf16[512,256]{1,0:T(8,128)(2,1)S(1)}, u32[]{:S(2)}, u32[]{:S(2)}) %collective-permute-start.16) | collective-permute-done | bytes 262176 | tf_op jit(solution)/shard_map/ppermute | solution.py:687
  73.0 10.4 %attend.1 = (bf16[512,1024]{1,0:T(8,128)(2,1)S(1)}, f32[512,8]{1,0:T(8,128)S(1)}, bf16[1536,256]{1,0:T(8,128)(2,1)S(1)}) custom-call(s32[7]{0:T(128)S(1)} %copy-done.59, bf16[512,1024]{1,0:T(8,128)(2,1)S(1)} %get-tuple-element.161.refs_0_.refs_3_, bf16[512,256]{1,0:T(8,128)(2,1)S(1)} %collective-permute-done.18.refs_1_, ...), custom_call_target="tpu_custom_call" | custom-call | flops 167772160 | bytes 327680 | tf_op jit(solution)/shard_map/attend/pallas_call | solution.py:79
  86.0 7.8 %collective-permute-done.12 = bf16[1024,128]{1,0:T(8,128)(2,1)} collective-permute-done((bf16[1024,128]{1,0:T(8,128)(2,1)S(1)}, bf16[1024,128]{1,0:T(8,128)(2,1)}, u32[]{:S(2)}, u32[]{:S(2)}) %collective-permute-start.12) | collective-permute-done | bytes 262176 | tf_op jit(solution)/shard_map/ppermute | solution.py:678
  97.2 3.1 collective-permute-done.19.refs_4_.refs_8_
  105.8 6.8 %mlp.4 = (bf16[512,768]{1,0:T(8,128)(2,1)S(1)}, bf16[512,1536]{1,0:T(8,128)(2,1)S(1)}, bf16[512,1024]{1,0:T(8,128)(2,1)S(1)}, bf16[512,1024]{1,0:T(8,128)(2,1)S(1)}) custom-call(s32[7]{0:T(128)S(1)} %copy-done.59, bf16[512,1024]{1,0:T(8,128)(2,1)S(1)} %get-tuple-element.170.refs_0_, bf16[512,1024]{1,0:T(8,128)(2,1)S(1)} %get-tuple-element.177.refs_1_.refs_2_, ...), custom_call_target="tpu_custom_call" | custom-call | flops 301989888 | bytes 917504 | tf_op jit(solution)/shard_map/mlp/pallas_call | solution.py:79
  113.6 13.7 %collective-permute-done.20.refs_0_.refs_1_ = bf16[512,1024]{1,0:T(8,128)(2,1)S(1)} collective-permute-done((bf16[512,1024]{1,0:T(8,128)(2,1)S(1)}, bf16[512,1024]{1,0:T(8,128)(2,1)S(1)}, u32[]{:S(2)}, u32[]{:S(2)}) %collective-permute-start.20) | collective-permute-done | bytes 1048608 | tf_op jit(solution)/shard_map/ppermute | solution.py:678
  127.2 6.8 %mlp.5 = (bf16[512,768]{1,0:T(8,128)(2,1)S(1)}, bf16[512,1536]{1,0:T(8,128)(2,1)S(1)}, bf16[512,1024]{1,0:T(8,128)(2,1)S(1)}, bf16[512,1024]{1,0:T(8,128)(2,1)S(1)}) custom-call(s32[7]{0:T(128)S(1)} %copy-done.59, bf16[512,1024]{1,0:T(8,128)(2,1)S(1)} %collective-permute-done.20.refs_0_.refs_1_, bf16[512,1024]{1,0:T(8,128)(2,1)S(1)} %get-tuple-element.181.refs_1_.refs_3_, ...), custom_call_target="tpu_custom_call" | custom-call | flops 301989888 | bytes 917504 | tf_op jit(solution)/shard_map/mlp/pallas_call | solution.py:79
  136.0 7.6 %unit_grads.2 = (bf16[1024,1152]{1,0:T(8,128)(2,1)S(1)}, bf16[1024,1152]{1,0:T(8,128)(2,1)S(1)}) custom-call(s32[7]{0:T(128)S(1)} %copy-done.59, bf16[512,1024]{1,0:T(8,128)(2,1)S(1)} %get-tuple-element.170.refs_0_, bf16[512,1024]{1,0:T(8,128)(2,1)S(1)} %collective-permute-done.20.refs_0_.refs_1_, bf16[512,1024]{1,0:T(8,128)(2,1)S(1)} %get-tuple-element.177.refs_1_.refs_2_, ...), custom_call_target="tpu_custom_call" | custom-call | flops 301989888 | bytes 917504 | tf_op jit(solution)/shard_map/unit_grads/pallas_call | solution.py:79
  143.6 4.2 %collective-permute-done.22.refs_2_ = bf16[1024,1152]{1,0:T(8,128)(2,1)} collective-permute-done((bf16[1024,1152]{1,0:T(8,128)(2,1)}, bf16[1024,1152]{1,0:T(8,128)(2,1)}, u32[]{:S(2)}, u32[]{:S(2)}) %collective-permute-start.22) | collective-permute-done | bytes 2359328 | tf_op jit(solution)/shard_map/ppermute | solution.py:678
  148.6 7.5 %collective-permute-done.23 = bf16[1024,1152]{1,0:T(8,128)(2,1)S(1)} collective-permute-done((bf16[1024,1152]{1,0:T(8,128)(2,1)S(1)}, bf16[1024,1152]{1,0:T(8,128)(2,1)S(1)}, u32[]{:S(2)}, u32[]{:S(2)}) %collective-permute-start.23) | collective-permute-done | bytes 2359328 | tf_op jit(solution)/shard_map/ppermute | solution.py:678
  161.9 9.1 %mlp.6 = (bf16[512,768]{1,0:T(8,128)(2,1)S(1)}, bf16[512,1536]{1,0:T(8,128)(2,1)S(1)}, bf16[512,1024]{1,0:T(8,128)(2,1)S(1)}, bf16[256,1024]{1,0:T(8,128)(2,1)S(1)}, bf16[256,1024]{1,0:T(8,128)(2,1)S(1)}) custom-call(s32[7]{0:T(128)S(1)} %copy-done.59, bf16[512,1024]{1,0:T(8,128)(2,1)S(1)} %collective-permute-done.20.refs_0_.refs_1_, ...), custom_call_target="tpu_custom_call" | custom-call | flops 301989888 | bytes 917504 | tf_op jit(solution)/shard_map/mlp/pallas_call | solution.py:79
  172.6 9.0 %mlp.7 = (bf16[512,768]{1,0:T(8,128)(2,1)S(1)}, bf16[512,1536]{1,0:T(8,128)(2,1)S(1)}, bf16[512,1024]{1,0:T(8,128)(2,1)S(1)}, bf16[512,1024]{1,0:T(8,128)(2,1)S(1)}) custom-call(s32[7]{0:T(128)S(1)} %copy-done.59, bf16[512,1024]{1,0:T(8,128)(2,1)S(1)} %get-tuple-element.170.refs_0_, bf16[512,1024]{1,0:T(8,128)(2,1)S(1)} %get-tuple-element.177.refs_1_.refs_2_, ...), custom_call_target="tpu_custom_call" | custom-call | flops 301989888 | bytes 917504 | tf_op jit(solution)/shard_map/mlp/pallas_call | solution.py:79
  184.3 7.4 %unit_grads.3 = (bf16[1024,1152]{1,0:T(8,128)(2,1)S(1)}, bf16[1024,1152]{1,0:T(8,128)(2,1)S(1)}) custom-call(s32[7]{0:T(128)S(1)} %copy-done.59, bf16[512,1024]{1,0:T(8,128)(2,1)S(1)} %get-tuple-element.170.refs_0_, bf16[512,1024]{1,0:T(8,128)(2,1)S(1)} %collective-permute-done.20.refs_0_.refs_1_, bf16[512,1024]{1,0:T(8,128)(2,1)S(1)} %get-tuple-element.177.refs_1_.refs_2_, ...), custom_call_target="tpu_custom_call" | custom-call | flops 301989888 | bytes 917504 | tf_op jit(solution)/shard_map/unit_grads/pallas_call | solution.py:79
  191.8 3.8 %collective-permute-done.26.refs_5_ = bf16[256,1024]{1,0:T(8,128)(2,1)S(1)} collective-permute-done((bf16[256,1024]{1,0:T(8,128)(2,1)S(1)}, bf16[256,1024]{1,0:T(8,128)(2,1)S(1)}, u32[]{:S(2)}, u32[]{:S(2)}) %collective-permute-start.26) | collective-permute-done | bytes 524320 | tf_op jit(solution)/shard_map/ppermute | solution.py:678
  205.7 20.1 %attend_back.1 = (bf16[512,1024]{1,0:T(8,128)(2,1)}, bf16[512,256]{1,0:T(8,128)(2,1)}, bf16[512,256]{1,0:T(8,128)(2,1)}, f32[512,256]{1,0:T(8,128)}) custom-call(s32[7]{0:T(128)} %stack.68.info, bf16[512,1024]{1,0:T(8,128)(2,1)} %copy-done.24, f32[512,128]{1,0:T(8,128)} %copy-done.19, f32[512,128]{1,0:T(8,128)} %copy-done.17, bf16[512,1024]{1,0:T(8,128)(2,1)} %copy-done.26, ...), custom_call_target="tpu_custom_call" | custom-call | flops 461373440 | bytes 786432 | tf_op jit(solution)/shard_map/attend_back/pallas_call | solution.py:79
  228.5 5.1 %collective-permute-done.31.refs_2_ = bf16[512,256]{1,0:T(8,128)(2,1)S(1)} collective-permute-done((bf16[512,256]{1,0:T(8,128)(2,1)}, bf16[512,256]{1,0:T(8,128)(2,1)S(1)}, u32[]{:S(2)}, u32[]{:S(2)}) %collective-permute-start.31) | collective-permute-done | bytes 262176 | tf_op jit(solution)/shard_map/ppermute | solution.py:687
  234.9 3.0 head_grads.1
  239.1 3.8 %collective-permute-done.32.refs_1_ = bf16[4,4,256,256]{3,2,1,0:T(8,128)(2,1)S(1)} collective-permute-done((bf16[4,4,256,256]{3,2,1,0:T(8,128)(2,1)S(1)}, bf16[4,4,256,256]{3,2,1,0:T(8,128)(2,1)S(1)}, u32[]{:S(2)}, u32[]{:S(2)}) %collective-permute-start.32) | collective-permute-done | bytes 2097184 | tf_op jit(solution)/shard_map/ppermute | solution.py:678
  249.9 3.3 %project_back.1 = (bf16[512,256]{1,0:T(8,128)(2,1)S(1)}, f32[8,1024]{1,0:T(8,128)S(1)}, bf16[512,256]{1,0:T(8,128)(2,1)S(1)}, bf16[512,256]{1,0:T(8,128)(2,1)S(1...) custom-call(s32[7]{0:T(128)S(1)} %copy-done.60, bf16[512,1024]{1,0:T(8,128)(2,1)S(1)} %copy-done.16, ...), custom_call_target="tpu_custom_call" | custom-call | flops 83886080 | bytes 655360 | tf_op jit(solution)/shard_map/project_back/pallas_call | solution.py:79
  254.8 3.5 %collective-permute-done.35 = bf16[4,256,256]{2,1,0:T(8,128)(2,1)} collective-permute-done((bf16[4,256,256]{2,1,0:T(8,128)(2,1)}, bf16[4,256,256]{2,1,0:T(8,128)(2,1)}, u32[]{:S(2)}, u32[]{:S(2)}) %collective-permute-start.35) | collective-permute-done | bytes 524320 | tf_op jit(solution)/shard_map/ppermute | solution.py:678
  259.6 10.8 %collective-permute-done.37 = bf16[4,256,256]{2,1,0:T(8,128)(2,1)} collective-permute-done((bf16[4,256,256]{2,1,0:T(8,128)(2,1)}, bf16[4,256,256]{2,1,0:T(8,128)(2,1)}, u32[]{:S(2)}, u32[]{:S(2)}) %collective-permute-start.37) | collective-permute-done | bytes 524320 | tf_op jit(solution)/shard_map/ppermute | solution.py:682
  272.3 2.9 collective-permute-start.41
  281.8 9.4 %collective-permute-done.42 = bf16[400,256]{1,0:T(8,128)(2,1)S(1)} collective-permute-done((bf16[400,256]{1,0:T(8,128)(2,1)S(1)}, bf16[400,256]{1,0:T(8,128)(2,1)S(1)}, u32[]{:S(2)}, u32[]{:S(2)}) %collective-permute-start.42) | collective-permute-done | bytes 204832 | tf_op jit(solution)/shard_map/ppermute | solution.py:724
  302.8 5.4 %collective-permute-done.44 = bf16[144,256]{1,0:T(8,128)(2,1)S(1)} collective-permute-done((bf16[144,256]{1,0:T(8,128)(2,1)S(1)}, bf16[144,256]{1,0:T(8,128)(2,1)S(1)}, u32[]{:S(2)}, u32[]{:S(2)}) %collective-permute-start.44) | collective-permute-done | bytes 73760 | tf_op jit(solution)/shard_map/ppermute | solution.py:678
  312.7 3.6 %collective-permute-start.48 = (bf16[128,1152]{1,0:T(8,128)(2,1)S(1)}, bf16[128,1152]{1,0:T(8,128)(2,1)S(1)}, u32[]{:S(2)}, u32[]{:S(2)}) collective-permute-start(bf16[128,1152]{1,0:T(8,128)(2,1)S(1)} %constant_dynamic-slice_fusion.2), channel_id=1, source_target_pairs={{0,4},{4,0},{1,5},{5,1},{2,6},{6,2},{3,7},{7,3},{8,12},{12,8},{9,1... | collective-permute-start | bytes 884744 | tf_op jit(solution)/shard_map/ppermute | solution.py:678
  (274 shorter events, 104.3 us)
Async XLA Ops:
  7.2 86.7 %all-gather.2.cloned.1.call-start = ((), (), s32[]{:S(2)}) async-start(), calls=%async_computation.2 | async-start | bytes 2949120 | tf_op jit(solution)/shard_map/all_gather | solution.py:790
  14.3 16.6 %collective-permute-start.2 = (bf16[3,256,128]{2,1,0:T(8,128)(2,1)}, bf16[3,256,128]{2,1,0:T(8,128)(2,1)S(1)}, u32[]{:S(2)}, u32[]{:S(2)}) collective-permute-start(bf16[3,256,128]{2,1,0:T(8,128)(2,1)} %get-tuple-element.144), channel_id=1, source_target_pairs={{0,24},{8,0},{16,8},{24,16},{1,25},{9,1},{17,9},{25,17},{2,26},{10... | collective-permute-start | bytes 589832 | tf_op jit(solution)/shard_map/ppermute | solution.py:724
  14.5 16.4 %collective-permute-start.1 = (bf16[3,256,128]{2,1,0:T(8,128)(2,1)}, bf16[3,256,128]{2,1,0:T(8,128)(2,1)S(1)}, u32[]{:S(2)}, u32[]{:S(2)}) collective-permute-start(bf16[3,256,128]{2,1,0:T(8,128)(2,1)} %get-tuple-element.144), channel_id=1, source_target_pairs={{0,16},{8,24},{16,0},{24,8},{1,17},{9,25},{17,1},{25,9},{2,18},{10... | collective-permute-start | bytes 589832 | tf_op jit(solution)/shard_map/ppermute | solution.py:724
  16.8 14.1 %collective-permute-start.3 = (bf16[528,256]{1,0:T(8,128)(2,1)}, bf16[528,256]{1,0:T(8,128)(2,1)S(1)}, u32[]{:S(2)}, u32[]{:S(2)}) collective-permute-start(bf16[528,256]{1,0:T(8,128)(2,1)} %get-tuple-element.147), channel_id=1, source_target_pairs={{0,1},{1,0},{2,3},{3,2},{4,5},{5,4},{6,7},{7,6},{8,9},{9,8},{10,11... | collective-permute-start | bytes 811016 | tf_op jit(solution)/shard_map/ppermute | solution.py:678
  18.0 12.9 %collective-permute-start.4 = (bf16[528,256]{1,0:T(8,128)(2,1)}, bf16[528,256]{1,0:T(8,128)(2,1)S(1)}, u32[]{:S(2)}, u32[]{:S(2)}) collective-permute-start(bf16[528,256]{1,0:T(8,128)(2,1)} %get-tuple-element.148), channel_id=1, source_target_pairs={{0,2},{2,0},{1,3},{3,1},{4,6},{6,4},{5,7},{7,5},{8,10},{10,8},{9,1... | collective-permute-start | bytes 811016 | tf_op jit(solution)/shard_map/ppermute | solution.py:678
  31.8 196.8 %reduce-scatter.3.cloned.1.call-start = ((), (), s32[]{:S(2)}) async-start(), calls=%async_computation.3 | async-start | bytes 2949120 | tf_op jit(solution)/shard_map/reduce_scatter | solution.py:831
  49.3 13.4 %collective-permute-start.14 = (bf16[2,512,256]{2,1,0:T(8,128)(2,1)}, bf16[2,512,256]{2,1,0:T(8,128)(2,1)S(1)}, u32[]{:S(2)}, u32[]{:S(2)}) collective-permute-start(bf16[2,512,256]{2,1,0:T(8,128)(2,1)} %get-tuple-element.158), channel_id=1, source_target_pairs={{0,1},{1,0},{2,3},{3,2},{4,5},{5,4},{6,7},{7,6},{8,9},{9,8},{10,11... | collective-permute-start | bytes 1572872 | tf_op jit(solution)/shard_map/ppermute | solution.py:678
  50.6 12.9 %collective-permute-start.15 = (bf16[2,512,256]{2,1,0:T(8,128)(2,1)S(1)}, bf16[2,512,256]{2,1,0:T(8,128)(2,1)S(1)}, u32[]{:S(2)}, u32[]{:S(2)}) collective-permute-start(bf16[2,512,256]{2,1,0:T(8,128)(2,1)S(1)} %copy-done.38), channel_id=1, source_target_pairs={{0,2},{2,0},{1,3},{3,1},{4,6},{6,4},{5,7},{7,5},{8,10},{10,8},{9,1... | collective-permute-start | bytes 1572872 | tf_op jit(solution)/shard_map/ppermute | solution.py:678
  68.8 25.0 %collective-permute-start.17 = (bf16[2,512,256]{2,1,0:T(8,128)(2,1)S(1)}, bf16[2,512,256]{2,1,0:T(8,128)(2,1)S(1)}, u32[]{:S(2)}, u32[]{:S(2)}) collective-permute-start(bf16[2,512,256]{2,1,0:T(8,128)(2,1)S(1)} %collective-permute-done.14.refs_1_), channel_id=1, source_target_pairs={{0,2},{2,0},{1,3},{3,1},{4,6},{6,4},{5,7},{7,5},{8,10},{10,8},{9,1... | collective-permute-start | bytes 1572872 | tf_op jit(solution)/shard_map/ppermute | solution.py:678
  70.1 15.9 %collective-permute-start.13 = (bf16[1024,128]{1,0:T(8,128)(2,1)S(1)}, bf16[1024,128]{1,0:T(8,128)(2,1)}, u32[]{:S(2)}, u32[]{:S(2)}) collective-permute-start(bf16[1024,128]{1,0:T(8,128)(2,1)S(1)} %slice_bitcast_fusion.1), channel_id=1, source_target_pairs={{0,3},{1,2},{2,1},{3,0},{4,7},{5,6},{6,5},{7,4},{8,11},{9,10},{10,... | collective-permute-start | bytes 786440 | tf_op jit(solution)/shard_map/ppermute | solution.py:682
  72.3 21.5 %collective-permute-start.12 = (bf16[1024,128]{1,0:T(8,128)(2,1)S(1)}, bf16[1024,128]{1,0:T(8,128)(2,1)}, u32[]{:S(2)}, u32[]{:S(2)}) collective-permute-start(bf16[1024,128]{1,0:T(8,128)(2,1)S(1)} %slice_bitcast_fusion.1), channel_id=1, source_target_pairs={{0,2},{2,0},{1,3},{3,1},{4,6},{6,4},{5,7},{7,5},{8,10},{10,8},{9,1... | collective-permute-start | bytes 786440 | tf_op jit(solution)/shard_map/ppermute | solution.py:678
  73.0 20.9 %collective-permute-start.11 = (bf16[1024,128]{1,0:T(8,128)(2,1)S(1)}, bf16[1024,128]{1,0:T(8,128)(2,1)}, u32[]{:S(2)}, u32[]{:S(2)}) collective-permute-start(bf16[1024,128]{1,0:T(8,128)(2,1)S(1)} %slice_bitcast_fusion.1), channel_id=1, source_target_pairs={{0,1},{1,0},{2,3},{3,2},{4,5},{5,4},{6,7},{7,6},{8,9},{9,8},{10,11... | collective-permute-start | bytes 786440 | tf_op jit(solution)/shard_map/ppermute | solution.py:678
  94.6 53.1 %collective-permute-start.22 = (bf16[1024,1152]{1,0:T(8,128)(2,1)}, bf16[1024,1152]{1,0:T(8,128)(2,1)}, u32[]{:S(2)}, u32[]{:S(2)}) collective-permute-start(bf16[1024,1152]{1,0:T(8,128)(2,1)} %all-gather.2.cloned.1.call-done.refs_2_), channel_id=1, source_target_pairs={{0,1},{1,0},{2,3},{3,2},{4,5},{5,4},{6,7},{7,6},{8,9},{9,8},{10,11... | collective-permute-start | bytes 7077896 | tf_op jit(solution)/shard_map/ppermute | solution.py:678
  102.7 24.5 %collective-permute-start.20 = (bf16[512,1024]{1,0:T(8,128)(2,1)S(1)}, bf16[512,1024]{1,0:T(8,128)(2,1)S(1)}, u32[]{:S(2)}, u32[]{:S(2)}) collective-permute-start(bf16[512,1024]{1,0:T(8,128)(2,1)S(1)} %get-tuple-element.170.refs_0_), channel_id=1, source_target_pairs={{0,2},{2,0},{1,3},{3,1},{4,6},{6,4},{5,7},{7,5},{8,10},{10,8},{9,1... | collective-permute-start | bytes 3145736 | tf_op jit(solution)/shard_map/ppermute | solution.py:678
  158.2 113.9 %reduce-scatter.5.cloned.1.call-start = ((), (), s32[]{:S(2)}) async-start(), calls=%async_computation.4 | async-start | bytes 2949120 | tf_op jit(solution)/shard_map/reduce_scatter | solution.py:831
  171.1 13.3 %collective-permute-start.25 = (bf16[256,1024]{1,0:T(8,128)(2,1)S(1)}, bf16[256,1024]{1,0:T(8,128)(2,1)S(1)}, u32[]{:S(2)}, u32[]{:S(2)}) collective-permute-start(bf16[256,1024]{1,0:T(8,128)(2,1)S(1)} %get-tuple-element.196), channel_id=1, source_target_pairs={{0,2},{2,0},{1,3},{3,1},{4,6},{6,4},{5,7},{7,5},{8,10},{10,8},{9,1... | collective-permute-start | bytes 1572872 | tf_op jit(solution)/shard_map/ppermute | solution.py:678
  172.3 23.3 %collective-permute-start.26 = (bf16[256,1024]{1,0:T(8,128)(2,1)S(1)}, bf16[256,1024]{1,0:T(8,128)(2,1)S(1)}, u32[]{:S(2)}, u32[]{:S(2)}) collective-permute-start(bf16[256,1024]{1,0:T(8,128)(2,1)S(1)} %get-tuple-element.197), channel_id=1, source_target_pairs={{0,2},{2,0},{1,3},{3,1},{4,6},{6,4},{5,7},{7,5},{8,10},{10,8},{9,1... | collective-permute-start | bytes 1572872 | tf_op jit(solution)/shard_map/ppermute | solution.py:678
  202.9 24.7 %collective-permute-start.28 = (bf16[2,512,256]{2,1,0:T(8,128)(2,1)}, bf16[2,512,256]{2,1,0:T(8,128)(2,1)}, u32[]{:S(2)}, u32[]{:S(2)}) collective-permute-start(bf16[2,512,256]{2,1,0:T(8,128)(2,1)} %get-tuple-element.227), channel_id=1, source_target_pairs={{0,1},{1,0},{2,3},{3,2},{4,5},{5,4},{6,7},{7,6},{8,9},{9,8},{10,11... | collective-permute-start | bytes 1572872 | tf_op jit(solution)/shard_map/ppermute | solution.py:678
  203.7 23.9 %collective-permute-start.29 = (bf16[2,512,256]{2,1,0:T(8,128)(2,1)}, bf16[2,512,256]{2,1,0:T(8,128)(2,1)}, u32[]{:S(2)}, u32[]{:S(2)}) collective-permute-start(bf16[2,512,256]{2,1,0:T(8,128)(2,1)} %get-tuple-element.228), channel_id=1, source_target_pairs={{0,2},{2,0},{1,3},{3,1},{4,6},{6,4},{5,7},{7,5},{8,10},{10,8},{9,1... | collective-permute-start | bytes 1572872 | tf_op jit(solution)/shard_map/ppermute | solution.py:678
  204.4 24.1 %collective-permute-start.30 = (bf16[2,512,256]{2,1,0:T(8,128)(2,1)}, bf16[2,512,256]{2,1,0:T(8,128)(2,1)}, u32[]{:S(2)}, u32[]{:S(2)}) collective-permute-start(bf16[2,512,256]{2,1,0:T(8,128)(2,1)} %get-tuple-element.229), channel_id=1, source_target_pairs={{0,3},{1,2},{2,1},{3,0},{4,7},{5,6},{6,5},{7,4},{8,11},{9,10},{10,... | collective-permute-start | bytes 1572872 | tf_op jit(solution)/shard_map/ppermute | solution.py:682
  244.8 13.5 %collective-permute-start.35 = (bf16[4,256,256]{2,1,0:T(8,128)(2,1)}, bf16[4,256,256]{2,1,0:T(8,128)(2,1)}, u32[]{:S(2)}, u32[]{:S(2)}) collective-permute-start(bf16[4,256,256]{2,1,0:T(8,128)(2,1)} %get-tuple-element.246), channel_id=1, source_target_pairs={{0,1},{1,0},{2,3},{3,2},{4,5},{5,4},{6,7},{7,6},{8,9},{9,8},{10,11... | collective-permute-start | bytes 1572872 | tf_op jit(solution)/shard_map/ppermute | solution.py:678
  246.2 13.4 %collective-permute-start.36 = (bf16[4,256,256]{2,1,0:T(8,128)(2,1)}, bf16[4,256,256]{2,1,0:T(8,128)(2,1)}, u32[]{:S(2)}, u32[]{:S(2)}) collective-permute-start(bf16[4,256,256]{2,1,0:T(8,128)(2,1)} %get-tuple-element.247), channel_id=1, source_target_pairs={{0,2},{2,0},{1,3},{3,1},{4,6},{6,4},{5,7},{7,5},{8,10},{10,8},{9,1... | collective-permute-start | bytes 1572872 | tf_op jit(solution)/shard_map/ppermute | solution.py:678
  247.4 23.0 %collective-permute-start.37 = (bf16[4,256,256]{2,1,0:T(8,128)(2,1)}, bf16[4,256,256]{2,1,0:T(8,128)(2,1)}, u32[]{:S(2)}, u32[]{:S(2)}) collective-permute-start(bf16[4,256,256]{2,1,0:T(8,128)(2,1)} %get-tuple-element.248), channel_id=1, source_target_pairs={{0,3},{1,2},{2,1},{3,0},{4,7},{5,6},{6,5},{7,4},{8,11},{9,10},{10,... | collective-permute-start | bytes 1572872 | tf_op jit(solution)/shard_map/ppermute | solution.py:682
  254.4 17.7 %collective-permute-start.34 = (bf16[4,144,256]{2,1,0:T(8,128)(2,1)S(1)}, bf16[4,144,256]{2,1,0:T(8,128)(2,1)S(1)}, u32[]{:S(2)}, u32[]{:S(2)}) collective-permute-start(bf16[4,144,256]{2,1,0:T(8,128)(2,1)S(1)} %get-tuple-element.256), channel_id=1, source_target_pairs={{0,4},{4,0},{1,5},{5,1},{2,6},{6,2},{3,7},{7,3},{8,12},{12,8},{9,1... | collective-permute-start | bytes 884744 | tf_op jit(solution)/shard_map/ppermute | solution.py:678
  275.2 16.1 %collective-permute-start.42 = (bf16[400,256]{1,0:T(8,128)(2,1)S(1)}, bf16[400,256]{1,0:T(8,128)(2,1)S(1)}, u32[]{:S(2)}, u32[]{:S(2)}) collective-permute-start(bf16[400,256]{1,0:T(8,128)(2,1)S(1)} %get-tuple-element.301), channel_id=1, source_target_pairs={{0,16},{8,24},{16,0},{24,8},{1,17},{9,25},{17,1},{25,9},{2,18},{10... | collective-permute-start | bytes 614408 | tf_op jit(solution)/shard_map/ppermute | solution.py:724
  277.4 17.0 %collective-permute-start.43 = (bf16[400,256]{1,0:T(8,128)(2,1)S(1)}, bf16[400,256]{1,0:T(8,128)(2,1)S(1)}, u32[]{:S(2)}, u32[]{:S(2)}) collective-permute-start(bf16[400,256]{1,0:T(8,128)(2,1)S(1)} %get-tuple-element.302), channel_id=1, source_target_pairs={{0,24},{8,0},{16,8},{24,16},{1,25},{9,1},{17,9},{25,17},{2,26},{10... | collective-permute-start | bytes 614408 | tf_op jit(solution)/shard_map/ppermute | solution.py:724
  279.0 18.5 %collective-permute-start.38 = (bf16[512,256]{1,0:T(8,128)(2,1)S(1)}, bf16[512,256]{1,0:T(8,128)(2,1)S(1)}, u32[]{:S(2)}, u32[]{:S(2)}) collective-permute-start(bf16[512,256]{1,0:T(8,128)(2,1)S(1)} %copy-done.66), channel_id=1, source_target_pairs={{0,1},{1,0},{2,3},{3,2},{4,5},{5,4},{6,7},{7,6},{8,9},{9,8},{10,11... | collective-permute-start | bytes 786440 | tf_op jit(solution)/shard_map/ppermute | solution.py:678
  280.6 17.0 %collective-permute-start.39 = (bf16[512,256]{1,0:T(8,128)(2,1)S(1)}, bf16[512,256]{1,0:T(8,128)(2,1)}, u32[]{:S(2)}, u32[]{:S(2)}) collective-permute-start(bf16[512,256]{1,0:T(8,128)(2,1)S(1)} %copy-done.64), channel_id=1, source_target_pairs={{0,2},{2,0},{1,3},{3,1},{4,6},{6,4},{5,7},{7,5},{8,10},{10,8},{9,1... | collective-permute-start | bytes 786440 | tf_op jit(solution)/shard_map/ppermute | solution.py:678
  280.7 18.0 %collective-permute-start.40 = (bf16[512,256]{1,0:T(8,128)(2,1)S(1)}, bf16[512,256]{1,0:T(8,128)(2,1)}, u32[]{:S(2)}, u32[]{:S(2)}) collective-permute-start(bf16[512,256]{1,0:T(8,128)(2,1)S(1)} %copy-done.62), channel_id=1, source_target_pairs={{0,3},{1,2},{2,1},{3,0},{4,7},{5,6},{6,5},{7,4},{8,11},{9,10},{10,... | collective-permute-start | bytes 786440 | tf_op jit(solution)/shard_map/ppermute | solution.py:682
  291.3 20.2 %collective-permute-start.47 = (bf16[256,1152]{1,0:T(8,128)(2,1)}, bf16[256,1152]{1,0:T(8,128)(2,1)}, u32[]{:S(2)}, u32[]{:S(2)}) collective-permute-start(bf16[256,1152]{1,0:T(8,128)(2,1)} %reduce-scatter.5.cloned.1.call-done), channel_id=1, source_target_pairs={{0,1},{1,0},{2,3},{3,2},{4,5},{5,4},{6,7},{7,6},{8,9},{9,8},{10,11... | collective-permute-start | bytes 1769480 | tf_op jit(solution)/shard_map/ppermute | solution.py:678
  294.5 13.6 %collective-permute-start.44 = (bf16[144,256]{1,0:T(8,128)(2,1)S(1)}, bf16[144,256]{1,0:T(8,128)(2,1)S(1)}, u32[]{:S(2)}, u32[]{:S(2)}) collective-permute-start(bf16[144,256]{1,0:T(8,128)(2,1)S(1)} %slice.133), channel_id=1, source_target_pairs={{0,1},{1,0},{2,3},{3,2},{4,5},{5,4},{6,7},{7,6},{8,9},{9,8},{10,11... | collective-permute-start | bytes 221192 | tf_op jit(solution)/shard_map/ppermute | solution.py:678
  297.6 13.1 %collective-permute-start.46 = (bf16[144,256]{1,0:T(8,128)(2,1)S(1)}, bf16[144,256]{1,0:T(8,128)(2,1)S(1)}, u32[]{:S(2)}, u32[]{:S(2)}) collective-permute-start(bf16[144,256]{1,0:T(8,128)(2,1)S(1)} %slice.133), channel_id=1, source_target_pairs={{0,3},{1,2},{2,1},{3,0},{4,7},{5,6},{6,5},{7,4},{8,11},{9,10},{10,... | collective-permute-start | bytes 221192 | tf_op jit(solution)/shard_map/ppermute | solution.py:682
  (90 other events, 914.7 us)
Sparse Core Ops, SparseCore 0:
  31.9 55.7 all-gather.1
  158.3 45.5 reduce-scatter.2
  206.3 47.5 reduce-scatter.4

commit v4 on v3

--- a/solution.py
+++ b/solution.py
@@ -833,7 +833,8 @@
     own_grads = unit_grads(info, mlp_rows, cots, [near_gu, far_gu], [near_act, far_act])
     w_far, own_grads = after([w_far, own_grads])
     w_far = [w_far, swap(w_far, "ctx")]
-    own_grads, w_far = after([over_cores(own_grads), w_far])
+    own_grads = over_cores(own_grads)
+    w_far = after(w_far, own_grads)
     own_sums = over_fsdp(own_grads)
     far_act, far_gu, far_branch, *gn_y = mlp(
         info, far, cots[1], w_far, [far_sums[1], far_sums[0]], True
@@ -859,11 +860,11 @@
         info, grad_low, cosine, sine, q, kv, mixed, lse, w_o
     )
     kv_near, kv_far = to_next(kv_near, True), swap(kv_far, "ctx")
-    grad_q, out_came, own_sums = after([grad_q, out_came, own_sums])
-    mine, other = head_grads(
-        info, c, shards, after([normed_attn, grad_q, grad_low, mixed], kv_near)
-    )
-    chip = sum_parts(info, mine, swap(other, "ctx"))
+    grad_q, own_sums = after([grad_q, own_sums])
+    head_inputs = after([normed_attn, grad_q, grad_low, mixed], kv_near, kv_far)
+    mine, other = head_grads(info, c, shards, head_inputs)
+    out_came = after(out_came, mine)
+    chip = sum_parts(info, mine, swap(after(other, out_came), "ctx"))
     plane = exchange(chip)
     kv_here = after(kv_here, chip)
     grad_kv, gg_attn, *grad_pieces = project_back(

time: 331 us -> 331 us (level)
    unnamed x142 -> x140, local copies, waits for them, and re-layouts: 20.1 us -> 20.8 us
  transfers between devices with their start and end apart: 52 -> 52, of which waited for: 26 -> 24; matrix products, arithmetic and copies ran while one was open for 6% -> 6% of each run, Pallas kernels for 30% -> 30%
where the time goes in v4:
time: 331 us; the launch traced here: 326 us
  waiting for transfers between devices  111 us (34%)
  Pallas kernels  102 us (31%)
  starting transfers between devices  56.2 us (17%)
  local copies, waits for them, and re-layouts  24.6 us (7%)
  other arithmetic  17.5 us (5%)
  between operations  14.9 us (5%)
    pallas_call x18, Pallas kernels, kernel(): return call(*args)  102 us
    ppermute x34, waiting for transfers between devices, swap(): return lax.ppermute(value, axis, [(0, 1), (1, 0)])  62.1 us
    ppermute x34, starting transfers between devices, swap(): return lax.ppermute(value, axis, [(0, 1), (1, 0)])  35.6 us
    unnamed x140, local copies, waits for them, and re-layouts  20.8 us
    ppermute x6, waiting for transfers between devices, to_shard(): lax.ppermute(value, 'fsdp', [(i, (i + step) % shards) for i in range(shar...  20.5 us
    ppermute x7, waiting for transfers between devices, swap_both(): return lax.ppermute(value, ('ty', 'tx'), [(i, i ^ 3) for i in range(4)])  17.9 us
    ppermute x2, waiting for transfers between devices, to_next(): lax.ppermute(value, ('ctx', 'tx'), [p[::-1] for p in pairs] if back else...  10.6 us
    ppermute x7, starting transfers between devices, swap_both(): return lax.ppermute(value, ('ty', 'tx'), [(i, i ^ 3) for i in range(4)])  8.87 us
  transfers between devices with their start and end apart: 52, of which 24 were waited for; matrix products, arithmetic and copies ran while one was open for 6% of the time, Pallas kernels for 30%

profile of v4, /device:TPU:9, one launch (start us, length us, event | category | flops | bytes accessed | tf_op | source)
XLA Modules:
  0.0 326.1 jit_solution(9968147154617581522)
XLA Ops:
  8.5 4.5 %prepare.1 = (bf16[528,256]{1,0:T(8,128)(2,1)}, bf16[528,256]{1,0:T(8,128)(2,1)}, bf16[528,256]{1,0:T(8,128)(2,1)}, bf16[528,256]{1,0:T(8,128)(2,1)}, bf16[2,512...) custom-call(s32[7]{0:T(128)} %stack.68.info, ...), custom_call_target="tpu_custom_call" | custom-call | bytes 393216 | tf_op jit(solution)/shard_map/prepare/pallas_call | solution.py:79
  21.1 9.6 %collective-permute-done.1 = bf16[3,256,128]{2,1,0:T(8,128)(2,1)S(1)} collective-permute-done((bf16[3,256,128]{2,1,0:T(8,128)(2,1)}, bf16[3,256,128]{2,1,0:T(8,128)(2,1)S(1)}, u32[]{:S(2)}, u32[]{:S(2)}) %collective-permute-start.1) | collective-permute-done | bytes 196640 | tf_op jit(solution)/shard_map/ppermute | solution.py:724
  34.6 4.5 %collective-permute-done.8 = bf16[1024,128]{1,0:T(8,128)(2,1)S(1)} collective-permute-done((bf16[1024,128]{1,0:T(8,128)(2,1)S(1)}, bf16[1024,128]{1,0:T(8,128)(2,1)S(1)}, u32[]{:S(2)}, u32[]{:S(2)}) %collective-permute-start.8) | collective-permute-done | bytes 262176 | tf_op jit(solution)/shard_map/ppermute | solution.py:682
  39.0 2.7 collective-permute-done.7
  42.0 7.1 %collective-permute-start.9 = (bf16[4,1024,128]{2,1,0:T(8,128)(2,1)S(1)}, bf16[4,1024,128]{2,1,0:T(8,128)(2,1)S(1)}, u32[]{:S(2)}, u32[]{:S(2)}) collective-permute-start(bf16[4,1024,128]{2,1,0:T(8,128)(2,1)S(1)} %pad_maximum_fusion.refs_4_.refs_9_), channel_id=1, source_target_pairs={{0,4},{4,0},{1,5},{5,1},{2,6},{6,2},{3,7},{7,3},{8,12},{12,8},{9,1... | collective-permute-start | bytes 3145736 | tf_op jit(solution)/shard_map/ppermute | solution.py:678
  54.5 2.8 project.1
  59.2 3.4 %collective-permute-done.14.refs_1_ = bf16[2,512,256]{2,1,0:T(8,128)(2,1)S(1)} collective-permute-done((bf16[2,512,256]{2,1,0:T(8,128)(2,1)}, bf16[2,512,256]{2,1,0:T(8,128)(2,1)S(1)}, u32[]{:S(2)}, u32[]{:S(2)}) %collective-permute-start.14) | collective-permute-done | bytes 524320 | tf_op jit(solution)/shard_map/ppermute | solution.py:678
  64.1 4.6 %collective-permute-done.16.refs_2_ = bf16[512,256]{1,0:T(8,128)(2,1)S(1)} collective-permute-done((bf16[512,256]{1,0:T(8,128)(2,1)S(1)}, bf16[512,256]{1,0:T(8,128)(2,1)S(1)}, u32[]{:S(2)}, u32[]{:S(2)}) %collective-permute-start.16) | collective-permute-done | bytes 262176 | tf_op jit(solution)/shard_map/ppermute | solution.py:687
  72.9 10.4 %attend.1 = (bf16[512,1024]{1,0:T(8,128)(2,1)S(1)}, f32[512,8]{1,0:T(8,128)S(1)}, bf16[1536,256]{1,0:T(8,128)(2,1)S(1)}) custom-call(s32[7]{0:T(128)S(1)} %copy-done.59, bf16[512,1024]{1,0:T(8,128)(2,1)S(1)} %get-tuple-element.161.refs_0_.refs_3_, bf16[512,256]{1,0:T(8,128)(2,1)S(1)} %collective-permute-done.18.refs_1_, ...), custom_call_target="tpu_custom_call" | custom-call | flops 167772160 | bytes 327680 | tf_op jit(solution)/shard_map/attend/pallas_call | solution.py:79
  85.9 7.8 %collective-permute-done.12 = bf16[1024,128]{1,0:T(8,128)(2,1)} collective-permute-done((bf16[1024,128]{1,0:T(8,128)(2,1)S(1)}, bf16[1024,128]{1,0:T(8,128)(2,1)}, u32[]{:S(2)}, u32[]{:S(2)}) %collective-permute-start.12) | collective-permute-done | bytes 262176 | tf_op jit(solution)/shard_map/ppermute | solution.py:678
  97.1 3.1 collective-permute-done.19.refs_4_.refs_8_
  105.7 6.8 %mlp.4 = (bf16[512,768]{1,0:T(8,128)(2,1)S(1)}, bf16[512,1536]{1,0:T(8,128)(2,1)S(1)}, bf16[512,1024]{1,0:T(8,128)(2,1)S(1)}, bf16[512,1024]{1,0:T(8,128)(2,1)S(1)}) custom-call(s32[7]{0:T(128)S(1)} %copy-done.59, bf16[512,1024]{1,0:T(8,128)(2,1)S(1)} %get-tuple-element.170.refs_0_, bf16[512,1024]{1,0:T(8,128)(2,1)S(1)} %get-tuple-element.177.refs_1_.refs_2_, ...), custom_call_target="tpu_custom_call" | custom-call | flops 301989888 | bytes 917504 | tf_op jit(solution)/shard_map/mlp/pallas_call | solution.py:79
  113.5 13.7 %collective-permute-done.21.refs_0_.refs_1_ = bf16[512,1024]{1,0:T(8,128)(2,1)S(1)} collective-permute-done((bf16[512,1024]{1,0:T(8,128)(2,1)S(1)}, bf16[512,1024]{1,0:T(8,128)(2,1)S(1)}, u32[]{:S(2)}, u32[]{:S(2)}) %collective-permute-start.21) | collective-permute-done | bytes 1048608 | tf_op jit(solution)/shard_map/ppermute | solution.py:678
  127.2 6.8 %mlp.5 = (bf16[512,768]{1,0:T(8,128)(2,1)S(1)}, bf16[512,1536]{1,0:T(8,128)(2,1)S(1)}, bf16[512,1024]{1,0:T(8,128)(2,1)S(1)}, bf16[512,1024]{1,0:T(8,128)(2,1)S(1)}) custom-call(s32[7]{0:T(128)S(1)} %copy-done.59, bf16[512,1024]{1,0:T(8,128)(2,1)S(1)} %collective-permute-done.21.refs_0_.refs_1_, bf16[512,1024]{1,0:T(8,128)(2,1)S(1)} %get-tuple-element.181.refs_1_.refs_3_, ...), custom_call_target="tpu_custom_call" | custom-call | flops 301989888 | bytes 917504 | tf_op jit(solution)/shard_map/mlp/pallas_call | solution.py:79
  135.9 7.6 %unit_grads.2 = (bf16[1024,1152]{1,0:T(8,128)(2,1)S(1)}, bf16[1024,1152]{1,0:T(8,128)(2,1)S(1)}) custom-call(s32[7]{0:T(128)S(1)} %copy-done.59, bf16[512,1024]{1,0:T(8,128)(2,1)S(1)} %get-tuple-element.170.refs_0_, bf16[512,1024]{1,0:T(8,128)(2,1)S(1)} %collective-permute-done.21.refs_0_.refs_1_, bf16[512,1024]{1,0:T(8,128)(2,1)S(1)} %get-tuple-element.177.refs_1_.refs_2_, ...), custom_call_target="tpu_custom_call" | custom-call | flops 301989888 | bytes 917504 | tf_op jit(solution)/shard_map/unit_grads/pallas_call | solution.py:79
  143.5 4.2 %collective-permute-done.20.refs_2_ = bf16[1024,1152]{1,0:T(8,128)(2,1)} collective-permute-done((bf16[1024,1152]{1,0:T(8,128)(2,1)}, bf16[1024,1152]{1,0:T(8,128)(2,1)}, u32[]{:S(2)}, u32[]{:S(2)}) %collective-permute-start.20) | collective-permute-done | bytes 2359328 | tf_op jit(solution)/shard_map/ppermute | solution.py:678
  148.5 7.5 %collective-permute-done.24 = bf16[1024,1152]{1,0:T(8,128)(2,1)S(1)} collective-permute-done((bf16[1024,1152]{1,0:T(8,128)(2,1)S(1)}, bf16[1024,1152]{1,0:T(8,128)(2,1)S(1)}, u32[]{:S(2)}, u32[]{:S(2)}) %collective-permute-start.24) | collective-permute-done | bytes 2359328 | tf_op jit(solution)/shard_map/ppermute | solution.py:678
  161.9 9.1 %mlp.6 = (bf16[512,768]{1,0:T(8,128)(2,1)S(1)}, bf16[512,1536]{1,0:T(8,128)(2,1)S(1)}, bf16[512,1024]{1,0:T(8,128)(2,1)S(1)}, bf16[256,1024]{1,0:T(8,128)(2,1)S(1)}, bf16[256,1024]{1,0:T(8,128)(2,1)S(1)}) custom-call(s32[7]{0:T(128)S(1)} %copy-done.59, bf16[512,1024]{1,0:T(8,128)(2,1)S(1)} %collective-permute-done.21.refs_0_.refs_1_, ...), custom_call_target="tpu_custom_call" | custom-call | flops 301989888 | bytes 917504 | tf_op jit(solution)/shard_map/mlp/pallas_call | solution.py:79
  172.5 9.0 %mlp.7 = (bf16[512,768]{1,0:T(8,128)(2,1)S(1)}, bf16[512,1536]{1,0:T(8,128)(2,1)S(1)}, bf16[512,1024]{1,0:T(8,128)(2,1)S(1)}, bf16[512,1024]{1,0:T(8,128)(2,1)S(1)}) custom-call(s32[7]{0:T(128)S(1)} %copy-done.59, bf16[512,1024]{1,0:T(8,128)(2,1)S(1)} %get-tuple-element.170.refs_0_, bf16[512,1024]{1,0:T(8,128)(2,1)S(1)} %get-tuple-element.177.refs_1_.refs_2_, ...), custom_call_target="tpu_custom_call" | custom-call | flops 301989888 | bytes 917504 | tf_op jit(solution)/shard_map/mlp/pallas_call | solution.py:79
  184.3 7.4 %unit_grads.3 = (bf16[1024,1152]{1,0:T(8,128)(2,1)S(1)}, bf16[1024,1152]{1,0:T(8,128)(2,1)S(1)}) custom-call(s32[7]{0:T(128)S(1)} %copy-done.59, bf16[512,1024]{1,0:T(8,128)(2,1)S(1)} %get-tuple-element.170.refs_0_, bf16[512,1024]{1,0:T(8,128)(2,1)S(1)} %collective-permute-done.21.refs_0_.refs_1_, bf16[512,1024]{1,0:T(8,128)(2,1)S(1)} %get-tuple-element.177.refs_1_.refs_2_, ...), custom_call_target="tpu_custom_call" | custom-call | flops 301989888 | bytes 917504 | tf_op jit(solution)/shard_map/unit_grads/pallas_call | solution.py:79
  191.7 3.8 %collective-permute-done.26.refs_5_ = bf16[256,1024]{1,0:T(8,128)(2,1)S(1)} collective-permute-done((bf16[256,1024]{1,0:T(8,128)(2,1)S(1)}, bf16[256,1024]{1,0:T(8,128)(2,1)S(1)}, u32[]{:S(2)}, u32[]{:S(2)}) %collective-permute-start.26) | collective-permute-done | bytes 524320 | tf_op jit(solution)/shard_map/ppermute | solution.py:678
  205.6 20.1 %attend_back.1 = (bf16[512,1024]{1,0:T(8,128)(2,1)}, bf16[512,256]{1,0:T(8,128)(2,1)}, bf16[512,256]{1,0:T(8,128)(2,1)}, f32[512,256]{1,0:T(8,128)}) custom-call(s32[7]{0:T(128)} %stack.68.info, bf16[512,1024]{1,0:T(8,128)(2,1)} %copy-done.24, f32[512,128]{1,0:T(8,128)} %copy-done.19, f32[512,128]{1,0:T(8,128)} %copy-done.17, bf16[512,1024]{1,0:T(8,128)(2,1)} %copy-done.26, ...), custom_call_target="tpu_custom_call" | custom-call | flops 461373440 | bytes 786432 | tf_op jit(solution)/shard_map/attend_back/pallas_call | solution.py:79
  227.6 6.0 %collective-permute-done.31.refs_2_ = bf16[512,256]{1,0:T(8,128)(2,1)S(1)} collective-permute-done((bf16[512,256]{1,0:T(8,128)(2,1)}, bf16[512,256]{1,0:T(8,128)(2,1)S(1)}, u32[]{:S(2)}, u32[]{:S(2)}) %collective-permute-start.31) | collective-permute-done | bytes 262176 | tf_op jit(solution)/shard_map/ppermute | solution.py:687
  234.8 3.0 head_grads.1
  239.0 3.8 %collective-permute-done.33.refs_1_ = bf16[4,4,256,256]{3,2,1,0:T(8,128)(2,1)S(1)} collective-permute-done((bf16[4,4,256,256]{3,2,1,0:T(8,128)(2,1)S(1)}, bf16[4,4,256,256]{3,2,1,0:T(8,128)(2,1)S(1)}, u32[]{:S(2)}, u32[]{:S(2)}) %collective-permute-start.33) | collective-permute-done | bytes 2097184 | tf_op jit(solution)/shard_map/ppermute | solution.py:678
  247.5 4.2 %project_back.1 = (bf16[512,256]{1,0:T(8,128)(2,1)S(1)}, f32[8,1024]{1,0:T(8,128)S(1)}, bf16[512,256]{1,0:T(8,128)(2,1)S(1)}, bf16[512,256]{1,0:T(8,128)(2,1)S(1...) custom-call(s32[7]{0:T(128)S(1)} %copy-done.60, bf16[512,1024]{1,0:T(8,128)(2,1)S(1)} %copy-done.16, ...), custom_call_target="tpu_custom_call" | custom-call | flops 83886080 | bytes 655360 | tf_op jit(solution)/shard_map/project_back/pallas_call | solution.py:79
  254.8 3.4 %collective-permute-done.35 = bf16[4,256,256]{2,1,0:T(8,128)(2,1)} collective-permute-done((bf16[4,256,256]{2,1,0:T(8,128)(2,1)}, bf16[4,256,256]{2,1,0:T(8,128)(2,1)}, u32[]{:S(2)}, u32[]{:S(2)}) %collective-permute-start.35) | collective-permute-done | bytes 524320 | tf_op jit(solution)/shard_map/ppermute | solution.py:678
  259.5 10.8 %collective-permute-done.37 = bf16[4,256,256]{2,1,0:T(8,128)(2,1)} collective-permute-done((bf16[4,256,256]{2,1,0:T(8,128)(2,1)S(1)}, bf16[4,256,256]{2,1,0:T(8,128)(2,1)}, u32[]{:S(2)}, u32[]{:S(2)}) %collective-permute-start.37) | collective-permute-done | bytes 524320 | tf_op jit(solution)/shard_map/ppermute | solution.py:682
  272.2 2.9 collective-permute-start.41
  281.7 9.5 %collective-permute-done.42 = bf16[400,256]{1,0:T(8,128)(2,1)S(1)} collective-permute-done((bf16[400,256]{1,0:T(8,128)(2,1)S(1)}, bf16[400,256]{1,0:T(8,128)(2,1)S(1)}, u32[]{:S(2)}, u32[]{:S(2)}) %collective-permute-start.42) | collective-permute-done | bytes 204832 | tf_op jit(solution)/shard_map/ppermute | solution.py:724
  302.6 5.4 %collective-permute-done.44 = bf16[144,256]{1,0:T(8,128)(2,1)S(1)} collective-permute-done((bf16[144,256]{1,0:T(8,128)(2,1)S(1)}, bf16[144,256]{1,0:T(8,128)(2,1)S(1)}, u32[]{:S(2)}, u32[]{:S(2)}) %collective-permute-start.44) | collective-permute-done | bytes 73760 | tf_op jit(solution)/shard_map/ppermute | solution.py:678
  312.6 3.6 %collective-permute-start.48 = (bf16[128,1152]{1,0:T(8,128)(2,1)S(1)}, bf16[128,1152]{1,0:T(8,128)(2,1)S(1)}, u32[]{:S(2)}, u32[]{:S(2)}) collective-permute-start(bf16[128,1152]{1,0:T(8,128)(2,1)S(1)} %constant_dynamic-slice_fusion.2), channel_id=1, source_target_pairs={{0,4},{4,0},{1,5},{5,1},{2,6},{6,2},{3,7},{7,3},{8,12},{12,8},{9,1... | collective-permute-start | bytes 884744 | tf_op jit(solution)/shard_map/ppermute | solution.py:678
  (272 shorter events, 102.3 us)
Async XLA Ops:
  7.2 86.6 %all-gather.2.cloned.1.call-start = ((), (), s32[]{:S(2)}) async-start(), calls=%async_computation.2 | async-start | bytes 2949120 | tf_op jit(solution)/shard_map/all_gather | solution.py:790
  14.2 16.6 %collective-permute-start.2 = (bf16[3,256,128]{2,1,0:T(8,128)(2,1)}, bf16[3,256,128]{2,1,0:T(8,128)(2,1)S(1)}, u32[]{:S(2)}, u32[]{:S(2)}) collective-permute-start(bf16[3,256,128]{2,1,0:T(8,128)(2,1)} %get-tuple-element.144), channel_id=1, source_target_pairs={{0,24},{8,0},{16,8},{24,16},{1,25},{9,1},{17,9},{25,17},{2,26},{10... | collective-permute-start | bytes 589832 | tf_op jit(solution)/shard_map/ppermute | solution.py:724
  14.4 16.4 %collective-permute-start.1 = (bf16[3,256,128]{2,1,0:T(8,128)(2,1)}, bf16[3,256,128]{2,1,0:T(8,128)(2,1)S(1)}, u32[]{:S(2)}, u32[]{:S(2)}) collective-permute-start(bf16[3,256,128]{2,1,0:T(8,128)(2,1)} %get-tuple-element.144), channel_id=1, source_target_pairs={{0,16},{8,24},{16,0},{24,8},{1,17},{9,25},{17,1},{25,9},{2,18},{10... | collective-permute-start | bytes 589832 | tf_op jit(solution)/shard_map/ppermute | solution.py:724
  16.7 14.1 %collective-permute-start.3 = (bf16[528,256]{1,0:T(8,128)(2,1)}, bf16[528,256]{1,0:T(8,128)(2,1)S(1)}, u32[]{:S(2)}, u32[]{:S(2)}) collective-permute-start(bf16[528,256]{1,0:T(8,128)(2,1)} %get-tuple-element.147), channel_id=1, source_target_pairs={{0,1},{1,0},{2,3},{3,2},{4,5},{5,4},{6,7},{7,6},{8,9},{9,8},{10,11... | collective-permute-start | bytes 811016 | tf_op jit(solution)/shard_map/ppermute | solution.py:678
  17.9 12.9 %collective-permute-start.4 = (bf16[528,256]{1,0:T(8,128)(2,1)}, bf16[528,256]{1,0:T(8,128)(2,1)S(1)}, u32[]{:S(2)}, u32[]{:S(2)}) collective-permute-start(bf16[528,256]{1,0:T(8,128)(2,1)} %get-tuple-element.148), channel_id=1, source_target_pairs={{0,2},{2,0},{1,3},{3,1},{4,6},{6,4},{5,7},{7,5},{8,10},{10,8},{9,1... | collective-permute-start | bytes 811016 | tf_op jit(solution)/shard_map/ppermute | solution.py:678
  31.7 195.9 %reduce-scatter.3.cloned.1.call-start = ((), (), s32[]{:S(2)}) async-start(), calls=%async_computation.3 | async-start | bytes 2949120 | tf_op jit(solution)/shard_map/reduce_scatter | solution.py:831
  49.2 13.4 %collective-permute-start.14 = (bf16[2,512,256]{2,1,0:T(8,128)(2,1)}, bf16[2,512,256]{2,1,0:T(8,128)(2,1)S(1)}, u32[]{:S(2)}, u32[]{:S(2)}) collective-permute-start(bf16[2,512,256]{2,1,0:T(8,128)(2,1)} %get-tuple-element.158), channel_id=1, source_target_pairs={{0,1},{1,0},{2,3},{3,2},{4,5},{5,4},{6,7},{7,6},{8,9},{9,8},{10,11... | collective-permute-start | bytes 1572872 | tf_op jit(solution)/shard_map/ppermute | solution.py:678
  50.5 12.9 %collective-permute-start.15 = (bf16[2,512,256]{2,1,0:T(8,128)(2,1)S(1)}, bf16[2,512,256]{2,1,0:T(8,128)(2,1)S(1)}, u32[]{:S(2)}, u32[]{:S(2)}) collective-permute-start(bf16[2,512,256]{2,1,0:T(8,128)(2,1)S(1)} %copy-done.38), channel_id=1, source_target_pairs={{0,2},{2,0},{1,3},{3,1},{4,6},{6,4},{5,7},{7,5},{8,10},{10,8},{9,1... | collective-permute-start | bytes 1572872 | tf_op jit(solution)/shard_map/ppermute | solution.py:678
  68.8 25.0 %collective-permute-start.17 = (bf16[2,512,256]{2,1,0:T(8,128)(2,1)S(1)}, bf16[2,512,256]{2,1,0:T(8,128)(2,1)S(1)}, u32[]{:S(2)}, u32[]{:S(2)}) collective-permute-start(bf16[2,512,256]{2,1,0:T(8,128)(2,1)S(1)} %collective-permute-done.14.refs_1_), channel_id=1, source_target_pairs={{0,2},{2,0},{1,3},{3,1},{4,6},{6,4},{5,7},{7,5},{8,10},{10,8},{9,1... | collective-permute-start | bytes 1572872 | tf_op jit(solution)/shard_map/ppermute | solution.py:678
  70.0 15.9 %collective-permute-start.13 = (bf16[1024,128]{1,0:T(8,128)(2,1)S(1)}, bf16[1024,128]{1,0:T(8,128)(2,1)}, u32[]{:S(2)}, u32[]{:S(2)}) collective-permute-start(bf16[1024,128]{1,0:T(8,128)(2,1)S(1)} %slice_bitcast_fusion.1), channel_id=1, source_target_pairs={{0,3},{1,2},{2,1},{3,0},{4,7},{5,6},{6,5},{7,4},{8,11},{9,10},{10,... | collective-permute-start | bytes 786440 | tf_op jit(solution)/shard_map/ppermute | solution.py:682
  72.2 21.5 %collective-permute-start.12 = (bf16[1024,128]{1,0:T(8,128)(2,1)S(1)}, bf16[1024,128]{1,0:T(8,128)(2,1)}, u32[]{:S(2)}, u32[]{:S(2)}) collective-permute-start(bf16[1024,128]{1,0:T(8,128)(2,1)S(1)} %slice_bitcast_fusion.1), channel_id=1, source_target_pairs={{0,2},{2,0},{1,3},{3,1},{4,6},{6,4},{5,7},{7,5},{8,10},{10,8},{9,1... | collective-permute-start | bytes 786440 | tf_op jit(solution)/shard_map/ppermute | solution.py:678
  72.9 20.9 %collective-permute-start.11 = (bf16[1024,128]{1,0:T(8,128)(2,1)S(1)}, bf16[1024,128]{1,0:T(8,128)(2,1)}, u32[]{:S(2)}, u32[]{:S(2)}) collective-permute-start(bf16[1024,128]{1,0:T(8,128)(2,1)S(1)} %slice_bitcast_fusion.1), channel_id=1, source_target_pairs={{0,1},{1,0},{2,3},{3,2},{4,5},{5,4},{6,7},{7,6},{8,9},{9,8},{10,11... | collective-permute-start | bytes 786440 | tf_op jit(solution)/shard_map/ppermute | solution.py:678
  94.5 53.1 %collective-permute-start.20 = (bf16[1024,1152]{1,0:T(8,128)(2,1)}, bf16[1024,1152]{1,0:T(8,128)(2,1)}, u32[]{:S(2)}, u32[]{:S(2)}) collective-permute-start(bf16[1024,1152]{1,0:T(8,128)(2,1)} %all-gather.2.cloned.1.call-done.refs_2_), channel_id=1, source_target_pairs={{0,1},{1,0},{2,3},{3,2},{4,5},{5,4},{6,7},{7,6},{8,9},{9,8},{10,11... | collective-permute-start | bytes 7077896 | tf_op jit(solution)/shard_map/ppermute | solution.py:678
  102.6 24.5 %collective-permute-start.21 = (bf16[512,1024]{1,0:T(8,128)(2,1)S(1)}, bf16[512,1024]{1,0:T(8,128)(2,1)S(1)}, u32[]{:S(2)}, u32[]{:S(2)}) collective-permute-start(bf16[512,1024]{1,0:T(8,128)(2,1)S(1)} %get-tuple-element.170.refs_0_), channel_id=1, source_target_pairs={{0,2},{2,0},{1,3},{3,1},{4,6},{6,4},{5,7},{7,5},{8,10},{10,8},{9,1... | collective-permute-start | bytes 3145736 | tf_op jit(solution)/shard_map/ppermute | solution.py:678
  158.1 113.9 %reduce-scatter.5.cloned.1.call-start = ((), (), s32[]{:S(2)}) async-start(), calls=%async_computation.4 | async-start | bytes 2949120 | tf_op jit(solution)/shard_map/reduce_scatter | solution.py:831
  171.0 13.3 %collective-permute-start.25 = (bf16[256,1024]{1,0:T(8,128)(2,1)S(1)}, bf16[256,1024]{1,0:T(8,128)(2,1)S(1)}, u32[]{:S(2)}, u32[]{:S(2)}) collective-permute-start(bf16[256,1024]{1,0:T(8,128)(2,1)S(1)} %get-tuple-element.196), channel_id=1, source_target_pairs={{0,2},{2,0},{1,3},{3,1},{4,6},{6,4},{5,7},{7,5},{8,10},{10,8},{9,1... | collective-permute-start | bytes 1572872 | tf_op jit(solution)/shard_map/ppermute | solution.py:678
  172.2 23.3 %collective-permute-start.26 = (bf16[256,1024]{1,0:T(8,128)(2,1)S(1)}, bf16[256,1024]{1,0:T(8,128)(2,1)S(1)}, u32[]{:S(2)}, u32[]{:S(2)}) collective-permute-start(bf16[256,1024]{1,0:T(8,128)(2,1)S(1)} %get-tuple-element.197), channel_id=1, source_target_pairs={{0,2},{2,0},{1,3},{3,1},{4,6},{6,4},{5,7},{7,5},{8,10},{10,8},{9,1... | collective-permute-start | bytes 1572872 | tf_op jit(solution)/shard_map/ppermute | solution.py:678
  202.9 35.0 %collective-permute-start.27 = (bf16[2,512,256]{2,1,0:T(8,128)(2,1)}, bf16[2,512,256]{2,1,0:T(8,128)(2,1)}, u32[]{:S(2)}, u32[]{:S(2)}) collective-permute-start(bf16[2,512,256]{2,1,0:T(8,128)(2,1)} %get-tuple-element.220), channel_id=1, source_target_pairs={{0,1},{1,0},{2,3},{3,2},{4,5},{5,4},{6,7},{7,6},{8,9},{9,8},{10,11... | collective-permute-start | bytes 1572872 | tf_op jit(solution)/shard_map/ppermute | solution.py:678
  203.7 34.2 %collective-permute-start.28 = (bf16[2,512,256]{2,1,0:T(8,128)(2,1)}, bf16[2,512,256]{2,1,0:T(8,128)(2,1)}, u32[]{:S(2)}, u32[]{:S(2)}) collective-permute-start(bf16[2,512,256]{2,1,0:T(8,128)(2,1)} %get-tuple-element.221), channel_id=1, source_target_pairs={{0,2},{2,0},{1,3},{3,1},{4,6},{6,4},{5,7},{7,5},{8,10},{10,8},{9,1... | collective-permute-start | bytes 1572872 | tf_op jit(solution)/shard_map/ppermute | solution.py:678
  204.3 33.5 %collective-permute-start.29 = (bf16[2,512,256]{2,1,0:T(8,128)(2,1)}, bf16[2,512,256]{2,1,0:T(8,128)(2,1)}, u32[]{:S(2)}, u32[]{:S(2)}) collective-permute-start(bf16[2,512,256]{2,1,0:T(8,128)(2,1)} %get-tuple-element.222), channel_id=1, source_target_pairs={{0,3},{1,2},{2,1},{3,0},{4,7},{5,6},{6,5},{7,4},{8,11},{9,10},{10,... | collective-permute-start | bytes 1572872 | tf_op jit(solution)/shard_map/ppermute | solution.py:682
  244.7 13.5 %collective-permute-start.35 = (bf16[4,256,256]{2,1,0:T(8,128)(2,1)}, bf16[4,256,256]{2,1,0:T(8,128)(2,1)}, u32[]{:S(2)}, u32[]{:S(2)}) collective-permute-start(bf16[4,256,256]{2,1,0:T(8,128)(2,1)} %get-tuple-element.247), channel_id=1, source_target_pairs={{0,1},{1,0},{2,3},{3,2},{4,5},{5,4},{6,7},{7,6},{8,9},{9,8},{10,11... | collective-permute-start | bytes 1572872 | tf_op jit(solution)/shard_map/ppermute | solution.py:678
  246.1 13.4 %collective-permute-start.36 = (bf16[4,256,256]{2,1,0:T(8,128)(2,1)}, bf16[4,256,256]{2,1,0:T(8,128)(2,1)}, u32[]{:S(2)}, u32[]{:S(2)}) collective-permute-start(bf16[4,256,256]{2,1,0:T(8,128)(2,1)} %get-tuple-element.248), channel_id=1, source_target_pairs={{0,2},{2,0},{1,3},{3,1},{4,6},{6,4},{5,7},{7,5},{8,10},{10,8},{9,1... | collective-permute-start | bytes 1572872 | tf_op jit(solution)/shard_map/ppermute | solution.py:678
  247.3 23.0 %collective-permute-start.37 = (bf16[4,256,256]{2,1,0:T(8,128)(2,1)S(1)}, bf16[4,256,256]{2,1,0:T(8,128)(2,1)}, u32[]{:S(2)}, u32[]{:S(2)}) collective-permute-start(bf16[4,256,256]{2,1,0:T(8,128)(2,1)S(1)} %get-tuple-element.249), channel_id=1, source_target_pairs={{0,3},{1,2},{2,1},{3,0},{4,7},{5,6},{6,5},{7,4},{8,11},{9,10},{10,... | collective-permute-start | bytes 1572872 | tf_op jit(solution)/shard_map/ppermute | solution.py:682
  253.5 18.5 %collective-permute-start.34 = (bf16[4,144,256]{2,1,0:T(8,128)(2,1)S(1)}, bf16[4,144,256]{2,1,0:T(8,128)(2,1)S(1)}, u32[]{:S(2)}, u32[]{:S(2)}) collective-permute-start(bf16[4,144,256]{2,1,0:T(8,128)(2,1)S(1)} %get-tuple-element.256), channel_id=1, source_target_pairs={{0,4},{4,0},{1,5},{5,1},{2,6},{6,2},{3,7},{7,3},{8,12},{12,8},{9,1... | collective-permute-start | bytes 884744 | tf_op jit(solution)/shard_map/ppermute | solution.py:678
  275.1 16.1 %collective-permute-start.42 = (bf16[400,256]{1,0:T(8,128)(2,1)S(1)}, bf16[400,256]{1,0:T(8,128)(2,1)S(1)}, u32[]{:S(2)}, u32[]{:S(2)}) collective-permute-start(bf16[400,256]{1,0:T(8,128)(2,1)S(1)} %get-tuple-element.301), channel_id=1, source_target_pairs={{0,16},{8,24},{16,0},{24,8},{1,17},{9,25},{17,1},{25,9},{2,18},{10... | collective-permute-start | bytes 614408 | tf_op jit(solution)/shard_map/ppermute | solution.py:724
  277.2 17.0 %collective-permute-start.43 = (bf16[400,256]{1,0:T(8,128)(2,1)S(1)}, bf16[400,256]{1,0:T(8,128)(2,1)S(1)}, u32[]{:S(2)}, u32[]{:S(2)}) collective-permute-start(bf16[400,256]{1,0:T(8,128)(2,1)S(1)} %get-tuple-element.302), channel_id=1, source_target_pairs={{0,24},{8,0},{16,8},{24,16},{1,25},{9,1},{17,9},{25,17},{2,26},{10... | collective-permute-start | bytes 614408 | tf_op jit(solution)/shard_map/ppermute | solution.py:724
  278.9 18.5 %collective-permute-start.38 = (bf16[512,256]{1,0:T(8,128)(2,1)S(1)}, bf16[512,256]{1,0:T(8,128)(2,1)S(1)}, u32[]{:S(2)}, u32[]{:S(2)}) collective-permute-start(bf16[512,256]{1,0:T(8,128)(2,1)S(1)} %copy-done.66), channel_id=1, source_target_pairs={{0,1},{1,0},{2,3},{3,2},{4,5},{5,4},{6,7},{7,6},{8,9},{9,8},{10,11... | collective-permute-start | bytes 786440 | tf_op jit(solution)/shard_map/ppermute | solution.py:678
  280.4 17.0 %collective-permute-start.39 = (bf16[512,256]{1,0:T(8,128)(2,1)S(1)}, bf16[512,256]{1,0:T(8,128)(2,1)}, u32[]{:S(2)}, u32[]{:S(2)}) collective-permute-start(bf16[512,256]{1,0:T(8,128)(2,1)S(1)} %copy-done.64), channel_id=1, source_target_pairs={{0,2},{2,0},{1,3},{3,1},{4,6},{6,4},{5,7},{7,5},{8,10},{10,8},{9,1... | collective-permute-start | bytes 786440 | tf_op jit(solution)/shard_map/ppermute | solution.py:678
  280.5 18.0 %collective-permute-start.40 = (bf16[512,256]{1,0:T(8,128)(2,1)S(1)}, bf16[512,256]{1,0:T(8,128)(2,1)}, u32[]{:S(2)}, u32[]{:S(2)}) collective-permute-start(bf16[512,256]{1,0:T(8,128)(2,1)S(1)} %copy-done.62), channel_id=1, source_target_pairs={{0,3},{1,2},{2,1},{3,0},{4,7},{5,6},{6,5},{7,4},{8,11},{9,10},{10,... | collective-permute-start | bytes 786440 | tf_op jit(solution)/shard_map/ppermute | solution.py:682
  291.2 20.2 %collective-permute-start.47 = (bf16[256,1152]{1,0:T(8,128)(2,1)}, bf16[256,1152]{1,0:T(8,128)(2,1)}, u32[]{:S(2)}, u32[]{:S(2)}) collective-permute-start(bf16[256,1152]{1,0:T(8,128)(2,1)} %reduce-scatter.5.cloned.1.call-done), channel_id=1, source_target_pairs={{0,1},{1,0},{2,3},{3,2},{4,5},{5,4},{6,7},{7,6},{8,9},{9,8},{10,11... | collective-permute-start | bytes 1769480 | tf_op jit(solution)/shard_map/ppermute | solution.py:678
  294.4 13.6 %collective-permute-start.44 = (bf16[144,256]{1,0:T(8,128)(2,1)S(1)}, bf16[144,256]{1,0:T(8,128)(2,1)S(1)}, u32[]{:S(2)}, u32[]{:S(2)}) collective-permute-start(bf16[144,256]{1,0:T(8,128)(2,1)S(1)} %slice.133), channel_id=1, source_target_pairs={{0,1},{1,0},{2,3},{3,2},{4,5},{5,4},{6,7},{7,6},{8,9},{9,8},{10,11... | collective-permute-start | bytes 221192 | tf_op jit(solution)/shard_map/ppermute | solution.py:678
  297.5 13.2 %collective-permute-start.46 = (bf16[144,256]{1,0:T(8,128)(2,1)S(1)}, bf16[144,256]{1,0:T(8,128)(2,1)S(1)}, u32[]{:S(2)}, u32[]{:S(2)}) collective-permute-start(bf16[144,256]{1,0:T(8,128)(2,1)S(1)} %slice.133), channel_id=1, source_target_pairs={{0,3},{1,2},{2,1},{3,0},{4,7},{5,6},{6,5},{7,4},{8,11},{9,10},{10,... | collective-permute-start | bytes 221192 | tf_op jit(solution)/shard_map/ppermute | solution.py:682
  (89 other events, 867.8 us)
Sparse Core Ops, SparseCore 0:
  31.8 55.7 all-gather.1
  158.3 45.5 reduce-scatter.2
  206.2 47.5 reduce-scatter.4
